TPU v7x, 32 devices: a whole 2x2x4 slice. The times are simulated.
32 devices in a mesh: dp: 4 (over z), seq: 8 (over y, x, core).
Axes of the slice: x: 2, y: 2, z: 4, core: 2. Of those that a mesh axis runs over, the one named last changes fastest.
Arguments:
- inputs: bfloat16 [12, 1152, 1024], P('dp', 'seq'), may hold values from -6 to 6
- doc_lengths: int32 [12, 4], P('dp'), may hold values from 1 to 1080, 1152 in all within a row
- gain_attn: float32 [1024], replicated, may hold values from 0.25 to 1.75
- w_query: bfloat16 [1024, 256], replicated, may hold values from -0.1875 to 0.1875
- w_key: bfloat16 [1024, 256], replicated, may hold values from -0.1875 to 0.1875
- w_value: bfloat16 [1024, 1024], replicated, may hold values from -0.1875 to 0.1875
- w_out: bfloat16 [1024, 1024], replicated, may hold values from -1 to 1
- gain_ffn: float32 [1024], replicated, may hold values from 0.25 to 1.75
- w_gate: bfloat16 [1024, 2752], replicated, may hold values from -0.1875 to 0.1875
- w_up: bfloat16 [1024, 2752], replicated, may hold values from -0.1875 to 0.1875
- w_down: bfloat16 [2752, 1024], replicated, may hold values from -0.109375 to 0.109375
- cotangent: bfloat16 [12, 1152, 1024], P('dp', 'seq'), may hold values from -6 to 6
Outputs:
- output: bfloat16 [12, 1152, 1024], P('dp', 'seq')
- input_grad: bfloat16 [12, 1152, 1024], P('dp', 'seq')
- gain_attn_grad: float32 [1024], P(('dp', 'seq'))
- query_grad: float32 [1024, 256], P(('dp', 'seq'))
- key_grad: float32 [1024, 256], P(('dp', 'seq'))
- value_grad: float32 [1024, 1024], P(('dp', 'seq'))
- out_grad: float32 [1024, 1024], P(('dp', 'seq'))
- gain_ffn_grad: float32 [1024], P(('dp', 'seq'))
- gate_grad: float32 [1024, 2752], P(('dp', 'seq'))
- up_grad: float32 [1024, 2752], P(('dp', 'seq'))
- down_grad: float32 [2752, 1024], P(None, ('dp', 'seq'))
Inputs may be any that keep to these rules, and one draw needn't show every extreme that they name: `doc_lengths`: each row's 4 document lengths sum to 1152.
All inputs are finite; a program needn't handle non-finite values.
Results may differ from a plain program's by a relative error of at most 0.01.
Values may be sent and summed in bfloat16 or wider, within the bound.
A program may use at most 256 MiB of HBM per device.

v0:
```python
import jax
import jax.numpy as jnp
from jax import lax
from jax.sharding import PartitionSpec as P

D = 1024
H = 16
F = 16
HV = 64
BLOCK = 576


eps_norm = 1e-05


def rms_scale(stream, gain_vec):
    return (
        stream * lax.rsqrt(jnp.mean(stream * stream, axis=-1, keepdims=True) + eps_norm) * gain_vec
    )


def taylor_features(vectors):
    feat_width = vectors.shape[-1]
    outer_prod = (vectors[..., :, None] * vectors[..., None, :]).reshape(
        vectors.shape[:-1] + (feat_width * feat_width,)
    )
    ones_part = jnp.ones(vectors.shape[:-1] + (1,), jnp.float32)
    return jnp.concatenate(
        [ones_part, vectors * feat_width ** (-0.25), outer_prod * (0.5 / feat_width) ** 0.5],
        axis=-1,
    )


def document_ids(doc_lens, seq_length):
    doc_ends = jnp.cumsum(doc_lens, dtype=jnp.int32)
    positions = jnp.arange(seq_length, dtype=jnp.int32)
    return jnp.sum(
        (positions[:, None] >= doc_ends[None, :]).astype(jnp.int32), axis=1, dtype=jnp.int32
    )


def attend_row(queries, key_proj, value_proj, doc_row, block_rows):
    seq_length, head_count, feat_width = queries.shape
    value_width = value_proj.shape[-1]
    feat_count = 1 + feat_width + feat_width * feat_width
    block_count = seq_length // block_rows
    highest = lax.Precision.HIGHEST
    query_blocks = queries.reshape(block_count, block_rows, head_count, feat_width)
    key_blocks = key_proj.reshape(block_count, block_rows, head_count, feat_width)
    value_blocks = value_proj.reshape(block_count, block_rows, head_count, value_width)
    doc_blocks = doc_row.reshape(block_count, block_rows)
    previous = jnp.concatenate([jnp.full((1,), -1, jnp.int32), doc_blocks[:-1, -1]])
    positions = jnp.arange(block_rows, dtype=jnp.int32)
    causal = positions[:, None] >= positions[None, :]

    def block_step(carried, pieces):
        state_sum, norm_sum = carried
        query_block, key_block, value_block, doc_block, prior_doc = pieces
        scores = jnp.einsum(
            "thf,shf->hts", query_block, key_block, precision=highest
        ) * feat_width ** (-0.5)
        weights = 1.0 + scores + 0.5 * scores * scores
        same_doc = causal & (doc_block[:, None] == doc_block[None, :])
        weights = jnp.where(same_doc[None, :, :], weights, 0.0)
        numerator = jnp.einsum("hts,shv->thv", weights, value_block, precision=highest)
        denominator = jnp.transpose(jnp.sum(weights, axis=2))
        use_state = (doc_block == prior_doc).astype(jnp.float32)[:, None]
        query_feats = taylor_features(query_block)
        numerator = numerator + use_state[:, :, None] * jnp.einsum(
            "thp,hpv->thv", query_feats, state_sum, precision=highest
        )
        denominator = denominator + use_state * jnp.einsum(
            "thp,hp->th", query_feats, norm_sum, precision=highest
        )
        last_doc = doc_block[-1]
        keep_state = (last_doc == prior_doc).astype(jnp.float32)
        key_feats = (
            taylor_features(key_block) * (doc_block == last_doc).astype(jnp.float32)[:, None, None]
        )
        state_sum = keep_state * state_sum + jnp.einsum(
            "shp,shv->hpv", key_feats, value_block, precision=highest
        )
        norm_sum = keep_state * norm_sum + jnp.sum(key_feats, axis=0)
        return ((state_sum, norm_sum), numerator / denominator[:, :, None])

    initial = (
        jnp.zeros((head_count, feat_count, value_width), jnp.float32),
        jnp.zeros((head_count, feat_count), jnp.float32),
    )
    _, results = lax.scan(
        jax.checkpoint(block_step),
        initial,
        (query_blocks, key_blocks, value_blocks, doc_blocks, previous),
    )
    return results.reshape(seq_length, head_count, value_width)


def project(left, right):
    return jnp.dot(left, right, preferred_element_type=jnp.float32)


def back_project(left, right):
    return lax.dot_general(
        left, right, (((1,), (1,)), ((), ())), preferred_element_type=jnp.float32
    )


def weight_grad(left, right):
    return lax.dot_general(
        left, right, (((0,), (0,)), ((), ())), preferred_element_type=jnp.float32
    )


def swiglu(gate_proj, up_proj):
    return jax.nn.silu(gate_proj) * up_proj


def body(
    inputs,
    doc_lengths,
    gain_attn,
    w_query,
    w_key,
    w_value,
    w_out,
    gain_ffn,
    w_gate,
    w_up,
    w_down,
    cotangent,
):
    row_count, shard_len, _ = inputs.shape
    token_count = row_count * shard_len
    stream = inputs.reshape(token_count, D).astype(jnp.float32)
    normed, attn_norm_back = jax.vjp(rms_scale, stream, gain_attn)
    normed_low = normed.astype(jnp.bfloat16)
    query_proj = project(normed_low, w_query).astype(jnp.bfloat16)
    key_proj = project(normed_low, w_key).astype(jnp.bfloat16)
    value_proj = project(normed_low, w_value).astype(jnp.bfloat16)
    query_heads, key_heads, value_heads = (
        lax.all_to_all(
            query_proj.reshape(row_count, shard_len, H, F),
            "seq",
            split_axis=2,
            concat_axis=1,
            tiled=True,
        ),
        lax.all_to_all(
            key_proj.reshape(row_count, shard_len, H, F),
            "seq",
            split_axis=2,
            concat_axis=1,
            tiled=True,
        ),
        lax.all_to_all(
            value_proj.reshape(row_count, shard_len, H, HV),
            "seq",
            split_axis=2,
            concat_axis=1,
            tiled=True,
        ),
    )
    seq_length = query_heads.shape[1]
    doc_rows = jax.vmap(lambda doc_lens: document_ids(doc_lens, seq_length))(doc_lengths)

    def attend_all(queries, keys_in, values_in):
        return jax.vmap(attend_row, in_axes=(0, 0, 0, 0, None))(
            queries, keys_in, values_in, doc_rows, BLOCK
        )

    mixed_heads, attend_back = jax.vjp(
        attend_all,
        query_heads.astype(jnp.float32),
        key_heads.astype(jnp.float32),
        value_heads.astype(jnp.float32),
    )
    mixed_rows = lax.all_to_all(
        mixed_heads.astype(jnp.bfloat16), "seq", split_axis=1, concat_axis=2, tiled=True
    )
    mixed_flat = mixed_rows.reshape(token_count, D)
    residual = stream + project(mixed_flat, w_out)
    normed_ffn, ffn_norm_back = jax.vjp(rms_scale, residual, gain_ffn)
    ffn_low = normed_ffn.astype(jnp.bfloat16)
    gate_proj = project(ffn_low, w_gate)
    up_proj = project(ffn_low, w_up)
    hidden, act_back = jax.vjp(swiglu, gate_proj, up_proj)
    hidden_low = hidden.astype(jnp.bfloat16)
    output = residual + project(hidden_low, w_down)
    grad_out = cotangent.reshape(token_count, D)
    grad_gate, grad_up = act_back(back_project(grad_out, w_down))
    grad_gate_low = grad_gate.astype(jnp.bfloat16)
    grad_up_low = grad_up.astype(jnp.bfloat16)
    down_grad_t = weight_grad(grad_out, hidden_low)
    gate_grad = weight_grad(ffn_low, grad_gate_low)
    up_grad = weight_grad(ffn_low, grad_up_low)
    grad_normed_ffn = back_project(grad_gate_low, w_gate) + back_project(grad_up_low, w_up)
    grad_residual, gain_ffn_grad = ffn_norm_back(grad_normed_ffn)
    grad_residual = grad_residual + grad_out.astype(jnp.float32)
    grad_branch = grad_residual.astype(jnp.bfloat16)
    out_grad = weight_grad(mixed_flat, grad_branch)
    grad_mixed = (
        back_project(grad_branch, w_out).astype(jnp.bfloat16).reshape(row_count, shard_len, H, HV)
    )
    grad_heads = lax.all_to_all(grad_mixed, "seq", split_axis=2, concat_axis=1, tiled=True)
    grad_query, grad_key, grad_value = attend_back(grad_heads.astype(jnp.float32))
    back_query, back_key, back_value = (
        lax.all_to_all(
            grad_query.astype(jnp.bfloat16), "seq", split_axis=1, concat_axis=2, tiled=True
        ),
        lax.all_to_all(
            grad_key.astype(jnp.bfloat16), "seq", split_axis=1, concat_axis=2, tiled=True
        ),
        lax.all_to_all(
            grad_value.astype(jnp.bfloat16), "seq", split_axis=1, concat_axis=2, tiled=True
        ),
    )
    back_query = back_query.reshape(token_count, H * F)
    back_key = back_key.reshape(token_count, H * F)
    back_value = back_value.reshape(token_count, D)
    query_grad = weight_grad(normed_low, back_query)
    key_grad = weight_grad(normed_low, back_key)
    value_grad = weight_grad(normed_low, back_value)
    grad_normed = (
        back_project(back_query, w_query)
        + back_project(back_key, w_key)
        + back_project(back_value, w_value)
    )
    grad_stream, gain_attn_grad = attn_norm_back(grad_normed)
    input_grad = grad_residual + grad_stream
    (
        gain_attn_part,
        query_part,
        key_part,
        value_part,
        out_part,
        gain_ffn_part,
        gate_part,
        up_part,
        down_part,
    ) = (
        lax.psum_scatter(gain_attn_grad, ("dp", "seq"), scatter_dimension=0, tiled=True),
        lax.psum_scatter(query_grad, ("dp", "seq"), scatter_dimension=0, tiled=True),
        lax.psum_scatter(key_grad, ("dp", "seq"), scatter_dimension=0, tiled=True),
        lax.psum_scatter(value_grad, ("dp", "seq"), scatter_dimension=0, tiled=True),
        lax.psum_scatter(out_grad, ("dp", "seq"), scatter_dimension=0, tiled=True),
        lax.psum_scatter(gain_ffn_grad, ("dp", "seq"), scatter_dimension=0, tiled=True),
        lax.psum_scatter(gate_grad, ("dp", "seq"), scatter_dimension=0, tiled=True),
        lax.psum_scatter(up_grad, ("dp", "seq"), scatter_dimension=0, tiled=True),
        lax.psum_scatter(down_grad_t, ("dp", "seq"), scatter_dimension=0, tiled=True),
    )
    return (
        output.reshape(row_count, shard_len, D).astype(jnp.bfloat16),
        input_grad.reshape(row_count, shard_len, D).astype(jnp.bfloat16),
        gain_attn_part,
        query_part,
        key_part,
        value_part,
        out_part,
        gain_ffn_part,
        gate_part,
        up_part,
        jnp.transpose(down_part),
    )


def solution(mesh):
    in_specs = (
        P("dp", "seq", None),
        P("dp", None),
        P(),
        P(),
        P(),
        P(),
        P(),
        P(),
        P(),
        P(),
        P(),
        P("dp", "seq", None),
    )
    out_specs = (
        P("dp", "seq", None),
        P("dp", "seq", None),
        P(("dp", "seq")),
        P(("dp", "seq"), None),
        P(("dp", "seq"), None),
        P(("dp", "seq"), None),
        P(("dp", "seq"), None),
        P(("dp", "seq")),
        P(("dp", "seq"), None),
        P(("dp", "seq"), None),
        P(None, ("dp", "seq")),
    )
    return jax.shard_map(body, mesh=mesh, in_specs=in_specs, out_specs=out_specs, check_vma=False)
```

profile of v0, /device:TPU:0, one launch (start us, length us, event | category | flops | bytes accessed | tf_op | source)
XLA Modules:
  0.0 1578.0 jit_solution(4447294367722620317)
XLA Ops:
  58.8 10.1 all-to-all-done.1
  82.2 98.8 %while.45 = (s32[]{:T(128)}, f32[3,2,273,64]{2,3,1,0:T(8,128)}, f32[3,2,273]{2,1,0:T(2,128)S(1)}, bf16[2,3,576,2,64]{2,4,3,1,0:T(8,128)(2,1)}, f32[2,3,2,273,64]...) while((s32[]{:T(128)}, f32[3,2,273,64]{2,3,1,0:T(8,128)}, ...), condition=%wide.region_6.7_spmd.clone, body=%wide.region_3.6_spmd.clone.sunk | while | flops 3414981120 | bytes 106284016 | solution.py:90
  113.7 9.7 fusion.238
  127.8 7.8 bitcast_dynamic-update-slice_fusion.6
  152.5 9.7 fusion.238
  166.6 7.8 bitcast_dynamic-update-slice_fusion.6
  190.5 16.9 %all_to_all.96 = bf16[8,2,27648]{2,1,0:T(2,128)(2,1)} all-to-all(bf16[8,2,27648]{2,1,0:T(2,128)(2,1)S(1)} %reshape.500), channel_id=1, replica_groups=mesh['dp'=4,'seq'=8] {'seq'}, dimensions={0} | all-to-all | bytes 1769472 | tf_op jit(solution)/shard_map/all_to_all | solution.py:177
  224.7 8.6 fusion.114
  238.8 9.5 multiply_convert_fusion
  267.0 20.9 %all-to-all-done.4 = bf16[3,144,16,64]{1,3,0,2:T(8,128)(2,1)S(1)} async-done(((bf16[3,144,16,64]{1,3,0,2:T(8,128)(2,1)}), bf16[3,144,16,64]{1,3,0,2:T(8,128)(2,1)S(1)}, u32[]{:S(2)}, u32[]{:S(2)}) %all-to-all-start.4) | async-done | bytes 884768 | tf_op jit(solution)/shard_map/all_to_all | solution.py:204
  298.2 238.1 %while.46 = (s32[]{:T(128)}, f32[3,2,273,64]{2,3,1,0:T(8,128)}, f32[3,2,273]{2,1,0:T(2,128)S(1)}, bf16[2,3,576,2,16]{2,4,3,1,0:T(8,128)(2,1)}, bf16[2,3,576,2,16...) while((s32[]{:T(128)}, f32[3,2,273,64]{2,3,1,0:T(8,128)}, ...), condition=%wide.region_16.17_spmd.clone, body=%wide.region_9.16_spmd.clone.sunk | while | flops 9470423040 | bytes 253930272 | solution.py:90
  329.8 11.6 fusion.261
  342.7 16.4 %fusion.271 = bf16[2,3,576,2,64]{2,4,3,1,0:T(8,128)(2,1)} fusion(bf16[2,3,576,2,64]{2,4,3,1,0:T(8,128)(2,1)} %get-tuple-element.1187, s32[]{:T(128)S(6)} %sub.21, f32[3,2,64,576]{3,2,1,0:T(8,128)} %fusion.270, f32[3,2,576,576]{2,3,1,0:T(8,128)} %get-tuple-element.1109, pred[3,576,576]{1,2,0:T(8,128)(4,1)} %copy-done.10, ...), kind=kOutput, calls=%fused_computation.35.clone.1 | convolution fusion | flops 1541210112 | bytes 12719620 | tf_op jit(solution)/shard_map/transpose(jvp(vmap()))/while/body/eval_jaxpr/checkpoint/hts,shv->thv/dot_general | solution.py:65
  359.1 7.8 fusion.263
  370.4 10.8 fusion.267
  381.2 8.9 fusion.269
  445.6 11.6 fusion.261
  458.4 16.2 %fusion.271 = bf16[2,3,576,2,64]{2,4,3,1,0:T(8,128)(2,1)} fusion(bf16[2,3,576,2,64]{2,4,3,1,0:T(8,128)(2,1)} %get-tuple-element.1187, s32[]{:T(128)S(6)} %sub.21, f32[3,2,64,576]{3,2,1,0:T(8,128)} %fusion.270, f32[3,2,576,576]{2,3,1,0:T(8,128)} %get-tuple-element.1109, pred[3,576,576]{1,2,0:T(8,128)(4,1)} %copy-done.10, ...), kind=kOutput, calls=%fused_computation.35.clone.1 | convolution fusion | flops 1541210112 | bytes 12719620 | tf_op jit(solution)/shard_map/transpose(jvp(vmap()))/while/body/eval_jaxpr/checkpoint/hts,shv->thv/dot_general | solution.py:65
  474.7 7.8 fusion.263
  485.9 10.9 fusion.267
  496.8 9.1 fusion.269
  565.6 9.4 all_to_all.97
  598.9 18.2 %all_to_all.98 = bf16[8,2,27648]{2,1,0:T(2,128)(2,1)S(1)} all-to-all(bf16[8,2,27648]{2,1,0:T(2,128)(2,1)} %reshape.502), channel_id=1, replica_groups=mesh['dp'=4,'seq'=8] {'seq'}, dimensions={0} | all-to-all | bytes 1769472 | tf_op jit(solution)/shard_map/all_to_all | solution.py:213
  648.7 7.8 convolution_bitcast_fusion.2
  656.5 11.9 copy.288
  680.7 39.6 %all-reduce.3 = (f32[1024]{0:T(1024)S(1)}, f32[1024]{0:T(1024)S(1)}) all-reduce(f32[1024]{0:T(1024)S(1)} %get-tuple-element.809, f32[1024]{0:T(1024)S(1)} %copy-done.56), channel_id=2, replica_groups=mesh['dp'=4,'seq'=8] {'dp','seq'}, use_global_device_ids=true, to_apply=%region_19.20.clone | all-reduce | flops 2048 | bytes 16384
  724.9 105.5 %reduce-scatter.12.cloned.1.call-done = f32[32,256]{1,0:T(8,128)} async-done(((f32[1024,256]{1,0:T(8,128)}), f32[32,256]{1,0:T(8,128)}) %reduce-scatter.12.cloned.1.call-update) | async-done | bytes 32784 | tf_op jit(solution)/shard_map/reduce_scatter | solution.py:243
  830.4 140.1 %reduce-scatter.16.cloned.1.call-done = f32[32,1024]{1,0:T(8,128)} async-done(((f32[1024,1024]{1,0:T(8,128)}), f32[32,1024]{1,0:T(8,128)}) %reduce-scatter.16.cloned.1.call-update) | async-done | bytes 131088 | tf_op jit(solution)/shard_map/reduce_scatter | solution.py:245
  970.5 139.8 %reduce-scatter.14.cloned.1.call-done = f32[32,1024]{1,0:T(8,128)} async-done(((f32[1024,1024]{1,0:T(8,128)}), f32[32,1024]{1,0:T(8,128)}) %reduce-scatter.14.cloned.1.call-update) | async-done | bytes 131088 | tf_op jit(solution)/shard_map/reduce_scatter | solution.py:244
  1110.2 153.6 %reduce-scatter.18.cloned.1.call-done = f32[32,2752]{1,0:T(8,128)} async-done(((f32[1024,2752]{1,0:T(8,128)}), f32[32,2752]{1,0:T(8,128)}) %reduce-scatter.18.cloned.1.call-update) | async-done | bytes 352272 | tf_op jit(solution)/shard_map/reduce_scatter | solution.py:247
  1263.8 153.5 %reduce-scatter.20.cloned.1.call-done = f32[32,2752]{1,0:T(8,128)} async-done(((f32[1024,2752]{1,0:T(8,128)}), f32[32,2752]{1,0:T(8,128)}) %reduce-scatter.20.cloned.1.call-update) | async-done | bytes 352272 | tf_op jit(solution)/shard_map/reduce_scatter | solution.py:248
  1417.3 153.6 %reduce-scatter.22.cloned.1.call-done = f32[32,2752]{1,0:T(8,128)} async-done(((f32[1024,2752]{1,0:T(8,128)}), f32[32,2752]{1,0:T(8,128)}) %reduce-scatter.22.cloned.1.call-update) | async-done | bytes 352272
  (421 shorter events, 386.8 us)
Async XLA Ops:
  7.2 214.7 %copy-start = (bf16[1024,1024]{1,0:T(8,128)(2,1)S(1)}, bf16[1024,1024]{1,0:T(8,128)(2,1)}, u32[]{:S(2)}) copy-start(bf16[1024,1024]{1,0:T(8,128)(2,1)} %param.22) | copy-start | bytes 6291460
  15.1 13.5 all-to-all-start
  28.6 15.0 all-to-all-start.2
  35.9 12.0 copy-start.57
  43.6 25.3 %all-to-all-start.1 = ((bf16[3,144,16,64]{1,3,0,2:T(8,128)(2,1)}), bf16[3,144,16,64]{1,3,0,2:T(8,128)(2,1)}, u32[]{:S(2)}, u32[]{:S(2)}) async-start(bf16[3,144,16,64]{1,3,0,2:T(8,128)(2,1)} %copy.244), calls=%async_computation.1 | async-start | bytes 3145728 | tf_op jit(solution)/shard_map/all_to_all | solution.py:155
  207.5 14.4 copy-start.8
  221.9 11.5 slice-start.2
  224.4 32.2 %copy-start.25 = (f32[432,1024]{1,0:T(8,128)}, f32[432,1024]{1,0:T(8,128)S(1)}, u32[]{:S(2)}) copy-start(f32[432,1024]{1,0:T(8,128)S(1)} %get-tuple-element.892) | copy-start | bytes 5308420
  224.7 14.1 slice-start.4
  233.4 15.0 slice-start
  263.4 24.5 %all-to-all-start.4 = ((bf16[3,144,16,64]{1,3,0,2:T(8,128)(2,1)}), bf16[3,144,16,64]{1,3,0,2:T(8,128)(2,1)S(1)}, u32[]{:S(2)}, u32[]{:S(2)}) async-start(bf16[3,144,16,64]{1,3,0,2:T(8,128)(2,1)} %copy.256), calls=%async_computation.4 | async-start | bytes 3145728 | tf_op jit(solution)/shard_map/all_to_all | solution.py:204
  329.8 11.7 copy-start.10
  342.6 16.5 %copy-start.7 = (f32[3,576,2,64]{1,3,2,0:T(8,128)S(1)}, f32[3,576,2,64]{1,3,2,0:T(8,128)}, u32[]{:S(2)}) copy-start(f32[3,576,2,64]{1,3,2,0:T(8,128)} %get-tuple-element.1108) | copy-start | bytes 2654212 | tf_op jit(solution)/shard_map/transpose(jvp(vmap()))/while
  342.6 16.5 %copy-start.11 = (pred[3,576,576]{1,2,0:T(8,128)(4,1)S(1)}, pred[3,576,576]{1,2,0:T(8,128)(4,1)}, u32[]{:S(2)}) copy-start(pred[3,576,576]{1,2,0:T(8,128)(4,1)} %copy-done.10) | copy-start | bytes 2985988 | tf_op jit(solution)/shard_map/transpose(jvp(vmap()))/while
  342.6 16.5 %copy-start.60 = (f32[3,2,576,576]{2,3,1,0:T(8,128)S(1)}, f32[3,2,576,576]{2,3,1,0:T(8,128)}, u32[]{:S(2)}) copy-start(f32[3,2,576,576]{2,3,1,0:T(8,128)} %get-tuple-element.1109) | copy-start | bytes 23887876 | tf_op jit(solution)/shard_map/transpose(jvp(vmap()))/while
  445.6 11.7 copy-start.10
  458.4 16.2 %copy-start.7 = (f32[3,576,2,64]{1,3,2,0:T(8,128)S(1)}, f32[3,576,2,64]{1,3,2,0:T(8,128)}, u32[]{:S(2)}) copy-start(f32[3,576,2,64]{1,3,2,0:T(8,128)} %get-tuple-element.1108) | copy-start | bytes 2654212 | tf_op jit(solution)/shard_map/transpose(jvp(vmap()))/while
  458.4 16.2 %copy-start.11 = (pred[3,576,576]{1,2,0:T(8,128)(4,1)S(1)}, pred[3,576,576]{1,2,0:T(8,128)(4,1)}, u32[]{:S(2)}) copy-start(pred[3,576,576]{1,2,0:T(8,128)(4,1)} %copy-done.10) | copy-start | bytes 2985988 | tf_op jit(solution)/shard_map/transpose(jvp(vmap()))/while
  458.4 16.2 %copy-start.60 = (f32[3,2,576,576]{2,3,1,0:T(8,128)S(1)}, f32[3,2,576,576]{2,3,1,0:T(8,128)}, u32[]{:S(2)}) copy-start(f32[3,2,576,576]{2,3,1,0:T(8,128)} %get-tuple-element.1109) | copy-start | bytes 23887876 | tf_op jit(solution)/shard_map/transpose(jvp(vmap()))/while
  542.2 9.8 all-to-all-start.5
  545.6 179.3 %reduce-scatter.10.cloned.1.call-start = ((), (), s32[]{:S(2)}) async-start(), calls=%async_computation.15 | async-start | bytes 1081344 | tf_op jit(solution)/shard_map/reduce_scatter | solution.py:242
  546.0 15.9 %copy-start.20 = (bf16[3,144,1024]{2,1,0:T(8,128)(2,1)}, bf16[3,144,1024]{2,1,0:T(8,128)(2,1)S(1)}, u32[]{:S(2)}) copy-start(bf16[3,144,1024]{2,1,0:T(8,128)(2,1)S(1)} %multiply_convert_fusion.2) | copy-start | bytes 2654212
  546.0 16.0 %copy-start.35 = (bf16[2,3,576,2,16]{2,4,3,1,0:T(8,128)(2,1)S(1)}, bf16[2,3,576,2,16]{2,4,3,1,0:T(8,128)(2,1)}, u32[]{:S(2)}) copy-start(bf16[2,3,576,2,16]{2,4,3,1,0:T(8,128)(2,1)} %get-tuple-element.514) | copy-start | bytes 663556
  561.9 268.5 %reduce-scatter.12.cloned.1.call-start = ((), (), s32[]{:S(2)}) async-start(), calls=%async_computation.16 | async-start | bytes 1081344 | tf_op jit(solution)/shard_map/reduce_scatter | solution.py:243
  575.0 13.2 copy-start.17
  588.1 382.3 %reduce-scatter.16.cloned.1.call-start = ((), (), s32[]{:S(2)}) async-start(), calls=%async_computation.18 | async-start | bytes 4325376 | tf_op jit(solution)/shard_map/reduce_scatter | solution.py:245
  592.6 517.6 %reduce-scatter.14.cloned.1.call-start = ((), (), s32[]{:S(2)}) async-start(), calls=%async_computation.17 | async-start | bytes 4325376 | tf_op jit(solution)/shard_map/reduce_scatter | solution.py:244
  630.9 632.9 %reduce-scatter.18.cloned.1.call-start = ((), (), s32[]{:S(2)}) async-start(), calls=%async_computation.19 | async-start | bytes 11894784 | tf_op jit(solution)/shard_map/reduce_scatter | solution.py:247
  639.8 777.6 %reduce-scatter.20.cloned.1.call-start = ((), (), s32[]{:S(2)}) async-start(), calls=%async_computation.20 | async-start | bytes 11894784 | tf_op jit(solution)/shard_map/reduce_scatter | solution.py:248
  647.5 923.4 %reduce-scatter.22.cloned.1.call-start = ((), (), s32[]{:S(2)}) async-start(), calls=%async_computation.21 | async-start | bytes 11894784
  678.6 42.9 %copy-start.51 = (f32[432]{0:T(512)S(1)}, f32[432]{0:T(512)}, u32[]{:S(2)}) copy-start(f32[432]{0:T(512)} %copy-done.50) | copy-start | bytes 5188
  678.6 892.4 %copy-start.1 = (bf16[1024,1024]{1,0:T(8,128)(2,1)S(1)}, bf16[1024,1024]{1,0:T(8,128)(2,1)}, u32[]{:S(2)}) copy-start(bf16[1024,1024]{1,0:T(8,128)(2,1)} %param.22) | copy-start | bytes 6291460
  (76 other events, 407.4 us)
Sparse Core Ops, SparseCore 0:
  562.0 134.4 reduce-scatter.9
  699.4 130.9 reduce-scatter.11
  833.2 137.2 reduce-scatter.15
  973.2 137.0 reduce-scatter.13
  1113.0 150.8 reduce-scatter.17
  1266.6 150.7 reduce-scatter.19
  1420.2 150.6 reduce-scatter.21
where the time goes:
time: 1590 us; the launch traced here: 1580 us
  waiting for transfers between devices  889 us (56%)
  matrix products  332 us (21%)
  local copies, waits for them, and re-layouts  169 us (11%)
  blocking collectives  84.1 us (5%)
  other arithmetic  38.7 us (2%)
  loops' own time  30.8 us (2%)
  starting transfers between devices  20.2 us (1%)
    unnamed x8, waiting for transfers between devices  154 us
    reduce_scatter x1, waiting for transfers between devices, body(): lax.psum_scatter(gate_grad, ('dp', 'seq'), scatter_dimension=0, tiled=True)  154 us
    reduce_scatter x1, waiting for transfers between devices, body(): lax.psum_scatter(up_grad, ('dp', 'seq'), scatter_dimension=0, tiled=True)  154 us
    reduce_scatter x1, waiting for transfers between devices, body(): lax.psum_scatter(out_grad, ('dp', 'seq'), scatter_dimension=0, tiled=True)  140 us
    reduce_scatter x1, waiting for transfers between devices, body(): lax.psum_scatter(value_grad, ('dp', 'seq'), scatter_dimension=0, tiled=True)  140 us
    reduce_scatter x1, waiting for transfers between devices, body(): lax.psum_scatter(key_grad, ('dp', 'seq'), scatter_dimension=0, tiled=True)  105 us
    dot_general x8, matrix products, block_step(): jnp.einsum('hts,shv->thv', weights, value_block, precision=highest)  85.5 us
    dot_general x8, matrix products, block_step(): jnp.einsum('thf,shf->hts', query_block, key_block, precision=highest)  71 us
  transfers between devices with their start and end apart: 12, of which 10 were waited for; matrix products, arithmetic and copies ran while one was open for 7% of the time, Pallas kernels for 0%

commit v1 on v0

--- a/solution.py
+++ b/solution.py
@@ -1,6 +1,10 @@
+import functools
+
 import jax
 import jax.numpy as jnp
 from jax import lax
+from jax.experimental import pallas as pl
+from jax.experimental.pallas import tpu as pltpu
 from jax.sharding import PartitionSpec as P
 
 D = 1024
@@ -115,7 +119,7 @@
     return jax.nn.silu(gate_proj) * up_proj
 
 
-def body(
+def general_body(
     inputs,
     doc_lengths,
     gain_attn,
@@ -263,6 +267,485 @@
     )
 
 
+F32 = jnp.float32
+BF16 = jnp.bfloat16
+MESH = pl.DeviceIdType.MESH
+TILE = 384
+PAIR = 2 * HV
+
+
+def nt(left, right):
+    return lax.dot_general(left, right, (((1,), (1,)), ((), ())), preferred_element_type=F32)
+
+
+def nn(left, right):
+    return jnp.dot(left, right, preferred_element_type=F32)
+
+
+def lanes_of(shape):
+    return lax.broadcasted_iota(jnp.int32, shape, len(shape) - 1)
+
+
+def first_visible(ends, positions):
+    start = jnp.zeros_like(positions)
+    for end in ends:
+        start = jnp.where(positions >= end, end, start)
+    return start
+
+
+def row_ends(doc_ref, row):
+    ends, total = [], 0
+    for j in range(doc_ref.shape[1] - 1):
+        total = total + doc_ref[row, j]
+        ends.append(total)
+    return ends
+
+
+def spread_matrix():
+    half = H * F
+    shape = (2 * half, (H // 2) * 128)
+    source = lax.broadcasted_iota(jnp.int32, shape, 0)
+    column = lax.broadcasted_iota(jnp.int32, shape, 1)
+    pair, lane = column // 128, column % 64
+    wanted = pair * 32 + lane + jnp.where(lane < 32, 0, half - 32)
+    return jnp.where(source == wanted, 1.0, 0.0).astype(BF16)
+
+
+def gather_matrix():
+    half = H * F
+    shape = (2 * half, 2 * half)
+    source = lax.broadcasted_iota(jnp.int32, shape, 0)
+    column = lax.broadcasted_iota(jnp.int32, shape, 1)
+    pair, lane = source // 64, source % 64
+    wanted = pair * 32 + lane + jnp.where(lane < 32, 0, half - 32)
+    return jnp.where(column == wanted, 1.0, 0.0).astype(BF16)
+
+
+def packed_rows(length):
+    return (length // 2 + 15) // 16 * 16
+
+
+def prepare_row(got_ref, row, qa_ref, ka_ref, ve_ref, seq_devices, length):
+    low = packed_rows(length)
+
+    def part(peer, carry):
+        values = got_ref[row, peer, :length, :].astype(F32)
+        packed = got_ref[row, peer, length : length + low, :].astype(F32)
+        turned = pltpu.roll(packed, 64, 1)
+        both = jnp.concatenate([packed, turned[2 * low - length :]], axis=0)
+        lane = lanes_of((length, 128))
+        keys = pltpu.roll(both, 96, 1)
+        at = pl.ds(pl.multiple_of(peer * length, 16), length)
+        one = jnp.where(lane == 32, 1.0, 0.0)
+        qa_ref[at, :] = jnp.where(lane < 32, both * 0.25, one).astype(BF16)
+        ka_ref[0, at, :] = jnp.where(lane < 16, keys, one).astype(BF16)
+        ka_ref[1, at, :] = jnp.where((lane >= 16) & (lane < 32), keys, one).astype(BF16)
+        ve_ref[0, at, :] = jnp.where(lane < 64, values, 1.0).astype(BF16)
+        ve_ref[1, at, :] = jnp.where(lane >= 64, values, 1.0).astype(BF16)
+        return carry
+
+    lax.fori_loop(0, seq_devices, part, 0)
+
+
+def attend_forward(ends, qa_ref, ka_ref, ve_ref, mixed_ref, inverse_ref):
+    length = qa_ref.shape[0]
+    for block in range(length // TILE):
+        reach = (block + 1) * TILE
+        at = pl.ds(block * TILE, TILE)
+        queries = qa_ref[at, :]
+        t = lax.broadcasted_iota(jnp.int32, (TILE, 1), 0) + block * TILE
+        start = first_visible(ends, t)
+        s = lax.broadcasted_iota(jnp.int32, (TILE, reach), 1)
+        visible = (s >= start) & (s <= t)
+        sums = []
+        for head in range(2):
+            base = nt(queries, ka_ref[head, :reach, :])
+            weights = jnp.where(visible, base * base + 1.0, 0.0).astype(BF16)
+            sums.append(nn(weights, ve_ref[head, :reach, :]))
+        lower = lanes_of((TILE, 128)) < 64
+        numerator = jnp.where(lower, sums[0], sums[1])
+        inverse = 1.0 / pltpu.roll(jnp.where(lower, sums[1], sums[0]), 64, 1)
+        mixed_ref[at, :] = (numerator * inverse).astype(BF16)
+        inverse_ref[at, :] = inverse
+
+
+def attend_backward(
+    ends, grad_ref, qa_ref, ka_ref, ve_ref, mixed_ref, inverse_ref, dn_ref, qs_ref, kt_ref, dqt_ref, gqk_ref, gv_ref
+):
+    length = qa_ref.shape[0]
+    lane = lanes_of((length, 128))
+    lower = lane < 64
+    scaled = grad_ref[...].astype(F32) * inverse_ref[...]
+    away = pltpu.roll(-scaled * mixed_ref[...].astype(F32), 64, 1)
+    dn_ref[0] = jnp.where(lower, scaled, away).astype(BF16)
+    dn_ref[1] = jnp.where(lower, away, scaled).astype(BF16)
+    shifted = pltpu.roll(qa_ref[...].astype(F32), 32, 1)
+    qs_ref[...] = jnp.where((lane >= 32) & (lane < 64), shifted * 2.0, 0.0).astype(BF16)
+    for head in range(2):
+        kt_ref[head] = ka_ref[head].astype(F32).T[:32].astype(BF16)
+    dqt_ref[...] = jnp.zeros_like(dqt_ref)
+    for block in range(length // TILE):
+        first = block * TILE
+        at = pl.ds(first, TILE)
+        rest = pl.ds(first, length - first)
+        shape = (TILE, length - first)
+        t = lax.broadcasted_iota(jnp.int32, (1, shape[1]), 1) + first
+        s = lax.broadcasted_iota(jnp.int32, shape, 0) + first
+        visible = (s >= first_visible(ends, t)) & (s <= t)
+        value_sums, key_sums = [], []
+        for head in range(2):
+            base = nt(ka_ref[head, at, :], qa_ref[rest, :])
+            grad_weights = nt(ve_ref[head, at, :], dn_ref[head, rest, :])
+            weights = jnp.where(visible, base * base + 1.0, 0.0).astype(BF16)
+            grad_base = jnp.where(visible, grad_weights * base, 0.0).astype(BF16)
+            value_sums.append(nn(weights, dn_ref[head, rest, :]))
+            key_sums.append(nn(grad_base, qs_ref[rest, :]))
+            dqt_ref[:, rest] += nn(kt_ref[head, :, at], grad_base)
+        lane = lanes_of((TILE, 128))
+        gv_ref[at, :] = jnp.where(lane < 64, value_sums[0], value_sums[1]).astype(BF16)
+        gqk_ref[at, :] = jnp.where(
+            (lane >= 32) & (lane < 48), key_sums[0], jnp.where((lane >= 48) & (lane < 64), key_sums[1], 0.0)
+        )
+    queries = jnp.concatenate([dqt_ref[...] * 0.5, jnp.zeros((96, length), F32)], axis=0)
+    gqk_ref[...] += queries.T
+
+
+def greet(seq_devices):
+    row_group, me = lax.axis_index("dp"), lax.axis_index("seq")
+    barrier = pltpu.get_barrier_semaphore()
+    for step in range(1, seq_devices):
+        peer = lax.rem(me + step, seq_devices)
+        pl.semaphore_signal(barrier, inc=1, device_id=(row_group, peer), device_id_type=MESH)
+    pl.semaphore_wait(barrier, seq_devices - 1)
+    return row_group, me
+
+
+def sending(source, target, send_sem, recv_sem, row_group, peer):
+    return pltpu.make_async_remote_copy(
+        src_ref=source,
+        dst_ref=target,
+        send_sem=send_sem,
+        recv_sem=recv_sem,
+        device_id=(row_group, peer),
+        device_id_type=MESH,
+    )
+
+
+def forward_kernel(
+    seq_devices, rows, length,
+    x_ref, doc_ref, gain_ref, wq_ref, wk_ref, wv_ref,
+    branch_ref, got_out, head_out, inverse_ref,
+    out_buf, got, heads, back, spread, qa, ka, ve, send_a, recv_a, send_b, recv_b,
+):
+    row_group, me = greet(seq_devices)
+    low = packed_rows(length)
+    lower = lanes_of((low, 128)) < 64
+    spread[...] = spread_matrix()
+
+    def outgoing(row, step):
+        peer = lax.rem(me + step, seq_devices)
+        return sending(
+            out_buf.at[row, peer], got.at[row, me], send_a.at[row, step], recv_a.at[row, step], row_group, peer
+        )
+
+    def returning(row, step):
+        peer = lax.rem(me + step, seq_devices)
+        there = pl.ds(pl.multiple_of(peer * length, 16), length)
+        mine = pl.ds(pl.multiple_of(me * PAIR, 128), PAIR)
+        return sending(
+            heads.at[row, there, :], back.at[row, :, mine], send_b.at[row, step], recv_b.at[row, step], row_group, peer
+        )
+
+    def project_row(row, carry):
+        stream = x_ref[row].astype(F32)
+        normed = rms_scale(stream, gain_ref[...]).astype(BF16)
+        both = jnp.concatenate([nn(normed, wq_ref[...]), nn(normed, wk_ref[...])], axis=1).astype(BF16)
+        tiles = nn(both, spread[...])
+        values = nn(normed, wv_ref[...]).astype(BF16)
+        for pair in range(seq_devices):
+            tile = tiles[:, pair * 128 : (pair + 1) * 128]
+            out_buf[row, pair, :length, :] = values[:, pair * PAIR : (pair + 1) * PAIR]
+            out_buf[row, pair, length:, :] = jnp.where(lower, tile[:low], tile[length - low :]).astype(BF16)
+        for step in range(1, seq_devices):
+            outgoing(row, step).start()
+        got[row, me] = out_buf[row, me]
+        return carry
+
+    lax.fori_loop(0, rows, project_row, 0)
+
+    def attend(row, carry):
+        for step in range(1, seq_devices):
+            outgoing(row, step).wait_recv()
+        prepare_row(got, row, qa, ka, ve, seq_devices, length)
+        attend_forward(row_ends(doc_ref, row), qa, ka, ve, heads.at[row], inverse_ref.at[row])
+        for step in range(1, seq_devices):
+            returning(row, step).start()
+        here = pl.ds(pl.multiple_of(me * length, 16), length)
+        back[row, :, pl.ds(pl.multiple_of(me * PAIR, 128), PAIR)] = heads[row, here, :]
+        return carry
+
+    lax.fori_loop(0, rows, attend, 0)
+    got_out[...] = got[...]
+    head_out[...] = heads[...]
+
+    def finish(row, carry):
+        for step in range(1, seq_devices):
+            outgoing(row, step).wait_send()
+            returning(row, step).wait()
+        branch_ref[row] = back[row]
+        return carry
+
+    lax.fori_loop(0, rows, finish, 0)
+
+
+def backward_kernel(
+    seq_devices, rows, length,
+    grad_ref, doc_ref, got, heads, inverse_ref,
+    gqk_out, gv_out,
+    arrived, out_buf, back, gather, qa, ka, ve, dn, qs, kt, dqt, gqk, gv, send_a, recv_a, send_b, recv_b,
+):
+    row_group, me = greet(seq_devices)
+    low = packed_rows(length)
+    lower = lanes_of((low, 128)) < 64
+    here = pl.ds(pl.multiple_of(me * length, 16), length)
+
+    def outgoing(row, step):
+        peer = lax.rem(me + step, seq_devices)
+        theirs = pl.ds(pl.multiple_of(peer * PAIR, 128), PAIR)
+        return sending(
+            grad_ref.at[row, :, theirs], arrived.at[row, here, :], send_a.at[row, step], recv_a.at[row, step],
+            row_group, peer,
+        )
+
+    def returning(row, step):
+        peer = lax.rem(me + step, seq_devices)
+        return sending(
+            out_buf.at[row, peer], back.at[row, me], send_b.at[row, step], recv_b.at[row, step], row_group, peer
+        )
+
+    def send_row(row, carry):
+        for step in range(1, seq_devices):
+            outgoing(row, step).start()
+        arrived[row, here, :] = grad_ref[row, :, pl.ds(pl.multiple_of(me * PAIR, 128), PAIR)]
+        return carry
+
+    lax.fori_loop(0, rows, send_row, 0)
+    gather[...] = gather_matrix()
+
+    def attend(row, carry):
+        prepare_row(got, row, qa, ka, ve, seq_devices, length)
+        for step in range(1, seq_devices):
+            outgoing(row, step).wait_recv()
+        attend_backward(
+            row_ends(doc_ref, row), arrived.at[row], qa, ka, ve, heads.at[row], inverse_ref.at[row],
+            dn, qs, kt, dqt, gqk, gv,
+        )
+
+        def pack(peer, inner):
+            at = pl.multiple_of(peer * length, 16)
+            out_buf[row, peer, :length, :] = gv[pl.ds(at, length), :]
+            first = gqk[pl.ds(at, low), :]
+            second = pltpu.roll(gqk[pl.ds(at + length - low, low), :], 64, 1)
+            out_buf[row, peer, length:, :] = jnp.where(lower, first, second).astype(BF16)
+            return inner
+
+        lax.fori_loop(0, seq_devices, pack, 0)
+        for step in range(1, seq_devices):
+            returning(row, step).start()
+        back[row, me] = out_buf[row, me]
+        return carry
+
+    lax.fori_loop(0, rows, attend, 0)
+
+    def finish(row, carry):
+        for step in range(1, seq_devices):
+            outgoing(row, step).wait_send()
+            returning(row, step).wait()
+        tiles = []
+        for pair in range(0, seq_devices, 2):
+            halves = []
+            for one in (pair, pair + 1):
+                packed = back[row, one, length:, :].astype(F32)
+                turned = pltpu.roll(packed, 64, 1)
+                if one == pair:
+                    halves.append(jnp.concatenate([packed, turned[2 * low - length :]], axis=0))
+                else:
+                    halves.append(jnp.concatenate([turned, packed[2 * low - length :]], axis=0))
+            tiles.append(jnp.where(lanes_of((length, 128)) < 64, halves[0], halves[1]).astype(BF16))
+        gqk_out[row] = nn(jnp.concatenate(tiles, axis=1), gather[...]).astype(BF16)
+        for pair in range(seq_devices):
+            gv_out[row, :, pair * PAIR : (pair + 1) * PAIR] = back[row, pair, :length, :]
+        return carry
+
+    lax.fori_loop(0, rows, finish, 0)
+
+
+VMEM_SPEC = pl.BlockSpec(memory_space=pltpu.VMEM)
+SMEM_SPEC = pl.BlockSpec(memory_space=pltpu.SMEM)
+
+
+def attention_forward(seq_devices, x, doc_lengths, gain, w_query, w_key, w_value):
+    rows, length, _ = x.shape
+    total = seq_devices * length
+    message = (rows, seq_devices, length + packed_rows(length), 128)
+    sems = pltpu.SemaphoreType.DMA((rows, seq_devices))
+    return pl.pallas_call(
+        functools.partial(forward_kernel, seq_devices, rows, length),
+        name="attention_forward",
+        out_shape=[
+            jax.ShapeDtypeStruct((rows, length, D), BF16),
+            jax.ShapeDtypeStruct(message, BF16),
+            jax.ShapeDtypeStruct((rows, total, 128), BF16),
+            jax.ShapeDtypeStruct((rows, total, 128), F32),
+        ],
+        in_specs=[VMEM_SPEC, SMEM_SPEC, VMEM_SPEC, VMEM_SPEC, VMEM_SPEC, VMEM_SPEC],
+        out_specs=[VMEM_SPEC] * 4,
+        scratch_shapes=[
+            pltpu.VMEM(message, BF16),
+            pltpu.VMEM(message, BF16),
+            pltpu.VMEM((rows, total, 128), BF16),
+            pltpu.VMEM((rows, length, D), BF16),
+            pltpu.VMEM((2 * H * F, D), BF16),
+            pltpu.VMEM((total, 128), BF16),
+            pltpu.VMEM((2, total, 128), BF16),
+            pltpu.VMEM((2, total, 128), BF16),
+            sems, sems, sems, sems,
+        ],
+        compiler_params=pltpu.CompilerParams(collective_id=0, has_side_effects=True, vmem_limit_bytes=56 << 20),
+    )(x, doc_lengths, gain.reshape(1, D), w_query, w_key, w_value)
+
+
+def attention_backward(seq_devices, grad, doc_lengths, got, heads, inverse):
+    rows, length, _ = grad.shape
+    total = seq_devices * length
+    message = (rows, seq_devices, length + packed_rows(length), 128)
+    sems = pltpu.SemaphoreType.DMA((rows, seq_devices))
+    return pl.pallas_call(
+        functools.partial(backward_kernel, seq_devices, rows, length),
+        name="attention_backward",
+        out_shape=[
+            jax.ShapeDtypeStruct((rows, length, 2 * H * F), BF16),
+            jax.ShapeDtypeStruct((rows, length, D), BF16),
+        ],
+        in_specs=[VMEM_SPEC, SMEM_SPEC, VMEM_SPEC, VMEM_SPEC, VMEM_SPEC],
+        out_specs=[VMEM_SPEC] * 2,
+        scratch_shapes=[
+            pltpu.VMEM((rows, total, 128), BF16),
+            pltpu.VMEM(message, BF16),
+            pltpu.VMEM(message, BF16),
+            pltpu.VMEM((2 * H * F, 2 * H * F), BF16),
+            pltpu.VMEM((total, 128), BF16),
+            pltpu.VMEM((2, total, 128), BF16),
+            pltpu.VMEM((2, total, 128), BF16),
+            pltpu.VMEM((2, total, 128), BF16),
+            pltpu.VMEM((total, 128), BF16),
+            pltpu.VMEM((2, 32, total), BF16),
+            pltpu.VMEM((32, total), F32),
+            pltpu.VMEM((total, 128), F32),
+            pltpu.VMEM((total, 128), BF16),
+            sems, sems, sems, sems,
+        ],
+        compiler_params=pltpu.CompilerParams(collective_id=1, has_side_effects=True, vmem_limit_bytes=56 << 20),
+    )(grad, doc_lengths, got, heads, inverse)
+
+
+def body(
+    seq_devices,
+    inputs,
+    doc_lengths,
+    gain_attn,
+    w_query,
+    w_key,
+    w_value,
+    w_out,
+    gain_ffn,
+    w_gate,
+    w_up,
+    w_down,
+    cotangent,
+):
+    row_count, shard_len, _ = inputs.shape
+    token_count = row_count * shard_len
+    stream = inputs.reshape(token_count, D).astype(jnp.float32)
+    normed, attn_norm_back = jax.vjp(rms_scale, stream, gain_attn)
+    normed_low = normed.astype(jnp.bfloat16)
+    branch, got, heads, inverse = attention_forward(
+        seq_devices, inputs, doc_lengths, gain_attn, w_query, w_key, w_value
+    )
+    mixed_flat = branch.reshape(token_count, D)
+    residual = stream + project(mixed_flat, w_out)
+    normed_ffn, ffn_norm_back = jax.vjp(rms_scale, residual, gain_ffn)
+    ffn_low = normed_ffn.astype(jnp.bfloat16)
+    gate_proj = project(ffn_low, w_gate)
+    up_proj = project(ffn_low, w_up)
+    hidden, act_back = jax.vjp(swiglu, gate_proj, up_proj)
+    hidden_low = hidden.astype(jnp.bfloat16)
+    output = residual + project(hidden_low, w_down)
+    grad_out = cotangent.reshape(token_count, D)
+    grad_gate, grad_up = act_back(back_project(grad_out, w_down))
+    grad_gate_low = grad_gate.astype(jnp.bfloat16)
+    grad_up_low = grad_up.astype(jnp.bfloat16)
+    down_grad_t = weight_grad(grad_out, hidden_low)
+    gate_grad = weight_grad(ffn_low, grad_gate_low)
+    up_grad = weight_grad(ffn_low, grad_up_low)
+    grad_normed_ffn = back_project(grad_gate_low, w_gate) + back_project(grad_up_low, w_up)
+    grad_residual, gain_ffn_grad = ffn_norm_back(grad_normed_ffn)
+    grad_residual = grad_residual + grad_out.astype(jnp.float32)
+    grad_branch = grad_residual.astype(jnp.bfloat16)
+    out_grad = weight_grad(mixed_flat, grad_branch)
+    grad_mixed = back_project(grad_branch, w_out).astype(jnp.bfloat16)
+    back_both, back_value = attention_backward(
+        seq_devices, grad_mixed.reshape(row_count, shard_len, D), doc_lengths, got, heads, inverse
+    )
+    back_query = back_both.reshape(token_count, 2 * H * F)[:, : H * F]
+    back_key = back_both.reshape(token_count, 2 * H * F)[:, H * F :]
+    back_value = back_value.reshape(token_count, D)
+    query_grad = weight_grad(normed_low, back_query)
+    key_grad = weight_grad(normed_low, back_key)
+    value_grad = weight_grad(normed_low, back_value)
+    grad_normed = (
+        back_project(back_query, w_query)
+        + back_project(back_key, w_key)
+        + back_project(back_value, w_value)
+    )
+    grad_stream, gain_attn_grad = attn_norm_back(grad_normed)
+    input_grad = grad_residual + grad_stream
+    (
+        gain_attn_part,
+        query_part,
+        key_part,
+        value_part,
+        out_part,
+        gain_ffn_part,
+        gate_part,
+        up_part,
+        down_part,
+    ) = (
+        lax.psum_scatter(gain_attn_grad, ("dp", "seq"), scatter_dimension=0, tiled=True),
+        lax.psum_scatter(query_grad, ("dp", "seq"), scatter_dimension=0, tiled=True),
+        lax.psum_scatter(key_grad, ("dp", "seq"), scatter_dimension=0, tiled=True),
+        lax.psum_scatter(value_grad, ("dp", "seq"), scatter_dimension=0, tiled=True),
+        lax.psum_scatter(out_grad, ("dp", "seq"), scatter_dimension=0, tiled=True),
+        lax.psum_scatter(gain_ffn_grad, ("dp", "seq"), scatter_dimension=0, tiled=True),
+        lax.psum_scatter(gate_grad, ("dp", "seq"), scatter_dimension=0, tiled=True),
+        lax.psum_scatter(up_grad, ("dp", "seq"), scatter_dimension=0, tiled=True),
+        lax.psum_scatter(down_grad_t, ("dp", "seq"), scatter_dimension=0, tiled=True),
+    )
+    return (
+        output.reshape(row_count, shard_len, D).astype(jnp.bfloat16),
+        input_grad.reshape(row_count, shard_len, D).astype(jnp.bfloat16),
+        gain_attn_part,
+        query_part,
+        key_part,
+        value_part,
+        out_part,
+        gain_ffn_part,
+        gate_part,
+        up_part,
+        jnp.transpose(down_part),
+    )
+
+
 def solution(mesh):
     in_specs = (
         P("dp", "seq", None),
@@ -291,4 +774,6 @@
         P(("dp", "seq"), None),
         P(None, ("dp", "seq")),
     )
-    return jax.shard_map(body, mesh=mesh, in_specs=in_specs, out_specs=out_specs, check_vma=False)
+    seq_devices = mesh.shape["seq"]
+    step = functools.partial(body, seq_devices) if seq_devices * 2 == H else general_body
+    return jax.shard_map(step, mesh=mesh, in_specs=in_specs, out_specs=out_specs, check_vma=False)

time: 1590 us -> 1150 us (0.72)
  matrix products: 332 us -> 89.3 us
  local copies, waits for them, and re-layouts: 169 us -> 13.3 us
  Pallas kernels: 0 us -> 72.7 us
  blocking collectives: 84.1 us -> 39.9 us
  other arithmetic: 38.7 us -> 5.34 us
  loops' own time: 30.8 us -> 0 us
  starting transfers between devices: 20.2 us -> 0.54 us
  waiting for transfers between devices: 889 us -> 906 us
    dot_general x36 -> x0, matrix products: 244 us -> none  [the longest x8 85.5 us: block_step(): jnp.einsum('hts,shv->thv', weights, value_block, precision=highest)]
    reduce_scatter x1, waiting for transfers between devices: 0.01 us -> 134 us  [body(): lax.psum_scatter(query_grad, ('dp', 'seq'), scatter_dimension=0, tiled=True)]
    pallas_call x0 -> x2, Pallas kernels: none -> 72.7 us  [the longest x1 36.9 us: attention_backward(): pl.pallas_call(functools.partial(backward_kernel, seq_devices, rows, leng...]
    reduce_scatter x1, waiting for transfers between devices: 105 us -> 32.9 us  [body(): lax.psum_scatter(key_grad, ('dp', 'seq'), scatter_dimension=0, tiled=True)]
    all_to_all x3 -> x0, blocking collectives: 44.5 us -> none  [the longest x1 18.2 us: body(): lax.all_to_all(grad_value.astype(jnp.bfloat16), 'seq', split_axis=1, conc...]
    all_to_all x5 -> x0, waiting for transfers between devices: 42.5 us -> none  [the longest x1 20.9 us: body(): lax.all_to_all(grad_mixed, 'seq', split_axis=2, concat_axis=1, tiled=True)]
    unnamed x91 -> x49, local copies, waits for them, and re-layouts: 48.7 us -> 13.2 us
    another operation x2 -> x0, loops' own time: 30.8 us -> none  [attend_row(): lax.scan(jax.checkpoint(block_step), initial, (query_blocks, key_blocks,...]
  transfers between devices with their start and end apart: 12 -> 7, of which waited for: 10 -> 7; matrix products, arithmetic and copies ran while one was open for 7% -> 5% of each run, Pallas kernels for 0% -> 0%
where the time goes in v1:
time: 1150 us; the launch traced here: 1140 us
  waiting for transfers between devices  906 us (79%)
  matrix products  89.3 us (8%)
  Pallas kernels  72.7 us (6%)
  blocking collectives  39.9 us (3%)
  between operations  14.9 us (1%)
  local copies, waits for them, and re-layouts  13.3 us (1%)
    unnamed x8, waiting for transfers between devices  154 us
    reduce_scatter x1, waiting for transfers between devices, body(): lax.psum_scatter(gate_grad, ('dp', 'seq'), scatter_dimension=0, tiled=True)  154 us
    reduce_scatter x1, waiting for transfers between devices, body(): lax.psum_scatter(up_grad, ('dp', 'seq'), scatter_dimension=0, tiled=True)  153 us
    reduce_scatter x1, waiting for transfers between devices, body(): lax.psum_scatter(out_grad, ('dp', 'seq'), scatter_dimension=0, tiled=True)  139 us
    reduce_scatter x1, waiting for transfers between devices, body(): lax.psum_scatter(value_grad, ('dp', 'seq'), scatter_dimension=0, tiled=True)  139 us
    reduce_scatter x1, waiting for transfers between devices, body(): lax.psum_scatter(query_grad, ('dp', 'seq'), scatter_dimension=0, tiled=True)  134 us
    dot_general x7, matrix products, weight_grad(): lax.dot_general(left, right, (((0,), (0,)), ((), ())), preferred_element_...  41.3 us
    unnamed x1, blocking collectives  39.9 us
  transfers between devices with their start and end apart: 7, of which 7 were waited for; matrix products, arithmetic and copies ran while one was open for 5% of the time, Pallas kernels for 0%

profile of v1, /device:TPU:0, one launch (start us, length us, event | category | flops | bytes accessed | tf_op | source)
XLA Modules:
  0.0 1142.3 jit_solution(18309344242901984634)
XLA Ops:
  7.2 1.6 multiply_reduce_fusion.3
  8.8 35.8 %attention_forward.1 = (bf16[3,144,1024]{2,1,0:T(8,128)(2,1)}, bf16[3,8,224,128]{3,2,1,0:T(8,128)(2,1)}, bf16[3,1152,128]{2,1,0:T(8,128)(2,1)}, f32[3,1152,128]{2,1,0:T(8,128)}) custom-call(bf16[3,144,1024]{2,1,0:T(8,128)(2,1)} %x_ref.1, s32[3,4]{1,0:T(4,128)} %doc_ref.3, f32[1,1024]{1,0:T(1,128)} %bitcast.62, bf16[1024,256]{1,0:T(8,128)(2,1)} %wq_ref.1, ...), custom_call_target="tpu_custom_call" | custom-call | tf_op jit(solution)/shard_map/attention_forward/pallas_call | solution.py:592
  44.7 2.5 multiply_reduce_fusion.5
  47.5 5.3 fusion.22
  52.9 5.4 fusion.23
  58.2 10.1 multiply_convert_fusion
  68.4 2.8 fusion.24
  71.2 3.1 multiply_reduce_fusion
  74.8 2.1 convolution_convert_fusion
  76.8 36.9 %attention_backward.1 = (bf16[3,144,512]{2,1,0:T(8,128)(2,1)}, bf16[3,144,1024]{2,1,0:T(8,128)(2,1)}) custom-call(bf16[3,144,1024]{2,1,0:T(8,128)(2,1)} %bitcast.61, s32[3,4]{1,0:T(4,128)} %doc_ref.3, bf16[3,8,224,128]{3,2,1,0:T(8,128)(2,1)} %get-tuple-element.18.got, bf16[3,1152,128]{2,1,0:T(8,128)(2,1)} %get-tuple-element.19.heads, ...), custom_call_target="tpu_custom_call" | custom-call | tf_op jit(solution)/shard_map/attention_backward/pallas_call | solution.py:623
  113.8 2.7 fusion.18
  116.5 3.6 fusion.25
  120.3 4.1 multiply_reduce_fusion.1
  124.3 1.5 fusion.13
  125.9 2.8 fusion.16
  128.7 4.4 fusion.10
  133.2 4.6 convolution_bitcast_fusion.1
  137.8 9.5 fusion.26
  147.4 9.4 fusion.27
  157.1 9.1 convolution_bitcast_fusion
  166.3 11.9 %copy.25 = f32[1024,2752]{1,0:T(8,128)} copy(f32[1024,2752]{0,1:T(8,128)} %convolution_bitcast_fusion) | data formatting | bytes 22544384
  178.2 39.9 %all-reduce.2 = (f32[1024]{0:T(1024)S(1)}, f32[1024]{0:T(1024)S(1)}) all-reduce(f32[1024]{0:T(1024)S(1)} %get-tuple-element.47, f32[1024]{0:T(1024)S(1)} %get-tuple-element.45), channel_id=2, replica_groups=mesh['dp'=4,'seq'=8] {'dp','seq'}, use_global_device_ids=true, to_apply=%region_5.6.clone | all-reduce | flops 2048 | bytes 16384
  218.1 0.6 dynamic-slice
  219.2 3.0 fusion.6
  222.3 6.4 add_convert_fusion
  228.7 32.9 %reduce-scatter.12.cloned.1.call-done = f32[32,256]{1,0:T(8,128)} async-done(((f32[1024,256]{1,0:T(8,128)}), f32[32,256]{1,0:T(8,128)}) %reduce-scatter.12.cloned.1.call-update) | async-done | bytes 32784 | tf_op jit(solution)/shard_map/reduce_scatter | solution.py:726
  261.6 133.7 %reduce-scatter.10.cloned.1.call-done = f32[32,256]{1,0:T(8,128)} async-done(((f32[1024,256]{1,0:T(8,128)}), f32[32,256]{1,0:T(8,128)}) %reduce-scatter.10.cloned.1.call-update) | async-done | bytes 32784 | tf_op jit(solution)/shard_map/reduce_scatter | solution.py:725
  395.3 139.5 %reduce-scatter.16.cloned.1.call-done = f32[32,1024]{1,0:T(8,128)} async-done(((f32[1024,1024]{1,0:T(8,128)}), f32[32,1024]{1,0:T(8,128)}) %reduce-scatter.16.cloned.1.call-update) | async-done | bytes 131088 | tf_op jit(solution)/shard_map/reduce_scatter | solution.py:728
  534.8 139.5 %reduce-scatter.14.cloned.1.call-done = f32[32,1024]{1,0:T(8,128)} async-done(((f32[1024,1024]{1,0:T(8,128)}), f32[32,1024]{1,0:T(8,128)}) %reduce-scatter.14.cloned.1.call-update) | async-done | bytes 131088 | tf_op jit(solution)/shard_map/reduce_scatter | solution.py:727
  674.3 153.7 %reduce-scatter.18.cloned.1.call-done = f32[32,2752]{1,0:T(8,128)} async-done(((f32[1024,2752]{1,0:T(8,128)}), f32[32,2752]{1,0:T(8,128)}) %reduce-scatter.18.cloned.1.call-update) | async-done | bytes 352272 | tf_op jit(solution)/shard_map/reduce_scatter | solution.py:730
  827.9 153.4 %reduce-scatter.20.cloned.1.call-done = f32[32,2752]{1,0:T(8,128)} async-done(((f32[1024,2752]{1,0:T(8,128)}), f32[32,2752]{1,0:T(8,128)}) %reduce-scatter.20.cloned.1.call-update) | async-done | bytes 352272 | tf_op jit(solution)/shard_map/reduce_scatter | solution.py:731
  981.4 153.7 %reduce-scatter.22.cloned.1.call-done = f32[32,2752]{1,0:T(8,128)} async-done(((f32[1024,2752]{1,0:T(8,128)}), f32[32,2752]{1,0:T(8,128)}) %reduce-scatter.22.cloned.1.call-update) | async-done | bytes 352272
  (71 shorter events, 2.3 us)
Async XLA Ops:
  7.2 37.4 %copy-start = (bf16[1024,1024]{1,0:T(8,128)(2,1)S(1)}, bf16[1024,1024]{1,0:T(8,128)(2,1)}, u32[]{:S(2)}) copy-start(bf16[1024,1024]{1,0:T(8,128)(2,1)} %param.18) | copy-start | bytes 6291460
  7.2 254.4 %reduce-scatter.12.cloned.1.call-start = ((), (), s32[]{:S(2)}) async-start(), calls=%async_computation.8 | async-start | bytes 1081344 | tf_op jit(solution)/shard_map/reduce_scatter | solution.py:726
  8.8 35.8 %copy-start.2 = (bf16[3,144,1024]{2,1,0:T(8,128)(2,1)S(1)}, bf16[3,144,1024]{2,1,0:T(8,128)(2,1)}, u32[]{:S(2)}) copy-start(bf16[3,144,1024]{2,1,0:T(8,128)(2,1)} %x_ref.1) | copy-start | bytes 2654212
  44.6 2.8 slice-start
  44.6 2.6 copy-start.15
  44.6 2.9 slice-start.1
  47.2 27.1 %copy-start.6 = (f32[432,1024]{1,0:T(8,128)}, f32[432,1024]{1,0:T(8,128)S(1)}, u32[]{:S(2)}) copy-start(f32[432,1024]{1,0:T(8,128)S(1)} %get-tuple-element.58) | copy-start | bytes 5308420
  47.2 5.6 slice-start.2
  47.5 5.3 copy-start.13
  47.5 5.3 slice-start.3
  52.9 5.4 copy-start.12
  68.3 2.8 copy-start.17
  68.3 2.8 copy-start.16
  74.8 2.1 copy-start.3
  76.8 36.9 %copy-start.8 = (bf16[1024,256]{1,0:T(8,128)(2,1)S(1)}, bf16[1024,256]{1,0:T(8,128)(2,1)}, u32[]{:S(2)}) copy-start(bf16[1024,256]{1,0:T(8,128)(2,1)} %wq_ref.1) | copy-start | bytes 1572868
  113.8 2.7 copy-start.9
  116.5 3.7 copy-start.10
  116.5 3.7 copy-start.11
  116.5 3.7 copy-start.14
  124.3 1.5 copy-start.5
  125.8 2.9 copy-start.4
  125.8 269.5 %reduce-scatter.10.cloned.1.call-start = ((), (), s32[]{:S(2)}) async-start(), calls=%async_computation.7 | async-start | bytes 1081344 | tf_op jit(solution)/shard_map/reduce_scatter | solution.py:725
  128.7 406.2 %reduce-scatter.16.cloned.1.call-start = ((), (), s32[]{:S(2)}) async-start(), calls=%async_computation.10 | async-start | bytes 4325376 | tf_op jit(solution)/shard_map/reduce_scatter | solution.py:728
  133.1 541.1 %reduce-scatter.14.cloned.1.call-start = ((), (), s32[]{:S(2)}) async-start(), calls=%async_computation.9 | async-start | bytes 4325376 | tf_op jit(solution)/shard_map/reduce_scatter | solution.py:727
  137.8 690.2 %reduce-scatter.18.cloned.1.call-start = ((), (), s32[]{:S(2)}) async-start(), calls=%async_computation.11 | async-start | bytes 11894784 | tf_op jit(solution)/shard_map/reduce_scatter | solution.py:730
  147.4 834.0 %reduce-scatter.20.cloned.1.call-start = ((), (), s32[]{:S(2)}) async-start(), calls=%async_computation.12 | async-start | bytes 11894784 | tf_op jit(solution)/shard_map/reduce_scatter | solution.py:731
  156.8 978.2 %reduce-scatter.22.cloned.1.call-start = ((), (), s32[]{:S(2)}) async-start(), calls=%async_computation.13 | async-start | bytes 11894784
  219.2 3.0 copy-start.7
  219.2 3.0 copy-start.18
  222.3 912.8 %copy-start.1 = (bf16[1024,1024]{1,0:T(8,128)(2,1)S(1)}, bf16[1024,1024]{1,0:T(8,128)(2,1)}, u32[]{:S(2)}) copy-start(bf16[1024,1024]{1,0:T(8,128)(2,1)} %param.18) | copy-start | bytes 6291460
Sparse Core Ops, SparseCore 0:
  125.9 135.6 reduce-scatter.11
  264.5 130.7 reduce-scatter.9
  398.2 136.5 reduce-scatter.15
  537.5 136.7 reduce-scatter.13
  677.0 150.8 reduce-scatter.17
  830.7 150.6 reduce-scatter.19
  984.3 150.7 reduce-scatter.21

commit v2 on v1

--- a/solution.py
+++ b/solution.py
@@ -498,88 +498,6 @@
     lax.fori_loop(0, rows, finish, 0)
 
 
-def backward_kernel(
-    seq_devices, rows, length,
-    grad_ref, doc_ref, got, heads, inverse_ref,
-    gqk_out, gv_out,
-    arrived, out_buf, back, gather, qa, ka, ve, dn, qs, kt, dqt, gqk, gv, send_a, recv_a, send_b, recv_b,
-):
-    row_group, me = greet(seq_devices)
-    low = packed_rows(length)
-    lower = lanes_of((low, 128)) < 64
-    here = pl.ds(pl.multiple_of(me * length, 16), length)
-
-    def outgoing(row, step):
-        peer = lax.rem(me + step, seq_devices)
-        theirs = pl.ds(pl.multiple_of(peer * PAIR, 128), PAIR)
-        return sending(
-            grad_ref.at[row, :, theirs], arrived.at[row, here, :], send_a.at[row, step], recv_a.at[row, step],
-            row_group, peer,
-        )
-
-    def returning(row, step):
-        peer = lax.rem(me + step, seq_devices)
-        return sending(
-            out_buf.at[row, peer], back.at[row, me], send_b.at[row, step], recv_b.at[row, step], row_group, peer
-        )
-
-    def send_row(row, carry):
-        for step in range(1, seq_devices):
-            outgoing(row, step).start()
-        arrived[row, here, :] = grad_ref[row, :, pl.ds(pl.multiple_of(me * PAIR, 128), PAIR)]
-        return carry
-
-    lax.fori_loop(0, rows, send_row, 0)
-    gather[...] = gather_matrix()
-
-    def attend(row, carry):
-        prepare_row(got, row, qa, ka, ve, seq_devices, length)
-        for step in range(1, seq_devices):
-            outgoing(row, step).wait_recv()
-        attend_backward(
-            row_ends(doc_ref, row), arrived.at[row], qa, ka, ve, heads.at[row], inverse_ref.at[row],
-            dn, qs, kt, dqt, gqk, gv,
-        )
-
-        def pack(peer, inner):
-            at = pl.multiple_of(peer * length, 16)
-            out_buf[row, peer, :length, :] = gv[pl.ds(at, length), :]
-            first = gqk[pl.ds(at, low), :]
-            second = pltpu.roll(gqk[pl.ds(at + length - low, low), :], 64, 1)
-            out_buf[row, peer, length:, :] = jnp.where(lower, first, second).astype(BF16)
-            return inner
-
-        lax.fori_loop(0, seq_devices, pack, 0)
-        for step in range(1, seq_devices):
-            returning(row, step).start()
-        back[row, me] = out_buf[row, me]
-        return carry
-
-    lax.fori_loop(0, rows, attend, 0)
-
-    def finish(row, carry):
-        for step in range(1, seq_devices):
-            outgoing(row, step).wait_send()
-            returning(row, step).wait()
-        tiles = []
-        for pair in range(0, seq_devices, 2):
-            halves = []
-            for one in (pair, pair + 1):
-                packed = back[row, one, length:, :].astype(F32)
-                turned = pltpu.roll(packed, 64, 1)
-                if one == pair:
-                    halves.append(jnp.concatenate([packed, turned[2 * low - length :]], axis=0))
-                else:
-                    halves.append(jnp.concatenate([turned, packed[2 * low - length :]], axis=0))
-            tiles.append(jnp.where(lanes_of((length, 128)) < 64, halves[0], halves[1]).astype(BF16))
-        gqk_out[row] = nn(jnp.concatenate(tiles, axis=1), gather[...]).astype(BF16)
-        for pair in range(seq_devices):
-            gv_out[row, :, pair * PAIR : (pair + 1) * PAIR] = back[row, pair, :length, :]
-        return carry
-
-    lax.fori_loop(0, rows, finish, 0)
-
-
 VMEM_SPEC = pl.BlockSpec(memory_space=pltpu.VMEM)
 SMEM_SPEC = pl.BlockSpec(memory_space=pltpu.SMEM)
 
@@ -615,20 +533,606 @@
     )(x, doc_lengths, gain.reshape(1, D), w_query, w_key, w_value)
 
 
-def attention_backward(seq_devices, grad, doc_lengths, got, heads, inverse):
+CHUNK = 256
+STEP_ROWS = 48
+EARLY = 4
+
+
+def place(me):
+    core = lax.rem(me, 2)
+    return core, 2 + 2 * core, 4 - 2 * core
+
+
+def blocks_of(core, groups):
+    first, second = 2 + 2 * core, 4 - 2 * core
+    return [
+        pl.multiple_of(32 * (8 * group + first * i + second * j + core), 32)
+        for i in range(2)
+        for j in range(2)
+        for group in range(groups)
+    ]
+
+
+class Reduction:
+    def __init__(self, groups, source, got_a, got_b, got_z, a_sems, b_sems, z_send, z_recv):
+        self.groups, self.source = groups, source
+        self.got_a, self.got_b, self.got_z = got_a, got_b, got_z
+        self.a_sems, self.b_sems, self.z_send, self.z_recv = a_sems, b_sems, z_send, z_recv
+        self.group, self.me = lax.axis_index("dp"), lax.axis_index("seq")
+        core, first, second = place(self.me)
+        self.bit_a, self.bit_b = lax.rem(self.me // first, 2), lax.rem(self.me // second, 2)
+        self.peer_a = self.me + first * (1 - 2 * self.bit_a)
+        self.peer_b = self.me + second * (1 - 2 * self.bit_b)
+
+    def a_copy(self, unit):
+        return sending(
+            self.source.at[unit, 1 - self.bit_a], self.got_a.at[unit], self.a_sems.at[0, unit],
+            self.a_sems.at[1, unit], self.group, self.peer_a,
+        )
+
+    def b_copy(self, unit):
+        return sending(
+            self.got_a.at[unit, 1 - self.bit_b], self.got_b.at[unit], self.b_sems.at[0, unit],
+            self.b_sems.at[1, unit], self.group, self.peer_b,
+        )
+
+    def z_copy(self, unit, step):
+        other = lax.rem(self.group + step, self.groups)
+        block = pl.ds(pl.multiple_of(other * 32, 32), 32)
+        return sending(
+            self.got_b.at[unit, block, :], self.got_z.at[unit, step - 1], self.z_send.at[unit, step - 1],
+            self.z_recv.at[unit, step - 1], other, self.me,
+        )
+
+    def a_step(self, unit):
+        self.a_copy(unit).wait_recv()
+        self.got_a[unit] = (self.source[unit, self.bit_a].astype(F32) + self.got_a[unit].astype(F32)).astype(BF16)
+        self.b_copy(unit).start()
+
+    def b_step(self, unit):
+        self.b_copy(unit).wait_recv()
+        self.got_b[unit] = (self.got_a[unit, self.bit_b].astype(F32) + self.got_b[unit].astype(F32)).astype(BF16)
+        for step in range(1, self.groups):
+            self.z_copy(unit, step).start()
+
+    def z_step(self, unit):
+        total = self.got_b[unit, pl.ds(pl.multiple_of(self.group * 32, 32), 32), :].astype(F32)
+        for step in range(1, self.groups):
+            self.z_copy(unit, step).wait_recv()
+            total += self.got_z[unit, step - 1].astype(F32)
+        return total
+
+    def wait_sent(self, unit):
+        self.a_copy(unit).wait_send()
+        self.b_copy(unit).wait_send()
+        for step in range(1, self.groups):
+            self.z_copy(unit, step).wait_send()
+
+
+def reduction_scratch(groups, units, cols, source=True):
+    rows = 32 * groups
+    dma = pltpu.SemaphoreType.DMA
+    buffers = [pltpu.VMEM((units, 2, 2, rows, cols), BF16)] if source else []
+    return buffers + [
+        pltpu.VMEM((units, 2, rows, cols), BF16),
+        pltpu.VMEM((units, rows, cols), BF16),
+        pltpu.VMEM((units, groups - 1, 32, cols), BF16),
+        dma((2, units)),
+        dma((2, units)),
+        dma((units, groups - 1)),
+        dma((units, groups - 1)),
+    ]
+
+
+def store_blocks(target, unit, col, values, groups):
+    rows = 32 * groups
+    for i in range(2):
+        for j in range(2):
+            at = (2 * i + j) * rows
+            target[unit, i, j, :, col : col + values.shape[1]] = values[at : at + rows].astype(BF16)
+
+
+def turn(source, tokens, padded, turned):
+    turned[...] = jnp.concatenate([source, jnp.zeros((padded - tokens, D), BF16)], axis=0).T
+
+
+def split_rows(turned, mine_ref, theirs_ref, core, groups):
+    padded = turned.shape[1]
+    for i, (mine, theirs) in enumerate(zip(blocks_of(core, groups), blocks_of(1 - core, groups))):
+        mine_ref[i * 32 : (i + 1) * 32, :padded] = turned[pl.ds(mine, 32), :]
+        theirs_ref[i * 32 : (i + 1) * 32, :] = turned[pl.ds(theirs, 32), :]
+
+
+def write_unit(total, at, w, gate_out, up_out, down_out):
+    down_out[:, pl.ds(at, w)] = total[:, :w]
+    gate_out[:, pl.ds(at, w)] = total[:, CHUNK : CHUNK + w]
+    up_out[:, pl.ds(at, w)] = total[:, 2 * CHUNK : 2 * CHUNK + w]
+
+
+def ffn_kernel(
+    groups, tokens, width,
+    branch_ref, x_ref, cot_ref, gain_ref, wo_ref, wg_hbm, wu_hbm, wd_hbm,
+    output_ref, gres_ref, gmixed_ref, gate_out, up_out, down_out, rest, parts_o, gain_out,
+    residual, normed, out_acc, gnf, w_buf, turned, lhs, lhs_send, right, right_out, parts,
+    got_a, got_b, got_z, a_sems, b_sems, z_send, z_recv, w_sem, lhs_sems, pair_sems,
+):
+    row_group, me = lax.axis_index("dp"), lax.axis_index("seq")
+    core, _, _ = place(me)
+    partner = me + 1 - 2 * core
+    reduction = Reduction(groups, parts, got_a, got_b, got_z, a_sems, b_sems, z_send, z_recv)
+    full = width // CHUNK
+    tail = width - full * CHUNK
+    padded = turned.shape[1]
+
+    barrier = pltpu.get_barrier_semaphore()
+    for peer in (partner, reduction.peer_a, reduction.peer_b):
+        pl.semaphore_signal(barrier, inc=1, device_id=(row_group, peer), device_id_type=MESH)
+    for step in range(1, groups):
+        other = lax.rem(row_group + step, groups)
+        pl.semaphore_signal(barrier, inc=1, device_id=(other, me), device_id_type=MESH)
+
+    def loads(chunk, slot, w):
+        at = pl.ds(pl.multiple_of(chunk * CHUNK, CHUNK), w)
+        return [
+            pltpu.make_async_copy(hbm.at[at, :], w_buf.at[slot, which, pl.ds(0, w), :], w_sem.at[slot, which])
+            for which, hbm in enumerate((wg_hbm, wu_hbm, wd_hbm))
+        ]
+
+    for copy in loads(0, 0, CHUNK):
+        copy.start()
+
+    def norm_forward(step, carry):
+        at = pl.ds(pl.multiple_of(step * STEP_ROWS, 16), STEP_ROWS)
+        value = x_ref[at, :].astype(F32) + residual[at, :]
+        residual[at, :] = value
+        out_acc[at, :] = value
+        normed[at, :] = rms_scale(value, gain_ref[...]).astype(BF16)
+        return carry
+
+    residual[...] = nn(branch_ref[...], wo_ref[...])
+    lax.fori_loop(0, tokens // STEP_ROWS, norm_forward, 0)
+    gnf[...] = jnp.zeros_like(gnf)
+
+    pl.semaphore_wait(barrier, 2 + groups)
+
+    def lhs_copy(which):
+        return sending(
+            lhs_send.at[which], lhs.at[which, :, pl.ds(padded, padded)],
+            lhs_sems.at[0, which], lhs_sems.at[1, which], row_group, partner,
+        )
+
+    for which, source in enumerate((cot_ref, normed, branch_ref)):
+        turn(source[...], tokens, padded, turned)
+        split_rows(turned, lhs.at[which], lhs_send.at[which], core, groups)
+        lhs_copy(which).start()
+    slots = right.shape[0]
+    gap = padded - tokens
+    for base in (tokens, padded + tokens):
+        right[:, base : base + gap, :] = jnp.zeros((slots, gap, 3 * CHUNK), BF16)
+        right_out[base : base + gap, :] = jnp.zeros((gap, D), BF16)
+
+    def pair_copy(chunk):
+        slot = lax.rem(chunk, slots)
+        return sending(
+            right.at[slot, pl.ds(0, tokens), :], right.at[slot, pl.ds(padded, tokens), :],
+            pair_sems.at[0, chunk], pair_sems.at[1, chunk], row_group, partner,
+        )
+
+    def forward_part(chunk, wg, wu, wd, w):
+        slot = lax.rem(chunk, slots)
+        gate = nt(normed[...], wg)
+        up = nt(normed[...], wu)
+        sigmoid = 1.0 / (1.0 + jnp.exp(-gate))
+        silu = gate * sigmoid
+        hidden = (silu * up).astype(BF16)
+        grad_hidden = nt(cot_ref[...], wd)
+        grad_gate = (grad_hidden * up * (sigmoid * (1.0 + gate * (1.0 - sigmoid)))).astype(BF16)
+        grad_up = (grad_hidden * silu).astype(BF16)
+        for part, values in enumerate((hidden, grad_gate, grad_up)):
+            right[slot, :tokens, part * CHUNK : part * CHUNK + w] = values
+            if w < CHUNK:
+                right[slot, :tokens, part * CHUNK + w : (part + 1) * CHUNK] = jnp.zeros((tokens, CHUNK - w), BF16)
+        pair_copy(chunk).start()
+        out_acc[...] += nn(hidden, wd)
+        gnf[...] += nn(grad_gate, wg) + nn(grad_up, wu)
+
+    def grad_part(chunk, early):
+        pair_copy(chunk).wait()
+        slot = lax.rem(chunk, slots)
+        down = nn(lhs[0], right[slot, :, 0:CHUNK])
+        both = nn(lhs[1], right[slot, :, CHUNK:])
+        target, unit = (parts, chunk) if early else (rest, chunk - EARLY)
+        store_blocks(target, unit, 0, down, groups)
+        store_blocks(target, unit, CHUNK, both, groups)
+        if early:
+            reduction.a_copy(chunk).start()
+
+    for which in range(3):
+        lhs_copy(which).wait()
+
+    def forward_step(chunk):
+        slot = lax.rem(chunk, 2)
+        for copy in loads(chunk, slot, CHUNK):
+            copy.wait()
+        forward_part(chunk, w_buf[slot, 0], w_buf[slot, 1], w_buf[slot, 2], CHUNK)
+
+    def main(early, chunk, carry):
+        for copy in loads(chunk + 1, lax.rem(chunk + 1, 2), CHUNK):
+            copy.start()
+        forward_step(chunk)
+        grad_part(chunk - 1, early)
+
+        @pl.when((chunk >= 4) & (chunk < 4 + EARLY))
+        def _():
+            reduction.a_step(chunk - 4)
+
+        @pl.when((chunk >= 6) & (chunk < 6 + EARLY))
+        def _():
+            reduction.b_step(chunk - 6)
+
+        return carry
+
+    for copy in loads(1, 1, CHUNK):
+        copy.start()
+    forward_step(0)
+    lax.fori_loop(1, EARLY + 1, functools.partial(main, True), 0)
+    lax.fori_loop(EARLY + 1, full - 1, functools.partial(main, False), 0)
+    for copy in loads(full, full % 2, tail):
+        copy.start()
+    forward_step(full - 1)
+    grad_part(full - 2, False)
+    for unit in range(max(0, full - 5), EARLY):
+        reduction.a_step(unit)
+    for unit in range(max(0, full - 7), EARLY):
+        reduction.b_step(unit)
+    for copy in loads(full, full % 2, tail):
+        copy.wait()
+    slot = full % 2
+    forward_part(full, w_buf[slot, 0, :tail], w_buf[slot, 1, :tail], w_buf[slot, 2, :tail], tail)
+    grad_part(full - 1, False)
+
+    gain_out[...] = jnp.zeros_like(gain_out)
+
+    def norm_backward(step, carry):
+        at = pl.ds(pl.multiple_of(step * STEP_ROWS, 16), STEP_ROWS)
+        value, grad = residual[at, :], gnf[at, :]
+        scale = lax.rsqrt(jnp.mean(value * value, axis=-1, keepdims=True) + eps_norm)
+        gain_out[0:1, :] += jnp.sum(grad * value * scale, axis=0, keepdims=True)
+        weighted = grad * gain_ref[...]
+        mean = jnp.mean(weighted * value, axis=-1, keepdims=True)
+        total = cot_ref[at, :].astype(F32) + scale * weighted - value * (scale * scale * scale * mean)
+        gres_ref[at, :] = total
+        right_out[at, :] = total.astype(BF16)
+        output_ref[at, :] = out_acc[at, :].astype(BF16)
+        return carry
+
+    lax.fori_loop(0, tokens // STEP_ROWS, norm_backward, 0)
+    out_pair = sending(
+        right_out.at[pl.ds(0, tokens), :], right_out.at[pl.ds(padded, tokens), :],
+        pair_sems.at[0, full + 1], pair_sems.at[1, full + 1], row_group, partner,
+    )
+    out_pair.start()
+    grad_part(full, False)
+    gmixed_ref[...] = nt(right_out[:tokens, :], wo_ref[...]).astype(BF16)
+    out_pair.wait()
+    for col in range(0, D, CHUNK):
+        store_blocks(parts_o, 0, col, nn(lhs[2], right_out[:, col : col + CHUNK]), groups)
+
+    def finish(unit, carry):
+        write_unit(reduction.z_step(unit), pl.multiple_of(unit * CHUNK, CHUNK), CHUNK, gate_out, up_out, down_out)
+        return carry
+
+    lax.fori_loop(0, EARLY, finish, 0)
+
+    def sent(unit, carry):
+        reduction.wait_sent(unit)
+        return carry
+
+    lax.fori_loop(0, EARLY, sent, 0)
+
+
+ANY_SPEC = pl.BlockSpec(memory_space=pl.ANY)
+
+
+def feed_forward(groups, branch, x, cotangent, gain, w_out, w_gate_t, w_up_t, w_down):
+    tokens = branch.shape[0]
+    width = w_down.shape[0]
+    full = width // CHUNK
+    padded = (tokens + 127) // 128 * 128
+    cols = 3 * CHUNK
+    rows = 32 * groups
+    dma = pltpu.SemaphoreType.DMA
+    return pl.pallas_call(
+        functools.partial(ffn_kernel, groups, tokens, width),
+        name="feed_forward",
+        out_shape=[
+            jax.ShapeDtypeStruct((tokens, D), BF16),
+            jax.ShapeDtypeStruct((tokens, D), F32),
+            jax.ShapeDtypeStruct((tokens, D), BF16),
+            jax.ShapeDtypeStruct((32, EARLY * CHUNK), F32),
+            jax.ShapeDtypeStruct((32, EARLY * CHUNK), F32),
+            jax.ShapeDtypeStruct((32, EARLY * CHUNK), F32),
+            jax.ShapeDtypeStruct((full + 1 - EARLY, 2, 2, rows, cols), BF16),
+            jax.ShapeDtypeStruct((1, 2, 2, rows, D), BF16),
+            jax.ShapeDtypeStruct((8, D), F32),
+        ],
+        in_specs=[VMEM_SPEC] * 5 + [ANY_SPEC] * 3,
+        out_specs=[VMEM_SPEC] * 9,
+        scratch_shapes=[
+            pltpu.VMEM((tokens, D), F32),
+            pltpu.VMEM((tokens, D), BF16),
+            pltpu.VMEM((tokens, D), F32),
+            pltpu.VMEM((tokens, D), F32),
+            pltpu.VMEM((2, 3, CHUNK, D), BF16),
+            pltpu.VMEM((D, padded), BF16),
+            pltpu.VMEM((3, D // 2, 2 * padded), BF16),
+            pltpu.VMEM((3, D // 2, padded), BF16),
+            pltpu.VMEM((4, 2 * padded, cols), BF16),
+            pltpu.VMEM((2 * padded, D), BF16),
+        ]
+        + reduction_scratch(groups, EARLY, cols)
+        + [dma((2, 3)), dma((2, 3)), dma((2, full + 2))],
+        compiler_params=pltpu.CompilerParams(collective_id=2, has_side_effects=True, vmem_limit_bytes=60 << 20),
+    )(branch, x, cotangent, gain.reshape(1, D), w_out, w_gate_t, w_up_t, w_down)
+
+
+def last_kernel(
+    groups, seq_devices, rows, length, width,
+    grad_ref, doc_ref, got, heads, inverse_ref, x_ref, gres_ref, gain_ref, wq_ref, wk_ref, wv_ref,
+    rest, parts_o, gate_early, up_early, down_early, gain_rows,
+    input_out, gate_out, up_out, down_out, wout_out, query_out, key_out, value_out, gains_out,
+    arrived, out_buf, back, gather, qa, ka, ve, dn, qs, kt, dqt, gqk, gv, turned, lhs, lhs_send, right, gnorm,
+    gains, gains_got,
+    send_a, recv_a, send_b, recv_b, lhs_sems, pair_sems, gain_send, gain_recv,
+    f_a, f_b, f_z, fa_sems, fb_sems, fz_send, fz_recv,
+    o_a, o_b, o_z, oa_sems, ob_sems, oz_send, oz_recv,
+    q_source, q_a, q_b, q_z, qa_sems, qb_sems, qz_send, qz_recv,
+):
+    row_group, me = lax.axis_index("dp"), lax.axis_index("seq")
+    core, _, _ = place(me)
+    partner = me + 1 - 2 * core
+    tokens = rows * length
+    padded = turned.shape[1]
+    low = packed_rows(length)
+    lower = lanes_of((low, 128)) < 64
+    here = pl.ds(pl.multiple_of(me * length, 16), length)
+    f_units = rest.shape[0]
+    feed = Reduction(groups, rest, f_a, f_b, f_z, fa_sems, fb_sems, fz_send, fz_recv)
+    outer = Reduction(groups, parts_o, o_a, o_b, o_z, oa_sems, ob_sems, oz_send, oz_recv)
+    qkv = Reduction(groups, q_source, q_a, q_b, q_z, qa_sems, qb_sems, qz_send, qz_recv)
+
+    barrier = pltpu.get_barrier_semaphore()
+    for step in range(1, seq_devices):
+        peer = lax.rem(me + step, seq_devices)
+        pl.semaphore_signal(barrier, inc=1, device_id=(row_group, peer), device_id_type=MESH)
+    for step in range(1, groups):
+        other = lax.rem(row_group + step, groups)
+        pl.semaphore_signal(barrier, inc=1, device_id=(other, me), device_id_type=MESH)
+    pl.semaphore_wait(barrier, seq_devices + groups - 2)
+
+    def outgoing(row, step):
+        peer = lax.rem(me + step, seq_devices)
+        theirs = pl.ds(pl.multiple_of(peer * PAIR, 128), PAIR)
+        return sending(
+            grad_ref.at[row, :, theirs], arrived.at[row, here, :], send_a.at[row, step], recv_a.at[row, step],
+            row_group, peer,
+        )
+
+    def returning(row, step):
+        peer = lax.rem(me + step, seq_devices)
+        return sending(
+            out_buf.at[row, peer], back.at[row, me], send_b.at[row, step], recv_b.at[row, step], row_group, peer
+        )
+
+    def send_row(row, carry):
+        for step in range(1, seq_devices):
+            outgoing(row, step).start()
+        arrived[row, here, :] = grad_ref[row, :, pl.ds(pl.multiple_of(me * PAIR, 128), PAIR)]
+        return carry
+
+    lax.fori_loop(0, rows, send_row, 0)
+
+    def norm_forward(row, carry):
+        at = pl.ds(pl.multiple_of(row * length, 16), length)
+        right[at, :D] = rms_scale(x_ref[at, :].astype(F32), gain_ref[...]).astype(BF16)
+        return carry
+
+    lax.fori_loop(0, rows, norm_forward, 0)
+    turn(right[:tokens, :D], tokens, padded, turned)
+    split_rows(turned, lhs, lhs_send, core, groups)
+    lhs_copy = sending(
+        lhs_send, lhs.at[:, pl.ds(padded, padded)], lhs_sems.at[0], lhs_sems.at[1], row_group, partner
+    )
+    lhs_copy.start()
+    gap = padded - tokens
+    for base in (tokens, padded + tokens):
+        right[base : base + gap, :] = jnp.zeros((gap, right.shape[1]), BF16)
+    gather[...] = gather_matrix()
+
+    def attend(row, carry):
+        prepare_row(got, row, qa, ka, ve, seq_devices, length)
+        for step in range(1, seq_devices):
+            outgoing(row, step).wait_recv()
+        attend_backward(
+            row_ends(doc_ref, row), arrived.at[row], qa, ka, ve, heads.at[row], inverse_ref.at[row],
+            dn, qs, kt, dqt, gqk, gv,
+        )
+
+        def pack(peer, inner):
+            at = pl.multiple_of(peer * length, 16)
+            out_buf[row, peer, :length, :] = gv[pl.ds(at, length), :]
+            first = gqk[pl.ds(at, low), :]
+            second = pltpu.roll(gqk[pl.ds(at + length - low, low), :], 64, 1)
+            out_buf[row, peer, length:, :] = jnp.where(lower, first, second).astype(BF16)
+            return inner
+
+        lax.fori_loop(0, seq_devices, pack, 0)
+        for step in range(1, seq_devices):
+            returning(row, step).start()
+        back[row, me] = out_buf[row, me]
+        feed.a_copy(row).start()
+        return carry
+
+    lax.fori_loop(0, rows, attend, 0)
+    for unit in range(rows, f_units):
+        feed.a_copy(unit).start()
+    outer.a_copy(0).start()
+    feed.a_step(0)
+    feed.a_step(1)
+    feed.a_step(2)
+
+    def unpack(row, carry):
+        for step in range(1, seq_devices):
+            outgoing(row, step).wait_send()
+            returning(row, step).wait()
+        tiles = []
+        for pair in range(0, seq_devices, 2):
+            halves = []
+            for one in (pair, pair + 1):
+                packed = back[row, one, length:, :].astype(F32)
+                turned_over = pltpu.roll(packed, 64, 1)
+                straight, other = (packed, turned_over) if one == pair else (turned_over, packed)
+                halves.append(jnp.concatenate([straight, other[2 * low - length :]], axis=0))
+            tiles.append(jnp.where(lanes_of((length, 128)) < 64, halves[0], halves[1]).astype(BF16))
+        at = pl.ds(pl.multiple_of(row * length, 16), length)
+        right[at, : 2 * H * F] = nn(jnp.concatenate(tiles, axis=1), gather[...]).astype(BF16)
+        for pair in range(seq_devices):
+            col = 2 * H * F + pair * PAIR
+            right[at, col : col + PAIR] = back[row, pair, :length, :]
+        return carry
+
+    lax.fori_loop(0, rows, unpack, 0)
+    pair = sending(
+        right.at[pl.ds(0, tokens), :], right.at[pl.ds(padded, tokens), :], pair_sems.at[0], pair_sems.at[1],
+        row_group, partner,
+    )
+    pair.start()
+    half = H * F
+    gnorm[...] = (
+        nt(right[:tokens, :half], wq_ref[...])
+        + nt(right[:tokens, half : 2 * half], wk_ref[...])
+        + nt(right[:tokens, 2 * half :], wv_ref[...])
+    )
+    lhs_copy.wait()
+    pair.wait()
+    for col in range(0, right.shape[1], CHUNK):
+        store_blocks(q_source, 0, col, nn(lhs[...], right[:, col : col + CHUNK]), groups)
+    qkv.a_copy(0).start()
+
+    gains[...] = gain_rows[...]
+
+    def norm_backward(step, carry):
+        at = pl.ds(pl.multiple_of(step * STEP_ROWS, 16), STEP_ROWS)
+        value, grad = x_ref[at, :].astype(F32), gnorm[at, :]
+        scale = lax.rsqrt(jnp.mean(value * value, axis=-1, keepdims=True) + eps_norm)
+        gains[1:2, :] += jnp.sum(grad * value * scale, axis=0, keepdims=True)
+        weighted = grad * gain_ref[...]
+        mean = jnp.mean(weighted * value, axis=-1, keepdims=True)
+        total = gres_ref[at, :] + scale * weighted - value * (scale * scale * scale * mean)
+        input_out[at, :] = total.astype(BF16)
+        return carry
+
+    lax.fori_loop(0, tokens // STEP_ROWS, norm_backward, 0)
+
+    def gain_copy(step, target_group, target):
+        return sending(
+            gains, gains_got.at[step], gain_send.at[step], gain_recv.at[step], target_group, target
+        )
+
+    gain_copies = [
+        gain_copy(0, row_group, partner),
+        gain_copy(1, row_group, feed.peer_a),
+        gain_copy(2, row_group, feed.peer_b),
+    ] + [gain_copy(2 + step, lax.rem(row_group + step, groups), me) for step in range(1, groups)]
+    gain_copies[0].start()
+    early = gate_early.shape[1]
+    gate_out[:, :early] = gate_early[...]
+    up_out[:, :early] = up_early[...]
+    down_out[:, :early] = down_early[...]
+    gain_copies[0].wait()
+    gains[...] += gains_got[0]
+    gain_copies[1].start()
+    for unit in range(3, f_units):
+        feed.a_step(unit)
+        feed.b_step(unit - 3)
+    gain_copies[1].wait()
+    gains[...] += gains_got[1]
+    gain_copies[2].start()
+    outer.a_step(0)
+    feed.b_step(f_units - 3)
+    qkv.a_step(0)
+    feed.b_step(f_units - 2)
+    feed.b_step(f_units - 1)
+    gain_copies[2].wait()
+    gains[...] += gains_got[2]
+    for copy in gain_copies[3:]:
+        copy.start()
+
+    def write_feed(unit, w):
+        at = early + unit * CHUNK
+        at = at if isinstance(at, int) else pl.multiple_of(at, CHUNK)
+        write_unit(feed.z_step(unit), at, w, gate_out, up_out, down_out)
+
+    def finish(unit, carry):
+        write_feed(unit, CHUNK)
+        return carry
+
+    lax.fori_loop(0, f_units - 3, finish, 0)
+    outer.b_step(0)
+    lax.fori_loop(f_units - 3, f_units - 1, finish, 0)
+    write_feed(f_units - 1, width - early - (f_units - 1) * CHUNK)
+    for copy in gain_copies[3:]:
+        copy.wait()
+    for step in range(1, groups):
+        gains[...] += gains_got[2 + step]
+    picked = lax.broadcasted_iota(jnp.int32, (D, 128), 0) == 32 * (seq_devices * row_group + me) + lanes_of((D, 128))
+    gains_out[...] = jnp.dot(
+        gains[...], jnp.where(picked, 1.0, 0.0), precision=lax.Precision.HIGHEST, preferred_element_type=F32
+    )
+    qkv.b_step(0)
+    wout_out[...] = outer.z_step(0)
+    total = qkv.z_step(0)
+    query_out[...] = total[:, :half]
+    key_out[...] = total[:, half : 2 * half]
+    value_out[...] = total[:, 2 * half :]
+
+    def sent(unit, carry):
+        feed.wait_sent(unit)
+        return carry
+
+    lax.fori_loop(0, f_units, sent, 0)
+    outer.wait_sent(0)
+    qkv.wait_sent(0)
+
+
+def last_part(
+    groups, seq_devices, grad, doc_lengths, got, heads, inverse, x, gres, gain, w_query, w_key, w_value,
+    rest, parts_o, gate_early, up_early, down_early, gain_rows, width,
+):
     rows, length, _ = grad.shape
+    tokens = rows * length
     total = seq_devices * length
+    padded = (tokens + 127) // 128 * 128
     message = (rows, seq_devices, length + packed_rows(length), 128)
-    sems = pltpu.SemaphoreType.DMA((rows, seq_devices))
+    dma = pltpu.SemaphoreType.DMA
+    sems = dma((rows, seq_devices))
+    cols = 2 * H * F + D
     return pl.pallas_call(
-        functools.partial(backward_kernel, seq_devices, rows, length),
+        functools.partial(last_kernel, groups, seq_devices, rows, length, width),
         name="attention_backward",
         out_shape=[
-            jax.ShapeDtypeStruct((rows, length, 2 * H * F), BF16),
-            jax.ShapeDtypeStruct((rows, length, D), BF16),
+            jax.ShapeDtypeStruct((tokens, D), BF16),
+            jax.ShapeDtypeStruct((32, width), F32),
+            jax.ShapeDtypeStruct((32, width), F32),
+            jax.ShapeDtypeStruct((32, width), F32),
+            jax.ShapeDtypeStruct((32, D), F32),
+            jax.ShapeDtypeStruct((32, H * F), F32),
+            jax.ShapeDtypeStruct((32, H * F), F32),
+            jax.ShapeDtypeStruct((32, D), F32),
+            jax.ShapeDtypeStruct((8, 128), F32),
         ],
-        in_specs=[VMEM_SPEC, SMEM_SPEC, VMEM_SPEC, VMEM_SPEC, VMEM_SPEC],
-        out_specs=[VMEM_SPEC] * 2,
+        in_specs=[VMEM_SPEC, SMEM_SPEC] + [VMEM_SPEC] * 15,
+        out_specs=[VMEM_SPEC] * 9,
         scratch_shapes=[
             pltpu.VMEM((rows, total, 128), BF16),
             pltpu.VMEM(message, BF16),
@@ -643,106 +1147,57 @@
             pltpu.VMEM((32, total), F32),
             pltpu.VMEM((total, 128), F32),
             pltpu.VMEM((total, 128), BF16),
+            pltpu.VMEM((D, padded), BF16),
+            pltpu.VMEM((D // 2, 2 * padded), BF16),
+            pltpu.VMEM((D // 2, padded), BF16),
+            pltpu.VMEM((2 * padded, cols), BF16),
+            pltpu.VMEM((tokens, D), F32),
+            pltpu.VMEM((8, D), F32),
+            pltpu.VMEM((2 + groups, 8, D), F32),
             sems, sems, sems, sems,
-        ],
-        compiler_params=pltpu.CompilerParams(collective_id=1, has_side_effects=True, vmem_limit_bytes=56 << 20),
-    )(grad, doc_lengths, got, heads, inverse)
-
-
-def body(
-    seq_devices,
-    inputs,
-    doc_lengths,
-    gain_attn,
-    w_query,
-    w_key,
-    w_value,
-    w_out,
-    gain_ffn,
-    w_gate,
-    w_up,
-    w_down,
-    cotangent,
+            dma((2,)), dma((2,)), dma((2 + groups,)), dma((2 + groups,)),
+        ]
+        + reduction_scratch(groups, rest.shape[0], 3 * CHUNK, source=False)
+        + reduction_scratch(groups, 1, D, source=False)
+        + reduction_scratch(groups, 1, cols),
+        compiler_params=pltpu.CompilerParams(collective_id=1, has_side_effects=True, vmem_limit_bytes=60 << 20),
+    )(
+        grad, doc_lengths, got, heads, inverse, x, gres, gain.reshape(1, D), w_query, w_key, w_value,
+        rest, parts_o, gate_early, up_early, down_early, gain_rows,
+    )
+
+
+def tuned_body(
+    seq_devices, groups, inputs, doc_lengths, gain_attn, w_query, w_key, w_value, w_out, gain_ffn, w_gate, w_up,
+    w_down, cotangent,
 ):
     row_count, shard_len, _ = inputs.shape
     token_count = row_count * shard_len
-    stream = inputs.reshape(token_count, D).astype(jnp.float32)
-    normed, attn_norm_back = jax.vjp(rms_scale, stream, gain_attn)
-    normed_low = normed.astype(jnp.bfloat16)
+    stream = inputs.reshape(token_count, D)
     branch, got, heads, inverse = attention_forward(
         seq_devices, inputs, doc_lengths, gain_attn, w_query, w_key, w_value
     )
-    mixed_flat = branch.reshape(token_count, D)
-    residual = stream + project(mixed_flat, w_out)
-    normed_ffn, ffn_norm_back = jax.vjp(rms_scale, residual, gain_ffn)
-    ffn_low = normed_ffn.astype(jnp.bfloat16)
-    gate_proj = project(ffn_low, w_gate)
-    up_proj = project(ffn_low, w_up)
-    hidden, act_back = jax.vjp(swiglu, gate_proj, up_proj)
-    hidden_low = hidden.astype(jnp.bfloat16)
-    output = residual + project(hidden_low, w_down)
-    grad_out = cotangent.reshape(token_count, D)
-    grad_gate, grad_up = act_back(back_project(grad_out, w_down))
-    grad_gate_low = grad_gate.astype(jnp.bfloat16)
-    grad_up_low = grad_up.astype(jnp.bfloat16)
-    down_grad_t = weight_grad(grad_out, hidden_low)
-    gate_grad = weight_grad(ffn_low, grad_gate_low)
-    up_grad = weight_grad(ffn_low, grad_up_low)
-    grad_normed_ffn = back_project(grad_gate_low, w_gate) + back_project(grad_up_low, w_up)
-    grad_residual, gain_ffn_grad = ffn_norm_back(grad_normed_ffn)
-    grad_residual = grad_residual + grad_out.astype(jnp.float32)
-    grad_branch = grad_residual.astype(jnp.bfloat16)
-    out_grad = weight_grad(mixed_flat, grad_branch)
-    grad_mixed = back_project(grad_branch, w_out).astype(jnp.bfloat16)
-    back_both, back_value = attention_backward(
-        seq_devices, grad_mixed.reshape(row_count, shard_len, D), doc_lengths, got, heads, inverse
-    )
-    back_query = back_both.reshape(token_count, 2 * H * F)[:, : H * F]
-    back_key = back_both.reshape(token_count, 2 * H * F)[:, H * F :]
-    back_value = back_value.reshape(token_count, D)
-    query_grad = weight_grad(normed_low, back_query)
-    key_grad = weight_grad(normed_low, back_key)
-    value_grad = weight_grad(normed_low, back_value)
-    grad_normed = (
-        back_project(back_query, w_query)
-        + back_project(back_key, w_key)
-        + back_project(back_value, w_value)
-    )
-    grad_stream, gain_attn_grad = attn_norm_back(grad_normed)
-    input_grad = grad_residual + grad_stream
-    (
-        gain_attn_part,
-        query_part,
-        key_part,
-        value_part,
-        out_part,
-        gain_ffn_part,
-        gate_part,
-        up_part,
-        down_part,
-    ) = (
-        lax.psum_scatter(gain_attn_grad, ("dp", "seq"), scatter_dimension=0, tiled=True),
-        lax.psum_scatter(query_grad, ("dp", "seq"), scatter_dimension=0, tiled=True),
-        lax.psum_scatter(key_grad, ("dp", "seq"), scatter_dimension=0, tiled=True),
-        lax.psum_scatter(value_grad, ("dp", "seq"), scatter_dimension=0, tiled=True),
-        lax.psum_scatter(out_grad, ("dp", "seq"), scatter_dimension=0, tiled=True),
-        lax.psum_scatter(gain_ffn_grad, ("dp", "seq"), scatter_dimension=0, tiled=True),
-        lax.psum_scatter(gate_grad, ("dp", "seq"), scatter_dimension=0, tiled=True),
-        lax.psum_scatter(up_grad, ("dp", "seq"), scatter_dimension=0, tiled=True),
-        lax.psum_scatter(down_grad_t, ("dp", "seq"), scatter_dimension=0, tiled=True),
+    output, gres, gmixed, gate_early, up_early, down_early, rest, parts_o, gain_rows = feed_forward(
+        groups, branch.reshape(token_count, D), stream, cotangent.reshape(token_count, D), gain_ffn, w_out,
+        w_gate.T, w_up.T, w_down,
+    )
+    input_grad, gate, up, down, out, query, key, value, gains = last_part(
+        groups, seq_devices, gmixed.reshape(row_count, shard_len, D), doc_lengths, got, heads, inverse, stream, gres,
+        gain_attn, w_query, w_key, w_value, rest, parts_o, gate_early, up_early, down_early, gain_rows,
+        w_down.shape[0],
     )
     return (
-        output.reshape(row_count, shard_len, D).astype(jnp.bfloat16),
-        input_grad.reshape(row_count, shard_len, D).astype(jnp.bfloat16),
-        gain_attn_part,
-        query_part,
-        key_part,
-        value_part,
-        out_part,
-        gain_ffn_part,
-        gate_part,
-        up_part,
-        jnp.transpose(down_part),
+        output.reshape(row_count, shard_len, D),
+        input_grad.reshape(row_count, shard_len, D),
+        gains[1, :32],
+        query,
+        key,
+        value,
+        out,
+        gains[0, :32],
+        gate,
+        up,
+        down.T,
     )
 
 
@@ -774,6 +1229,7 @@
         P(("dp", "seq"), None),
         P(None, ("dp", "seq")),
     )
-    seq_devices = mesh.shape["seq"]
-    step = functools.partial(body, seq_devices) if seq_devices * 2 == H else general_body
+    seq_devices, groups = mesh.shape["seq"], mesh.shape["dp"]
+    tuned = seq_devices == 8 and seq_devices * groups * 32 == D
+    step = functools.partial(tuned_body, seq_devices, groups) if tuned else general_body
     return jax.shard_map(step, mesh=mesh, in_specs=in_specs, out_specs=out_specs, check_vma=False)

time: 1150 us -> 232 us (0.20)
  waiting for transfers between devices: 906 us -> 0 us
  Pallas kernels: 72.7 us -> 224 us
  matrix products: 89.3 us -> 0 us
  blocking collectives: 39.9 us -> 0 us
  between operations: 14.9 us -> 0.73 us
    reduce_scatter x6 -> x0, waiting for transfers between devices: 753 us -> none  [the longest x1 154 us: body(): lax.psum_scatter(gate_grad, ('dp', 'seq'), scatter_dimension=0, tiled=True)]
    unnamed x8 -> x0, waiting for transfers between devices: 154 us -> none
    pallas_call x1 -> x2, Pallas kernels: 36.9 us -> 188 us  [the longest x1 128 us: last_part(): pl.pallas_call(functools.partial(last_kernel, groups, seq_devices, rows,...]
    dot_general x18 -> x0, matrix products: 89.3 us -> none  [the longest x7 41.3 us: weight_grad(): lax.dot_general(left, right, (((0,), (0,)), ((), ())), preferred_element_...]
    unnamed x1 -> x0, blocking collectives: 39.9 us -> none
  transfers between devices with their start and end apart: 7 -> 0, of which waited for: 7 -> 0; matrix products, arithmetic and copies ran while one was open for 5% -> 0% of each run, Pallas kernels for 0% -> 0%
where the time goes in v2:
time: 232 us
  Pallas kernels  224 us (97%)
  local copies, waits for them, and re-layouts  7.89 us (3%)
    pallas_call x1, Pallas kernels, last_part(): pl.pallas_call(functools.partial(last_kernel, groups, seq_devices, rows,...  128 us
    pallas_call x1, Pallas kernels, feed_forward(): pl.pallas_call(functools.partial(ffn_kernel, groups, tokens, width), name...  59.5 us
    pallas_call x1, Pallas kernels, attention_forward(): pl.pallas_call(functools.partial(forward_kernel, seq_devices, rows, lengt...  35.9 us
    unnamed x27, local copies, waits for them, and re-layouts  6.61 us

profile of v2, /device:TPU:0, one launch (start us, length us, event | category | flops | bytes accessed | tf_op | source)
XLA Modules:
  0.0 232.3 jit_solution(11695559712220094791)
XLA Ops:
  0.6 35.9 %attention_forward.1 = (bf16[3,144,1024]{2,1,0:T(8,128)(2,1)}, bf16[3,8,224,128]{3,2,1,0:T(8,128)(2,1)}, bf16[3,1152,128]{2,1,0:T(8,128)(2,1)}, f32[3,1152,128]{2,1,0:T(8,128)}) custom-call(bf16[3,144,1024]{2,1,0:T(8,128)(2,1)} %x_ref.1, s32[3,4]{1,0:T(4,128)} %doc_ref.3, f32[1,1024]{1,0:T(1,128)} %bitcast.25, bf16[1024,256]{1,0:T(8,128)(2,1)} %wq_ref.3, ...), custom_call_target="tpu_custom_call" | custom-call | tf_op jit(solution)/shard_map/attention_forward/pallas_call | solution.py:510
  36.6 59.5 %feed_forward.1 = (bf16[432,1024]{1,0:T(8,128)(2,1)}, f32[432,1024]{1,0:T(8,128)}, bf16[432,1024]{1,0:T(8,128)(2,1)}, f32[32,1024]{1,0:T(8,128)}, f32[32,1024]{1...) custom-call(bf16[432,1024]{1,0:T(8,128)(2,1)} %bitcast.23, ...), custom_call_target="tpu_custom_call" | custom-call | tf_op jit(solution)/shard_map/feed_forward/pallas_call | solution.py:845
  96.0 0.0 copy-start
  96.1 128.3 %attention_backward.1 = (bf16[432,1024]{1,0:T(8,128)(2,1)}, f32[32,2752]{1,0:T(8,128)}, f32[32,2752]{1,0:T(8,128)}, f32[32,2752]{1,0:T(8,128)}, f32[32,1024]{1,0...) custom-call(bf16[3,144,1024]{2,1,0:T(8,128)(2,1)} %bitcast.22, ...), custom_call_target="tpu_custom_call" | custom-call | tf_op jit(solution)/shard_map/attention_backward/pallas_call | solution.py:1120
  224.3 0.0 copy-start.1
  224.4 0.0 copy-start.8
  224.4 0.0 copy-start.7
  224.4 0.0 copy-start.6
  224.4 0.0 copy-start.5
  224.4 1.3 slice_bitcast_fusion
  225.7 0.0 copy-done
  225.7 0.0 copy-start.4
  225.7 0.0 copy-start.3
  225.7 0.9 copy.32
  226.6 0.0 copy-done.1
  226.6 0.0 copy-start.2
  226.6 0.9 copy.33
  227.5 0.0 copy-done.8
  227.5 0.6 copy.34
  228.1 0.0 copy-done.7
  228.1 0.6 copy.35
  228.8 0.0 copy-done.6
  228.8 0.7 copy.36
  229.4 0.0 copy-done.5
  229.4 0.7 copy.37
  230.1 0.0 copy-done.4
  230.1 0.7 copy.38
  230.8 0.0 copy-done.3
  230.8 0.7 copy.39
  231.5 0.0 copy-done.2
  231.5 0.7 copy.40
Async XLA Ops:
  96.0 129.6 %copy-start = (bf16[432,1024]{1,0:T(8,128)(2,1)S(1)}, bf16[432,1024]{1,0:T(8,128)(2,1)}, u32[]{:S(2)}) copy-start(bf16[432,1024]{1,0:T(8,128)(2,1)} %get-tuple-element.34) | copy-start | bytes 2654212
  224.3 2.3 copy-start.1
  224.4 3.2 %copy-start.8 = (f32[32,256]{1,0:T(8,128)S(1)}, f32[32,256]{1,0:T(8,128)}, u32[]{:S(2)}) copy-start(f32[32,256]{1,0:T(8,128)} %get-tuple-element.71) | copy-start | bytes 98308
  224.4 3.8 %copy-start.7 = (f32[32,256]{1,0:T(8,128)S(1)}, f32[32,256]{1,0:T(8,128)}, u32[]{:S(2)}) copy-start(f32[32,256]{1,0:T(8,128)} %get-tuple-element.72) | copy-start | bytes 98308
  224.4 4.4 %copy-start.6 = (f32[32,1024]{1,0:T(8,128)S(1)}, f32[32,1024]{1,0:T(8,128)}, u32[]{:S(2)}) copy-start(f32[32,1024]{1,0:T(8,128)} %get-tuple-element.73) | copy-start | bytes 393220
  224.4 5.0 %copy-start.5 = (f32[32,1024]{1,0:T(8,128)S(1)}, f32[32,1024]{1,0:T(8,128)}, u32[]{:S(2)}) copy-start(f32[32,1024]{1,0:T(8,128)} %get-tuple-element.74) | copy-start | bytes 393220
  225.7 4.4 %copy-start.4 = (f32[32,2752]{1,0:T(8,128)S(1)}, f32[32,2752]{1,0:T(8,128)}, u32[]{:S(2)}) copy-start(f32[32,2752]{1,0:T(8,128)} %get-tuple-element.76) | copy-start | bytes 1056772
  225.7 5.1 %copy-start.3 = (f32[32,2752]{1,0:T(8,128)S(1)}, f32[32,2752]{1,0:T(8,128)}, u32[]{:S(2)}) copy-start(f32[32,2752]{1,0:T(8,128)} %get-tuple-element.77) | copy-start | bytes 1056772
  226.6 4.9 %copy-start.2 = (f32[32,2752]{1,0:T(8,128)S(1)}, f32[32,2752]{1,0:T(8,128)}, u32[]{:S(2)}) copy-start(f32[32,2752]{1,0:T(8,128)} %get-tuple-element.54) | copy-start | bytes 1056772

commit v3 on v2

--- a/solution.py
+++ b/solution.py
@@ -535,7 +535,9 @@
 
 CHUNK = 256
 STEP_ROWS = 48
-EARLY = 4
+XY_EARLY = 6
+SLOTS = 7
+VMEM_BYTES = 63 << 20
 
 
 def place(me):
@@ -554,53 +556,110 @@
 
 
 class Reduction:
-    def __init__(self, groups, source, got_a, got_b, got_z, a_sems, b_sems, z_send, z_recv):
+    def __init__(self, groups, source, buffers, slot_of=None, place_of=None):
         self.groups, self.source = groups, source
-        self.got_a, self.got_b, self.got_z = got_a, got_b, got_z
-        self.a_sems, self.b_sems, self.z_send, self.z_recv = a_sems, b_sems, z_send, z_recv
+        self.got_a, self.got_b, self.got_z, self.a_sems, self.b_sems, self.z_send, self.z_recv = buffers
+        self.slot_of = slot_of or (lambda unit: unit)
+        self.place_of = place_of or (lambda unit: unit)
         self.group, self.me = lax.axis_index("dp"), lax.axis_index("seq")
         core, first, second = place(self.me)
         self.bit_a, self.bit_b = lax.rem(self.me // first, 2), lax.rem(self.me // second, 2)
         self.peer_a = self.me + first * (1 - 2 * self.bit_a)
         self.peer_b = self.me + second * (1 - 2 * self.bit_b)
 
+    def block(self, group):
+        return pl.ds(pl.multiple_of(group * 32, 32), 32)
+
+    def other(self, step):
+        return lax.rem(self.group + step, self.groups)
+
     def a_copy(self, unit):
+        at = self.place_of(unit)
         return sending(
-            self.source.at[unit, 1 - self.bit_a], self.got_a.at[unit], self.a_sems.at[0, unit],
-            self.a_sems.at[1, unit], self.group, self.peer_a,
+            self.source.at[self.slot_of(unit), 1 - self.bit_a], self.got_a.at[at], self.a_sems.at[0, at],
+            self.a_sems.at[1, at], self.group, self.peer_a,
         )
 
     def b_copy(self, unit):
+        at = self.place_of(unit)
         return sending(
-            self.got_a.at[unit, 1 - self.bit_b], self.got_b.at[unit], self.b_sems.at[0, unit],
-            self.b_sems.at[1, unit], self.group, self.peer_b,
+            self.got_a.at[at, 1 - self.bit_b], self.got_b.at[at], self.b_sems.at[0, at], self.b_sems.at[1, at],
+            self.group, self.peer_b,
         )
 
     def z_copy(self, unit, step):
-        other = lax.rem(self.group + step, self.groups)
-        block = pl.ds(pl.multiple_of(other * 32, 32), 32)
+        at = self.place_of(unit)
         return sending(
-            self.got_b.at[unit, block, :], self.got_z.at[unit, step - 1], self.z_send.at[unit, step - 1],
-            self.z_recv.at[unit, step - 1], other, self.me,
+            self.got_b.at[at, self.block(self.other(step)), :], self.got_z.at[at, step - 1],
+            self.z_send.at[at, step - 1], self.z_recv.at[at, step - 1], self.other(step), self.me,
         )
 
     def a_step(self, unit):
+        at = self.place_of(unit)
         self.a_copy(unit).wait_recv()
-        self.got_a[unit] = (self.source[unit, self.bit_a].astype(F32) + self.got_a[unit].astype(F32)).astype(BF16)
+        mine = self.source[self.slot_of(unit), self.bit_a].astype(F32)
+        self.got_a[at] = (mine + self.got_a[at].astype(F32)).astype(BF16)
         self.b_copy(unit).start()
 
     def b_step(self, unit):
+        at = self.place_of(unit)
         self.b_copy(unit).wait_recv()
-        self.got_b[unit] = (self.got_a[unit, self.bit_b].astype(F32) + self.got_b[unit].astype(F32)).astype(BF16)
+        self.got_b[at] = (self.got_a[at, self.bit_b].astype(F32) + self.got_b[at].astype(F32)).astype(BF16)
         for step in range(1, self.groups):
             self.z_copy(unit, step).start()
 
     def z_step(self, unit):
-        total = self.got_b[unit, pl.ds(pl.multiple_of(self.group * 32, 32), 32), :].astype(F32)
+        at = self.place_of(unit)
+        total = self.got_b[at, self.block(self.group), :].astype(F32)
         for step in range(1, self.groups):
             self.z_copy(unit, step).wait_recv()
-            total += self.got_z[unit, step - 1].astype(F32)
+            total += self.got_z[at, step - 1].astype(F32)
         return total
+
+    def wait_sent(self, unit):
+        self.b_copy(unit).wait_send()
+        for step in range(1, self.groups):
+            self.z_copy(unit, step).wait_send()
+
+
+class GroupsFirst(Reduction):
+    def z_copy(self, unit, step):
+        at = self.place_of(unit)
+        return sending(
+            self.source.at[self.slot_of(unit), :, :, self.block(self.other(step)), :], self.got_z.at[at, step - 1],
+            self.z_send.at[at, step - 1], self.z_recv.at[at, step - 1], self.other(step), self.me,
+        )
+
+    def a_copy(self, unit):
+        at = self.place_of(unit)
+        return sending(
+            self.got_z.at[at, 0, 1 - self.bit_a], self.got_a.at[at], self.a_sems.at[0, at], self.a_sems.at[1, at],
+            self.group, self.peer_a,
+        )
+
+    def start(self, unit):
+        for step in range(1, self.groups):
+            self.z_copy(unit, step).start()
+
+    def z_step(self, unit):
+        at = self.place_of(unit)
+        total = self.source[self.slot_of(unit), :, :, self.block(self.group), :].astype(F32)
+        for step in range(1, self.groups):
+            self.z_copy(unit, step).wait_recv()
+            total += self.got_z[at, step - 1].astype(F32)
+        self.got_z[at, 0] = total.astype(BF16)
+        self.a_copy(unit).start()
+
+    def a_step(self, unit):
+        at = self.place_of(unit)
+        self.a_copy(unit).wait_recv()
+        self.got_a[at] = (self.got_z[at, 0, self.bit_a].astype(F32) + self.got_a[at].astype(F32)).astype(BF16)
+        self.b_copy(unit).start()
+
+    def b_step(self, unit):
+        at = self.place_of(unit)
+        self.b_copy(unit).wait_recv()
+        return self.got_a[at, self.bit_b].astype(F32) + self.got_b[at].astype(F32)
 
     def wait_sent(self, unit):
         self.a_copy(unit).wait_send()
@@ -609,11 +668,10 @@
             self.z_copy(unit, step).wait_send()
 
 
-def reduction_scratch(groups, units, cols, source=True):
+def reduction_buffers(groups, units, cols):
     rows = 32 * groups
     dma = pltpu.SemaphoreType.DMA
-    buffers = [pltpu.VMEM((units, 2, 2, rows, cols), BF16)] if source else []
-    return buffers + [
+    return [
         pltpu.VMEM((units, 2, rows, cols), BF16),
         pltpu.VMEM((units, rows, cols), BF16),
         pltpu.VMEM((units, groups - 1, 32, cols), BF16),
@@ -624,6 +682,19 @@
     ]
 
 
+def groups_first_buffers(groups, units, cols):
+    dma = pltpu.SemaphoreType.DMA
+    return [
+        pltpu.VMEM((units, 2, 32, cols), BF16),
+        pltpu.VMEM((units, 32, cols), BF16),
+        pltpu.VMEM((units, groups - 1, 2, 2, 32, cols), BF16),
+        dma((2, units)),
+        dma((2, units)),
+        dma((units, groups - 1)),
+        dma((units, groups - 1)),
+    ]
+
+
 def store_blocks(target, unit, col, values, groups):
     rows = 32 * groups
     for i in range(2):
@@ -637,10 +708,10 @@
 
 
 def split_rows(turned, mine_ref, theirs_ref, core, groups):
-    padded = turned.shape[1]
     for i, (mine, theirs) in enumerate(zip(blocks_of(core, groups), blocks_of(1 - core, groups))):
-        mine_ref[i * 32 : (i + 1) * 32, :padded] = turned[pl.ds(mine, 32), :]
-        theirs_ref[i * 32 : (i + 1) * 32, :] = turned[pl.ds(theirs, 32), :]
+        a, b, group = i // (2 * groups), i // groups % 2, i % groups
+        mine_ref[a, b, group * 32 : (group + 1) * 32, :] = turned[pl.ds(mine, 32), :]
+        theirs_ref[a, b, group * 32 : (group + 1) * 32, :] = turned[pl.ds(theirs, 32), :]
 
 
 def write_unit(total, at, w, gate_out, up_out, down_out):
@@ -649,23 +720,44 @@
     up_out[:, pl.ds(at, w)] = total[:, 2 * CHUNK : 2 * CHUNK + w]
 
 
-def ffn_kernel(
-    groups, tokens, width,
+def backward_kernel(
+    groups, seq_devices, rows, length, width,
     branch_ref, x_ref, cot_ref, gain_ref, wo_ref, wg_hbm, wu_hbm, wd_hbm,
-    output_ref, gres_ref, gmixed_ref, gate_out, up_out, down_out, rest, parts_o, gain_out,
-    residual, normed, out_acc, gnf, w_buf, turned, lhs, lhs_send, right, right_out, parts,
-    got_a, got_b, got_z, a_sems, b_sems, z_send, z_recv, w_sem, lhs_sems, pair_sems,
+    doc_ref, got_hbm, heads_hbm, inverse_hbm, gain_attn_ref, wq_ref, wk_ref, wv_hbm,
+    output_ref, input_out, gate_out, up_out, down_out, wout_out, query_out, key_out, value_out, gains_out,
+    residual, normed, out_acc, gnf, w_buf, lhs, right, parts, parts_o, q_source,
+    got, heads, inverse, arrived, back, qa, ka, ve, dn, qs, kt, dqt, gqk, gv, gains, gains_got,
+    w_sem, wv_sems, in_sems, lhs_sems, pair_sems, send_a, recv_a, send_b, recv_b, gain_send, gain_recv,
+    *buffers,
 ):
     row_group, me = lax.axis_index("dp"), lax.axis_index("seq")
     core, _, _ = place(me)
     partner = me + 1 - 2 * core
-    reduction = Reduction(groups, parts, got_a, got_b, got_z, a_sems, b_sems, z_send, z_recv)
+    tokens = rows * length
+    padded = right.shape[1] // 2
     full = width // CHUNK
     tail = width - full * CHUNK
-    padded = turned.shape[1]
+    low = packed_rows(length)
+    lower = lanes_of((low, 128)) < 64
+    here = pl.ds(pl.multiple_of(me * length, 16), length)
+    half = H * F
+
+    def slot_of(unit):
+        return lax.rem(unit, SLOTS)
+
+    z_units = full - 1 - XY_EARLY
+
+    def place_of(unit):
+        return unit if isinstance(unit, int) and unit < XY_EARLY else jnp.where(unit < XY_EARLY, unit, unit - z_units)
+
+    feed = Reduction(groups, parts, buffers[:7], slot_of, place_of)
+    outer = Reduction(groups, parts_o, buffers[7:14])
+    qkv = Reduction(groups, q_source, buffers[14:21])
+    first = GroupsFirst(groups, parts, buffers[21:28], slot_of, lambda unit: unit - XY_EARLY)
 
     barrier = pltpu.get_barrier_semaphore()
-    for peer in (partner, reduction.peer_a, reduction.peer_b):
+    for step in range(1, seq_devices):
+        peer = lax.rem(me + step, seq_devices)
         pl.semaphore_signal(barrier, inc=1, device_id=(row_group, peer), device_id_type=MESH)
     for step in range(1, groups):
         other = lax.rem(row_group + step, groups)
@@ -678,7 +770,19 @@
             for which, hbm in enumerate((wg_hbm, wu_hbm, wd_hbm))
         ]
 
-    for copy in loads(0, 0, CHUNK):
+    def value_load(part):
+        return pltpu.make_async_copy(
+            wv_hbm.at[pl.ds(part * CHUNK, CHUNK), :], w_buf.at[part // 3, part % 3], wv_sems.at[part]
+        )
+
+    for chunk in range(2):
+        for copy in loads(chunk, chunk, CHUNK):
+            copy.start()
+    saved = [
+        pltpu.make_async_copy(source, target, in_sems.at[i])
+        for i, (source, target) in enumerate(((got_hbm, got), (heads_hbm, heads), (inverse_hbm, inverse)))
+    ]
+    for copy in saved:
         copy.start()
 
     def norm_forward(step, carry):
@@ -693,33 +797,48 @@
     lax.fori_loop(0, tokens // STEP_ROWS, norm_forward, 0)
     gnf[...] = jnp.zeros_like(gnf)
 
-    pl.semaphore_wait(barrier, 2 + groups)
+    pl.semaphore_wait(barrier, seq_devices + groups - 2)
 
     def lhs_copy(which):
         return sending(
-            lhs_send.at[which], lhs.at[which, :, pl.ds(padded, padded)],
+            q_source.at[0, :, :, :, pl.ds(which % 3 * padded, padded)],
+            lhs.at[which % 3, :, :, :, pl.ds(padded, padded)],
             lhs_sems.at[0, which], lhs_sems.at[1, which], row_group, partner,
         )
 
+    def prepare_lhs(which, source):
+        turned = right.at[3 if which < 3 else 1, :, pl.ds(0, padded)]
+        turn(source, tokens, padded, turned)
+        at = which % 3 * padded
+        split_rows(
+            turned, lhs.at[which % 3, :, :, :, pl.ds(0, padded)], q_source.at[0, :, :, :, pl.ds(at, padded)], core, groups
+        )
+
+    def left(which):
+        return lhs[which].reshape(D // 2, 2 * padded)
+
     for which, source in enumerate((cot_ref, normed, branch_ref)):
-        turn(source[...], tokens, padded, turned)
-        split_rows(turned, lhs.at[which], lhs_send.at[which], core, groups)
+        prepare_lhs(which, source[...])
         lhs_copy(which).start()
-    slots = right.shape[0]
     gap = padded - tokens
-    for base in (tokens, padded + tokens):
-        right[:, base : base + gap, :] = jnp.zeros((slots, gap, 3 * CHUNK), BF16)
-        right_out[base : base + gap, :] = jnp.zeros((gap, D), BF16)
+
+    def clear(slot, count):
+        for base in (tokens, padded + tokens):
+            right[slot : slot + count, base : base + gap, :] = jnp.zeros((count, gap, 3 * CHUNK), BF16)
+
+    clear(0, 4)
+
+    def right_copy(slot, cols, sem):
+        return sending(
+            right.at[slot, pl.ds(0, tokens), pl.ds(0, cols)], right.at[slot, pl.ds(padded, tokens), pl.ds(0, cols)],
+            pair_sems.at[0, sem], pair_sems.at[1, sem], row_group, partner,
+        )
 
     def pair_copy(chunk):
-        slot = lax.rem(chunk, slots)
-        return sending(
-            right.at[slot, pl.ds(0, tokens), :], right.at[slot, pl.ds(padded, tokens), :],
-            pair_sems.at[0, chunk], pair_sems.at[1, chunk], row_group, partner,
-        )
+        return right_copy(lax.rem(chunk, 4), 3 * CHUNK, chunk)
 
     def forward_part(chunk, wg, wu, wd, w):
-        slot = lax.rem(chunk, slots)
+        slot = lax.rem(chunk, 4)
         gate = nt(normed[...], wg)
         up = nt(normed[...], wu)
         sigmoid = 1.0 / (1.0 + jnp.exp(-gate))
@@ -736,19 +855,11 @@
         out_acc[...] += nn(hidden, wd)
         gnf[...] += nn(grad_gate, wg) + nn(grad_up, wu)
 
-    def grad_part(chunk, early):
+    def grad_part(chunk):
         pair_copy(chunk).wait()
-        slot = lax.rem(chunk, slots)
-        down = nn(lhs[0], right[slot, :, 0:CHUNK])
-        both = nn(lhs[1], right[slot, :, CHUNK:])
-        target, unit = (parts, chunk) if early else (rest, chunk - EARLY)
-        store_blocks(target, unit, 0, down, groups)
-        store_blocks(target, unit, CHUNK, both, groups)
-        if early:
-            reduction.a_copy(chunk).start()
-
-    for which in range(3):
-        lhs_copy(which).wait()
+        slot = lax.rem(chunk, 4)
+        store_blocks(parts, slot_of(chunk), 0, nn(left(0), right[slot, :, 0:CHUNK]), groups)
+        store_blocks(parts, slot_of(chunk), CHUNK, nn(left(1), right[slot, :, CHUNK:]), groups)
 
     def forward_step(chunk):
         slot = lax.rem(chunk, 2)
@@ -756,230 +867,160 @@
             copy.wait()
         forward_part(chunk, w_buf[slot, 0], w_buf[slot, 1], w_buf[slot, 2], CHUNK)
 
-    def main(early, chunk, carry):
+    def ticks(chunk):
+        @pl.when((chunk >= 4) & (lax.rem(chunk, 2) == 0))
+        def _():
+            feed.a_step((chunk - 4) // 2)
+
+        @pl.when((chunk >= 7) & (lax.rem(chunk, 2) == 1))
+        def _():
+            feed.b_step((chunk - 7) // 2)
+
+    def xy_main(chunk, carry):
         for copy in loads(chunk + 1, lax.rem(chunk + 1, 2), CHUNK):
             copy.start()
         forward_step(chunk)
-        grad_part(chunk - 1, early)
-
-        @pl.when((chunk >= 4) & (chunk < 4 + EARLY))
+        grad_part(chunk - 1)
+        feed.a_copy(chunk - 1).start()
+        ticks(chunk)
+        return carry
+
+    def z_main(chunk, carry):
+        @pl.when(chunk < full - 1)
         def _():
-            reduction.a_step(chunk - 4)
-
-        @pl.when((chunk >= 6) & (chunk < 6 + EARLY))
+            for copy in loads(chunk + 1, lax.rem(chunk + 1, 2), CHUNK):
+                copy.start()
+
+        @pl.when(chunk == full - 1)
         def _():
-            reduction.b_step(chunk - 6)
-
+            for copy in loads(full, full % 2, tail):
+                copy.start()
+
+        forward_step(chunk)
+
+        @pl.when(chunk - 1 >= SLOTS)
+        def _():
+            feed.a_copy(chunk - 1 - SLOTS).wait_send()
+
+        grad_part(chunk - 1)
+        first.start(chunk - 1)
+        ticks(chunk)
         return carry
 
-    for copy in loads(1, 1, CHUNK):
-        copy.start()
     forward_step(0)
-    lax.fori_loop(1, EARLY + 1, functools.partial(main, True), 0)
-    lax.fori_loop(EARLY + 1, full - 1, functools.partial(main, False), 0)
-    for copy in loads(full, full % 2, tail):
-        copy.start()
-    forward_step(full - 1)
-    grad_part(full - 2, False)
-    for unit in range(max(0, full - 5), EARLY):
-        reduction.a_step(unit)
-    for unit in range(max(0, full - 7), EARLY):
-        reduction.b_step(unit)
-    for copy in loads(full, full % 2, tail):
+    for which in range(3):
+        lhs_copy(which).wait()
+    lax.fori_loop(1, XY_EARLY + 1, xy_main, 0)
+    lax.fori_loop(XY_EARLY + 1, full, z_main, 0)
+    slot = full % 2
+    for copy in loads(full, slot, tail):
         copy.wait()
-    slot = full % 2
     forward_part(full, w_buf[slot, 0, :tail], w_buf[slot, 1, :tail], w_buf[slot, 2, :tail], tail)
-    grad_part(full - 1, False)
-
-    gain_out[...] = jnp.zeros_like(gain_out)
-
-    def norm_backward(step, carry):
+    for part in range(D // CHUNK):
+        value_load(part).start()
+    feed.a_copy(full - 1 - SLOTS).wait_send()
+    grad_part(full - 1)
+
+    gains[...] = jnp.zeros_like(gains)
+
+    def norm_backward_ffn(step, carry):
         at = pl.ds(pl.multiple_of(step * STEP_ROWS, 16), STEP_ROWS)
         value, grad = residual[at, :], gnf[at, :]
         scale = lax.rsqrt(jnp.mean(value * value, axis=-1, keepdims=True) + eps_norm)
-        gain_out[0:1, :] += jnp.sum(grad * value * scale, axis=0, keepdims=True)
+        gains[0:1, :] += jnp.sum(grad * value * scale, axis=0, keepdims=True)
         weighted = grad * gain_ref[...]
         mean = jnp.mean(weighted * value, axis=-1, keepdims=True)
         total = cot_ref[at, :].astype(F32) + scale * weighted - value * (scale * scale * scale * mean)
-        gres_ref[at, :] = total
-        right_out[at, :] = total.astype(BF16)
+        gnf[at, :] = total
+        right[3, at, :] = total[:, : 3 * CHUNK].astype(BF16)
+        right[0, at, :CHUNK] = total[:, 3 * CHUNK :].astype(BF16)
         output_ref[at, :] = out_acc[at, :].astype(BF16)
         return carry
 
-    lax.fori_loop(0, tokens // STEP_ROWS, norm_backward, 0)
-    out_pair = sending(
-        right_out.at[pl.ds(0, tokens), :], right_out.at[pl.ds(padded, tokens), :],
-        pair_sems.at[0, full + 1], pair_sems.at[1, full + 1], row_group, partner,
-    )
-    out_pair.start()
-    grad_part(full, False)
-    gmixed_ref[...] = nt(right_out[:tokens, :], wo_ref[...]).astype(BF16)
-    out_pair.wait()
-    for col in range(0, D, CHUNK):
-        store_blocks(parts_o, 0, col, nn(lhs[2], right_out[:, col : col + CHUNK]), groups)
-
-    def finish(unit, carry):
-        write_unit(reduction.z_step(unit), pl.multiple_of(unit * CHUNK, CHUNK), CHUNK, gate_out, up_out, down_out)
-        return carry
-
-    lax.fori_loop(0, EARLY, finish, 0)
-
-    def sent(unit, carry):
-        reduction.wait_sent(unit)
-        return carry
-
-    lax.fori_loop(0, EARLY, sent, 0)
-
-
-ANY_SPEC = pl.BlockSpec(memory_space=pl.ANY)
-
-
-def feed_forward(groups, branch, x, cotangent, gain, w_out, w_gate_t, w_up_t, w_down):
-    tokens = branch.shape[0]
-    width = w_down.shape[0]
-    full = width // CHUNK
-    padded = (tokens + 127) // 128 * 128
-    cols = 3 * CHUNK
-    rows = 32 * groups
-    dma = pltpu.SemaphoreType.DMA
-    return pl.pallas_call(
-        functools.partial(ffn_kernel, groups, tokens, width),
-        name="feed_forward",
-        out_shape=[
-            jax.ShapeDtypeStruct((tokens, D), BF16),
-            jax.ShapeDtypeStruct((tokens, D), F32),
-            jax.ShapeDtypeStruct((tokens, D), BF16),
-            jax.ShapeDtypeStruct((32, EARLY * CHUNK), F32),
-            jax.ShapeDtypeStruct((32, EARLY * CHUNK), F32),
-            jax.ShapeDtypeStruct((32, EARLY * CHUNK), F32),
-            jax.ShapeDtypeStruct((full + 1 - EARLY, 2, 2, rows, cols), BF16),
-            jax.ShapeDtypeStruct((1, 2, 2, rows, D), BF16),
-            jax.ShapeDtypeStruct((8, D), F32),
-        ],
-        in_specs=[VMEM_SPEC] * 5 + [ANY_SPEC] * 3,
-        out_specs=[VMEM_SPEC] * 9,
-        scratch_shapes=[
-            pltpu.VMEM((tokens, D), F32),
-            pltpu.VMEM((tokens, D), BF16),
-            pltpu.VMEM((tokens, D), F32),
-            pltpu.VMEM((tokens, D), F32),
-            pltpu.VMEM((2, 3, CHUNK, D), BF16),
-            pltpu.VMEM((D, padded), BF16),
-            pltpu.VMEM((3, D // 2, 2 * padded), BF16),
-            pltpu.VMEM((3, D // 2, padded), BF16),
-            pltpu.VMEM((4, 2 * padded, cols), BF16),
-            pltpu.VMEM((2 * padded, D), BF16),
-        ]
-        + reduction_scratch(groups, EARLY, cols)
-        + [dma((2, 3)), dma((2, 3)), dma((2, full + 2))],
-        compiler_params=pltpu.CompilerParams(collective_id=2, has_side_effects=True, vmem_limit_bytes=60 << 20),
-    )(branch, x, cotangent, gain.reshape(1, D), w_out, w_gate_t, w_up_t, w_down)
-
-
-def last_kernel(
-    groups, seq_devices, rows, length, width,
-    grad_ref, doc_ref, got, heads, inverse_ref, x_ref, gres_ref, gain_ref, wq_ref, wk_ref, wv_ref,
-    rest, parts_o, gate_early, up_early, down_early, gain_rows,
-    input_out, gate_out, up_out, down_out, wout_out, query_out, key_out, value_out, gains_out,
-    arrived, out_buf, back, gather, qa, ka, ve, dn, qs, kt, dqt, gqk, gv, turned, lhs, lhs_send, right, gnorm,
-    gains, gains_got,
-    send_a, recv_a, send_b, recv_b, lhs_sems, pair_sems, gain_send, gain_recv,
-    f_a, f_b, f_z, fa_sems, fb_sems, fz_send, fz_recv,
-    o_a, o_b, o_z, oa_sems, ob_sems, oz_send, oz_recv,
-    q_source, q_a, q_b, q_z, qa_sems, qb_sems, qz_send, qz_recv,
-):
-    row_group, me = lax.axis_index("dp"), lax.axis_index("seq")
-    core, _, _ = place(me)
-    partner = me + 1 - 2 * core
-    tokens = rows * length
-    padded = turned.shape[1]
-    low = packed_rows(length)
-    lower = lanes_of((low, 128)) < 64
-    here = pl.ds(pl.multiple_of(me * length, 16), length)
-    f_units = rest.shape[0]
-    feed = Reduction(groups, rest, f_a, f_b, f_z, fa_sems, fb_sems, fz_send, fz_recv)
-    outer = Reduction(groups, parts_o, o_a, o_b, o_z, oa_sems, ob_sems, oz_send, oz_recv)
-    qkv = Reduction(groups, q_source, q_a, q_b, q_z, qa_sems, qb_sems, qz_send, qz_recv)
-
-    barrier = pltpu.get_barrier_semaphore()
-    for step in range(1, seq_devices):
-        peer = lax.rem(me + step, seq_devices)
-        pl.semaphore_signal(barrier, inc=1, device_id=(row_group, peer), device_id_type=MESH)
-    for step in range(1, groups):
-        other = lax.rem(row_group + step, groups)
-        pl.semaphore_signal(barrier, inc=1, device_id=(other, me), device_id_type=MESH)
-    pl.semaphore_wait(barrier, seq_devices + groups - 2)
+    lax.fori_loop(0, tokens // STEP_ROWS, norm_backward_ffn, 0)
+    normed[...] = (
+        nt(right[3, :tokens, :], wo_ref[:, : 3 * CHUNK]) + nt(right[0, :tokens, :CHUNK], wo_ref[:, 3 * CHUNK :])
+    ).astype(BF16)
 
     def outgoing(row, step):
         peer = lax.rem(me + step, seq_devices)
         theirs = pl.ds(pl.multiple_of(peer * PAIR, 128), PAIR)
+        at = pl.ds(pl.multiple_of(row * length, 16), length)
         return sending(
-            grad_ref.at[row, :, theirs], arrived.at[row, here, :], send_a.at[row, step], recv_a.at[row, step],
+            normed.at[at, theirs], arrived.at[row, here, :], send_a.at[row, step], recv_a.at[row, step],
             row_group, peer,
         )
 
     def returning(row, step):
         peer = lax.rem(me + step, seq_devices)
         return sending(
-            out_buf.at[row, peer], back.at[row, me], send_b.at[row, step], recv_b.at[row, step], row_group, peer
+            got.at[row, peer], back.at[row, me], send_b.at[row, step], recv_b.at[row, step], row_group, peer
         )
 
     def send_row(row, carry):
         for step in range(1, seq_devices):
             outgoing(row, step).start()
-        arrived[row, here, :] = grad_ref[row, :, pl.ds(pl.multiple_of(me * PAIR, 128), PAIR)]
+        at = pl.ds(pl.multiple_of(row * length, 16), length)
+        arrived[row, here, :] = normed[at, pl.ds(pl.multiple_of(me * PAIR, 128), PAIR)]
         return carry
 
     lax.fori_loop(0, rows, send_row, 0)
-
-    def norm_forward(row, carry):
-        at = pl.ds(pl.multiple_of(row * length, 16), length)
-        right[at, :D] = rms_scale(x_ref[at, :].astype(F32), gain_ref[...]).astype(BF16)
-        return carry
-
-    lax.fori_loop(0, rows, norm_forward, 0)
-    turn(right[:tokens, :D], tokens, padded, turned)
-    split_rows(turned, lhs, lhs_send, core, groups)
-    lhs_copy = sending(
-        lhs_send, lhs.at[:, pl.ds(padded, padded)], lhs_sems.at[0], lhs_sems.at[1], row_group, partner
-    )
-    lhs_copy.start()
-    gap = padded - tokens
-    for base in (tokens, padded + tokens):
-        right[base : base + gap, :] = jnp.zeros((gap, right.shape[1]), BF16)
+    feed.a_step(3)
+    feed.a_copy(full - SLOTS).wait_send()
+    grad_part(full)
+    out_pairs = [right_copy(3, 3 * CHUNK, full + 1), right_copy(0, CHUNK, full + 2)]
+    for copy in out_pairs:
+        copy.start()
+    feed.a_copy(full - 1).start()
+    feed.a_copy(full).start()
+    prepare_lhs(3, rms_scale(x_ref[...].astype(F32), gain_attn_ref[...]).astype(BF16))
+    clear(1, 1)
+    for copy in out_pairs:
+        copy.wait()
+    lhs_copy(3).start()
+    for col in range(0, D, CHUNK):
+        columns = right[3, :, col : col + CHUNK] if col < 3 * CHUNK else right[0, :, :CHUNK]
+        store_blocks(parts_o, 0, col, nn(left(2), columns), groups)
+    gather = right.at[3, pl.ds(0, 2 * half), pl.ds(0, 2 * half)]
     gather[...] = gather_matrix()
+    for copy in saved:
+        copy.wait()
 
     def attend(row, carry):
         prepare_row(got, row, qa, ka, ve, seq_devices, length)
         for step in range(1, seq_devices):
             outgoing(row, step).wait_recv()
         attend_backward(
-            row_ends(doc_ref, row), arrived.at[row], qa, ka, ve, heads.at[row], inverse_ref.at[row],
+            row_ends(doc_ref, row), arrived.at[row], qa, ka, ve, heads.at[row], inverse.at[row],
             dn, qs, kt, dqt, gqk, gv,
         )
 
         def pack(peer, inner):
             at = pl.multiple_of(peer * length, 16)
-            out_buf[row, peer, :length, :] = gv[pl.ds(at, length), :]
-            first = gqk[pl.ds(at, low), :]
-            second = pltpu.roll(gqk[pl.ds(at + length - low, low), :], 64, 1)
-            out_buf[row, peer, length:, :] = jnp.where(lower, first, second).astype(BF16)
+            got[row, peer, :length, :] = gv[pl.ds(at, length), :]
+            front = gqk[pl.ds(at, low), :]
+            rear = pltpu.roll(gqk[pl.ds(at + length - low, low), :], 64, 1)
+            got[row, peer, length:, :] = jnp.where(lower, front, rear).astype(BF16)
             return inner
 
         lax.fori_loop(0, seq_devices, pack, 0)
         for step in range(1, seq_devices):
             returning(row, step).start()
-        back[row, me] = out_buf[row, me]
-        feed.a_copy(row).start()
+        back[row, me] = got[row, me]
+
+        @pl.when(row < 2)
+        def _():
+            feed.a_step(4 + row)
+
+        feed.b_step(2 + row)
         return carry
 
     lax.fori_loop(0, rows, attend, 0)
-    for unit in range(rows, f_units):
-        feed.a_copy(unit).start()
     outer.a_copy(0).start()
-    feed.a_step(0)
-    feed.a_step(1)
-    feed.a_step(2)
+    feed.b_step(2 + rows)
+    feed.a_step(full - 1)
+    first.z_step(XY_EARLY)
+    feed.a_step(full)
 
     def unpack(row, carry):
         for step in range(1, seq_devices):
@@ -995,40 +1036,44 @@
                 halves.append(jnp.concatenate([straight, other[2 * low - length :]], axis=0))
             tiles.append(jnp.where(lanes_of((length, 128)) < 64, halves[0], halves[1]).astype(BF16))
         at = pl.ds(pl.multiple_of(row * length, 16), length)
-        right[at, : 2 * H * F] = nn(jnp.concatenate(tiles, axis=1), gather[...]).astype(BF16)
+        right[1, at, : 2 * half] = nn(jnp.concatenate(tiles, axis=1), gather[...]).astype(BF16)
         for pair in range(seq_devices):
-            col = 2 * H * F + pair * PAIR
-            right[at, col : col + PAIR] = back[row, pair, :length, :]
+            slot, col = divmod(2 * half + pair * PAIR, 3 * CHUNK)
+            right[1 + slot, at, col : col + PAIR] = back[row, pair, :length, :]
         return carry
 
     lax.fori_loop(0, rows, unpack, 0)
-    pair = sending(
-        right.at[pl.ds(0, tokens), :], right.at[pl.ds(padded, tokens), :], pair_sems.at[0], pair_sems.at[1],
-        row_group, partner,
-    )
-    pair.start()
-    half = H * F
-    gnorm[...] = (
-        nt(right[:tokens, :half], wq_ref[...])
-        + nt(right[:tokens, half : 2 * half], wk_ref[...])
-        + nt(right[:tokens, 2 * half :], wv_ref[...])
-    )
-    lhs_copy.wait()
-    pair.wait()
-    for col in range(0, right.shape[1], CHUNK):
-        store_blocks(q_source, 0, col, nn(lhs[...], right[:, col : col + CHUNK]), groups)
+    q_pairs = [right_copy(1, 3 * CHUNK, full + 3), right_copy(2, 3 * CHUNK, full + 4)]
+    for copy in q_pairs:
+        copy.start()
+    for part in range(D // CHUNK):
+        value_load(part).wait()
+    q_and_k = nt(right[1, :tokens, :half], wq_ref[...]) + nt(right[1, :tokens, half : 2 * half], wk_ref[...])
+    for part in range(D // CHUNK):
+        at = slice(part * CHUNK, (part + 1) * CHUNK)
+        block = w_buf[part // 3, part % 3]
+        out_acc[:, at] = (
+            q_and_k[:, at]
+            + nt(right[1, :tokens, 2 * half :], block[:, : 3 * CHUNK - 2 * half])
+            + nt(right[2, :tokens, :], block[:, 3 * CHUNK - 2 * half :])
+        )
+    lhs_copy(3).wait()
+    for copy in q_pairs:
+        copy.wait()
+    for slot in range(2):
+        for col in range(0, 3 * CHUNK, CHUNK):
+            grads = nn(left(0), right[1 + slot, :, col : col + CHUNK])
+            store_blocks(q_source, 0, slot * 3 * CHUNK + col, grads, groups)
     qkv.a_copy(0).start()
-
-    gains[...] = gain_rows[...]
 
     def norm_backward(step, carry):
         at = pl.ds(pl.multiple_of(step * STEP_ROWS, 16), STEP_ROWS)
-        value, grad = x_ref[at, :].astype(F32), gnorm[at, :]
+        value, grad = x_ref[at, :].astype(F32), out_acc[at, :]
         scale = lax.rsqrt(jnp.mean(value * value, axis=-1, keepdims=True) + eps_norm)
         gains[1:2, :] += jnp.sum(grad * value * scale, axis=0, keepdims=True)
-        weighted = grad * gain_ref[...]
+        weighted = grad * gain_attn_ref[...]
         mean = jnp.mean(weighted * value, axis=-1, keepdims=True)
-        total = gres_ref[at, :] + scale * weighted - value * (scale * scale * scale * mean)
+        total = gnf[at, :] + scale * weighted - value * (scale * scale * scale * mean)
         input_out[at, :] = total.astype(BF16)
         return carry
 
@@ -1044,43 +1089,42 @@
         gain_copy(1, row_group, feed.peer_a),
         gain_copy(2, row_group, feed.peer_b),
     ] + [gain_copy(2 + step, lax.rem(row_group + step, groups), me) for step in range(1, groups)]
+
+    def write_feed(unit, total, w):
+        at = unit * CHUNK if isinstance(unit, int) else pl.multiple_of(unit * CHUNK, CHUNK)
+        write_unit(total, at, w, gate_out, up_out, down_out)
+
+    def finish(unit, carry):
+        write_feed(unit, feed.z_step(unit), CHUNK)
+        return carry
+
     gain_copies[0].start()
-    early = gate_early.shape[1]
-    gate_out[:, :early] = gate_early[...]
-    up_out[:, :early] = up_early[...]
-    down_out[:, :early] = down_early[...]
+    first.z_step(XY_EARLY + 1)
+    outer.a_step(0)
     gain_copies[0].wait()
     gains[...] += gains_got[0]
     gain_copies[1].start()
-    for unit in range(3, f_units):
-        feed.a_step(unit)
-        feed.b_step(unit - 3)
+    feed.b_step(full - 1)
+    first.a_step(XY_EARLY)
+    first.z_step(XY_EARLY + 2)
+    feed.b_step(full)
     gain_copies[1].wait()
     gains[...] += gains_got[1]
     gain_copies[2].start()
-    outer.a_step(0)
-    feed.b_step(f_units - 3)
     qkv.a_step(0)
-    feed.b_step(f_units - 2)
-    feed.b_step(f_units - 1)
+    outer.b_step(0)
+    first.a_step(XY_EARLY + 1)
     gain_copies[2].wait()
     gains[...] += gains_got[2]
     for copy in gain_copies[3:]:
         copy.start()
-
-    def write_feed(unit, w):
-        at = early + unit * CHUNK
-        at = at if isinstance(at, int) else pl.multiple_of(at, CHUNK)
-        write_unit(feed.z_step(unit), at, w, gate_out, up_out, down_out)
-
-    def finish(unit, carry):
-        write_feed(unit, CHUNK)
-        return carry
-
-    lax.fori_loop(0, f_units - 3, finish, 0)
-    outer.b_step(0)
-    lax.fori_loop(f_units - 3, f_units - 1, finish, 0)
-    write_feed(f_units - 1, width - early - (f_units - 1) * CHUNK)
+    first.a_step(XY_EARLY + 2)
+    lax.fori_loop(0, XY_EARLY, finish, 0)
+    qkv.b_step(0)
+    lax.fori_loop(full - 1, full, finish, 0)
+    write_feed(full, feed.z_step(full), tail)
+    for unit in range(XY_EARLY, full - 1):
+        write_feed(unit, first.b_step(unit), CHUNK)
     for copy in gain_copies[3:]:
         copy.wait()
     for step in range(1, groups):
@@ -1089,38 +1133,47 @@
     gains_out[...] = jnp.dot(
         gains[...], jnp.where(picked, 1.0, 0.0), precision=lax.Precision.HIGHEST, preferred_element_type=F32
     )
-    qkv.b_step(0)
     wout_out[...] = outer.z_step(0)
     total = qkv.z_step(0)
     query_out[...] = total[:, :half]
     key_out[...] = total[:, half : 2 * half]
     value_out[...] = total[:, 2 * half :]
 
-    def sent(unit, carry):
-        feed.wait_sent(unit)
-        return carry
-
-    lax.fori_loop(0, f_units, sent, 0)
-    outer.wait_sent(0)
-    qkv.wait_sent(0)
-
-
-def last_part(
-    groups, seq_devices, grad, doc_lengths, got, heads, inverse, x, gres, gain, w_query, w_key, w_value,
-    rest, parts_o, gate_early, up_early, down_early, gain_rows, width,
+    for unit in range(XY_EARLY, full - 1):
+        first.wait_sent(unit)
+    for unit in range(full + 1):
+        if unit < XY_EARLY or unit >= full - 1:
+            feed.wait_sent(unit)
+            if unit > full - SLOTS:
+                feed.a_copy(unit).wait_send()
+    for one in (outer, qkv):
+        one.wait_sent(0)
+        one.a_copy(0).wait_send()
+
+
+ANY_SPEC = pl.BlockSpec(memory_space=pl.ANY)
+
+
+def backward_part(
+    groups, seq_devices, branch, x, cotangent, gain_ffn, w_out, w_gate_t, w_up_t, w_down,
+    doc_lengths, got, heads, inverse, gain_attn, w_query, w_key, w_value,
 ):
-    rows, length, _ = grad.shape
-    tokens = rows * length
+    tokens = branch.shape[0]
+    rows = doc_lengths.shape[0]
+    length = tokens // rows
     total = seq_devices * length
+    width = w_down.shape[0]
+    full = width // CHUNK
     padded = (tokens + 127) // 128 * 128
-    message = (rows, seq_devices, length + packed_rows(length), 128)
+    unit_rows = 32 * groups
     dma = pltpu.SemaphoreType.DMA
     sems = dma((rows, seq_devices))
-    cols = 2 * H * F + D
+    z_units = full - 1 - XY_EARLY
     return pl.pallas_call(
-        functools.partial(last_kernel, groups, seq_devices, rows, length, width),
-        name="attention_backward",
+        functools.partial(backward_kernel, groups, seq_devices, rows, length, width),
+        name="backward",
         out_shape=[
+            jax.ShapeDtypeStruct((tokens, D), BF16),
             jax.ShapeDtypeStruct((tokens, D), BF16),
             jax.ShapeDtypeStruct((32, width), F32),
             jax.ShapeDtypeStruct((32, width), F32),
@@ -1131,13 +1184,24 @@
             jax.ShapeDtypeStruct((32, D), F32),
             jax.ShapeDtypeStruct((8, 128), F32),
         ],
-        in_specs=[VMEM_SPEC, SMEM_SPEC] + [VMEM_SPEC] * 15,
-        out_specs=[VMEM_SPEC] * 9,
+        in_specs=[VMEM_SPEC] * 5 + [ANY_SPEC] * 3 + [SMEM_SPEC] + [ANY_SPEC] * 3 + [VMEM_SPEC] * 3 + [ANY_SPEC],
+        out_specs=[VMEM_SPEC] * 10,
         scratch_shapes=[
+            pltpu.VMEM((tokens, D), F32),
+            pltpu.VMEM((tokens, D), BF16),
+            pltpu.VMEM((tokens, D), F32),
+            pltpu.VMEM((tokens, D), F32),
+            pltpu.VMEM((2, 3, CHUNK, D), BF16),
+            pltpu.VMEM((3, 2, 2, unit_rows, 2 * padded), BF16),
+            pltpu.VMEM((4, 2 * padded, 3 * CHUNK), BF16),
+            pltpu.VMEM((SLOTS, 2, 2, unit_rows, 3 * CHUNK), BF16),
+            pltpu.VMEM((1, 2, 2, unit_rows, D), BF16),
+            pltpu.VMEM((1, 2, 2, unit_rows, 6 * CHUNK), BF16),
+            pltpu.VMEM(got.shape, BF16),
+            pltpu.VMEM(heads.shape, BF16),
+            pltpu.VMEM(inverse.shape, F32),
             pltpu.VMEM((rows, total, 128), BF16),
-            pltpu.VMEM(message, BF16),
-            pltpu.VMEM(message, BF16),
-            pltpu.VMEM((2 * H * F, 2 * H * F), BF16),
+            pltpu.VMEM(got.shape, BF16),
             pltpu.VMEM((total, 128), BF16),
             pltpu.VMEM((2, total, 128), BF16),
             pltpu.VMEM((2, total, 128), BF16),
@@ -1147,23 +1211,19 @@
             pltpu.VMEM((32, total), F32),
             pltpu.VMEM((total, 128), F32),
             pltpu.VMEM((total, 128), BF16),
-            pltpu.VMEM((D, padded), BF16),
-            pltpu.VMEM((D // 2, 2 * padded), BF16),
-            pltpu.VMEM((D // 2, padded), BF16),
-            pltpu.VMEM((2 * padded, cols), BF16),
-            pltpu.VMEM((tokens, D), F32),
             pltpu.VMEM((8, D), F32),
             pltpu.VMEM((2 + groups, 8, D), F32),
-            sems, sems, sems, sems,
-            dma((2,)), dma((2,)), dma((2 + groups,)), dma((2 + groups,)),
+            dma((2, 3)), dma((D // CHUNK,)), dma((3,)), dma((2, 4)), dma((2, full + 5)),
+            sems, sems, sems, sems, dma((2 + groups,)), dma((2 + groups,)),
         ]
-        + reduction_scratch(groups, rest.shape[0], 3 * CHUNK, source=False)
-        + reduction_scratch(groups, 1, D, source=False)
-        + reduction_scratch(groups, 1, cols),
-        compiler_params=pltpu.CompilerParams(collective_id=1, has_side_effects=True, vmem_limit_bytes=60 << 20),
+        + reduction_buffers(groups, full + 1 - z_units, 3 * CHUNK)
+        + reduction_buffers(groups, 1, D)
+        + reduction_buffers(groups, 1, 6 * CHUNK)
+        + groups_first_buffers(groups, z_units, 3 * CHUNK),
+        compiler_params=pltpu.CompilerParams(collective_id=1, has_side_effects=True, vmem_limit_bytes=VMEM_BYTES),
     )(
-        grad, doc_lengths, got, heads, inverse, x, gres, gain.reshape(1, D), w_query, w_key, w_value,
-        rest, parts_o, gate_early, up_early, down_early, gain_rows,
+        branch, x, cotangent, gain_ffn.reshape(1, D), w_out, w_gate_t, w_up_t, w_down,
+        doc_lengths, got, heads, inverse, gain_attn.reshape(1, D), w_query, w_key, w_value,
     )
 
 
@@ -1173,18 +1233,13 @@
 ):
     row_count, shard_len, _ = inputs.shape
     token_count = row_count * shard_len
-    stream = inputs.reshape(token_count, D)
     branch, got, heads, inverse = attention_forward(
         seq_devices, inputs, doc_lengths, gain_attn, w_query, w_key, w_value
     )
-    output, gres, gmixed, gate_early, up_early, down_early, rest, parts_o, gain_rows = feed_forward(
-        groups, branch.reshape(token_count, D), stream, cotangent.reshape(token_count, D), gain_ffn, w_out,
-        w_gate.T, w_up.T, w_down,
-    )
-    input_grad, gate, up, down, out, query, key, value, gains = last_part(
-        groups, seq_devices, gmixed.reshape(row_count, shard_len, D), doc_lengths, got, heads, inverse, stream, gres,
-        gain_attn, w_query, w_key, w_value, rest, parts_o, gate_early, up_early, down_early, gain_rows,
-        w_down.shape[0],
+    output, input_grad, gate, up, down, out, query, key, value, gains = backward_part(
+        groups, seq_devices, branch.reshape(token_count, D), inputs.reshape(token_count, D),
+        cotangent.reshape(token_count, D), gain_ffn, w_out, w_gate.T, w_up.T, w_down,
+        doc_lengths, got, heads, inverse, gain_attn, w_query, w_key, w_value,
     )
     return (
         output.reshape(row_count, shard_len, D),

time: 232 us -> 182 us (0.78)
  Pallas kernels: 224 us -> 172 us
    pallas_call x2 -> x1, Pallas kernels: 188 us -> 136 us  [backward_part(): pl.pallas_call(functools.partial(backward_kernel, groups, seq_devices, ro...]
    unnamed x27 -> x25, local copies, waits for them, and re-layouts: 6.61 us -> 7.89 us
where the time goes in v3:
time: 182 us
  Pallas kernels  172 us (95%)
  local copies, waits for them, and re-layouts  9.17 us (5%)
    pallas_call x1, Pallas kernels, backward_part(): pl.pallas_call(functools.partial(backward_kernel, groups, seq_devices, ro...  136 us
    pallas_call x1, Pallas kernels, attention_forward(): pl.pallas_call(functools.partial(forward_kernel, seq_devices, rows, lengt...  35.8 us
    unnamed x25, local copies, waits for them, and re-layouts  7.89 us

profile of v3, /device:TPU:0, one launch (start us, length us, event | category | flops | bytes accessed | tf_op | source)
XLA Modules:
  0.0 181.9 jit_solution(17174734300902427402)
XLA Ops:
  0.6 35.8 %attention_forward.1 = (bf16[3,144,1024]{2,1,0:T(8,128)(2,1)}, bf16[3,8,224,128]{3,2,1,0:T(8,128)(2,1)}, bf16[3,1152,128]{2,1,0:T(8,128)(2,1)}, f32[3,1152,128]{2,1,0:T(8,128)}) custom-call(bf16[3,144,1024]{2,1,0:T(8,128)(2,1)} %x_ref.1, s32[3,4]{1,0:T(4,128)} %doc_ref.3, f32[1,1024]{1,0:T(1,128)} %bitcast.22, bf16[1024,256]{1,0:T(8,128)(2,1)} %wq_ref.3, ...), custom_call_target="tpu_custom_call" | custom-call | tf_op jit(solution)/shard_map/attention_forward/pallas_call | solution.py:510
  36.4 136.3 %backward.1 = (bf16[432,1024]{1,0:T(8,128)(2,1)}, bf16[432,1024]{1,0:T(8,128)(2,1)}, f32[32,2752]{1,0:T(8,128)}, f32[32,2752]{1,0:T(8,128)}, f32[32,2752]{1,0:T(...) custom-call(bf16[432,1024]{1,0:T(8,128)(2,1)} %bitcast.20, ...), custom_call_target="tpu_custom_call" | custom-call | tf_op jit(solution)/shard_map/backward/pallas_call | solution.py:1172
  172.7 0.0 copy-start
  172.7 0.0 copy-start.7
  172.7 0.0 copy-start.6
  172.7 0.0 copy-start.5
  172.8 0.0 copy-start.4
  172.8 1.3 slice_bitcast_fusion
  174.0 0.0 copy-start.3
  174.0 0.0 copy-start.2
  174.0 2.2 %copy.32 = bf16[3,144,1024]{2,1,0:T(8,128)(2,1)} copy(bf16[3,144,1024]{2,1,0:T(8,128)(2,1)} %bitcast.18) | data formatting | bytes 1769472
  176.3 0.0 copy-done
  176.3 0.0 copy-start.1
  176.3 0.9 copy.33
  177.2 0.0 copy-done.7
  177.2 0.6 copy.34
  177.8 0.0 copy-done.6
  177.8 0.6 copy.35
  178.4 0.0 copy-done.5
  178.4 0.7 copy.36
  179.1 0.0 copy-done.4
  179.1 0.7 copy.37
  179.7 0.0 copy-done.3
  179.7 0.7 copy.38
  180.5 0.0 copy-done.2
  180.5 0.7 copy.39
  181.2 0.0 copy-done.1
  181.2 0.7 copy.40
Async XLA Ops:
  172.7 3.5 %copy-start = (bf16[432,1024]{1,0:T(8,128)(2,1)S(1)}, bf16[432,1024]{1,0:T(8,128)(2,1)}, u32[]{:S(2)}) copy-start(bf16[432,1024]{1,0:T(8,128)(2,1)} %get-tuple-element.30) | copy-start | bytes 2654212
  172.7 4.4 %copy-start.7 = (f32[32,256]{1,0:T(8,128)S(1)}, f32[32,256]{1,0:T(8,128)}, u32[]{:S(2)}) copy-start(f32[32,256]{1,0:T(8,128)} %get-tuple-element.55) | copy-start | bytes 98308
  172.7 5.1 %copy-start.6 = (f32[32,256]{1,0:T(8,128)S(1)}, f32[32,256]{1,0:T(8,128)}, u32[]{:S(2)}) copy-start(f32[32,256]{1,0:T(8,128)} %get-tuple-element.56) | copy-start | bytes 98308
  172.7 5.7 %copy-start.5 = (f32[32,1024]{1,0:T(8,128)S(1)}, f32[32,1024]{1,0:T(8,128)}, u32[]{:S(2)}) copy-start(f32[32,1024]{1,0:T(8,128)} %get-tuple-element.57) | copy-start | bytes 393220
  172.8 6.3 %copy-start.4 = (f32[32,1024]{1,0:T(8,128)S(1)}, f32[32,1024]{1,0:T(8,128)}, u32[]{:S(2)}) copy-start(f32[32,1024]{1,0:T(8,128)} %get-tuple-element.58) | copy-start | bytes 393220
  174.0 5.7 %copy-start.3 = (f32[32,2752]{1,0:T(8,128)S(1)}, f32[32,2752]{1,0:T(8,128)}, u32[]{:S(2)}) copy-start(f32[32,2752]{1,0:T(8,128)} %get-tuple-element.60) | copy-start | bytes 1056772
  174.0 6.4 %copy-start.2 = (f32[32,2752]{1,0:T(8,128)S(1)}, f32[32,2752]{1,0:T(8,128)}, u32[]{:S(2)}) copy-start(f32[32,2752]{1,0:T(8,128)} %get-tuple-element.61) | copy-start | bytes 1056772
  176.3 4.9 %copy-start.1 = (f32[32,2752]{1,0:T(8,128)S(1)}, f32[32,2752]{1,0:T(8,128)}, u32[]{:S(2)}) copy-start(f32[32,2752]{1,0:T(8,128)} %get-tuple-element.38) | copy-start | bytes 1056772

commit v4 on v3

--- a/solution.py
+++ b/solution.py
@@ -410,16 +410,6 @@
     gqk_ref[...] += queries.T
 
 
-def greet(seq_devices):
-    row_group, me = lax.axis_index("dp"), lax.axis_index("seq")
-    barrier = pltpu.get_barrier_semaphore()
-    for step in range(1, seq_devices):
-        peer = lax.rem(me + step, seq_devices)
-        pl.semaphore_signal(barrier, inc=1, device_id=(row_group, peer), device_id_type=MESH)
-    pl.semaphore_wait(barrier, seq_devices - 1)
-    return row_group, me
-
-
 def sending(source, target, send_sem, recv_sem, row_group, peer):
     return pltpu.make_async_remote_copy(
         src_ref=source,
@@ -431,111 +421,13 @@
     )
 
 
-def forward_kernel(
-    seq_devices, rows, length,
-    x_ref, doc_ref, gain_ref, wq_ref, wk_ref, wv_ref,
-    branch_ref, got_out, head_out, inverse_ref,
-    out_buf, got, heads, back, spread, qa, ka, ve, send_a, recv_a, send_b, recv_b,
-):
-    row_group, me = greet(seq_devices)
-    low = packed_rows(length)
-    lower = lanes_of((low, 128)) < 64
-    spread[...] = spread_matrix()
-
-    def outgoing(row, step):
-        peer = lax.rem(me + step, seq_devices)
-        return sending(
-            out_buf.at[row, peer], got.at[row, me], send_a.at[row, step], recv_a.at[row, step], row_group, peer
-        )
-
-    def returning(row, step):
-        peer = lax.rem(me + step, seq_devices)
-        there = pl.ds(pl.multiple_of(peer * length, 16), length)
-        mine = pl.ds(pl.multiple_of(me * PAIR, 128), PAIR)
-        return sending(
-            heads.at[row, there, :], back.at[row, :, mine], send_b.at[row, step], recv_b.at[row, step], row_group, peer
-        )
-
-    def project_row(row, carry):
-        stream = x_ref[row].astype(F32)
-        normed = rms_scale(stream, gain_ref[...]).astype(BF16)
-        both = jnp.concatenate([nn(normed, wq_ref[...]), nn(normed, wk_ref[...])], axis=1).astype(BF16)
-        tiles = nn(both, spread[...])
-        values = nn(normed, wv_ref[...]).astype(BF16)
-        for pair in range(seq_devices):
-            tile = tiles[:, pair * 128 : (pair + 1) * 128]
-            out_buf[row, pair, :length, :] = values[:, pair * PAIR : (pair + 1) * PAIR]
-            out_buf[row, pair, length:, :] = jnp.where(lower, tile[:low], tile[length - low :]).astype(BF16)
-        for step in range(1, seq_devices):
-            outgoing(row, step).start()
-        got[row, me] = out_buf[row, me]
-        return carry
-
-    lax.fori_loop(0, rows, project_row, 0)
-
-    def attend(row, carry):
-        for step in range(1, seq_devices):
-            outgoing(row, step).wait_recv()
-        prepare_row(got, row, qa, ka, ve, seq_devices, length)
-        attend_forward(row_ends(doc_ref, row), qa, ka, ve, heads.at[row], inverse_ref.at[row])
-        for step in range(1, seq_devices):
-            returning(row, step).start()
-        here = pl.ds(pl.multiple_of(me * length, 16), length)
-        back[row, :, pl.ds(pl.multiple_of(me * PAIR, 128), PAIR)] = heads[row, here, :]
-        return carry
-
-    lax.fori_loop(0, rows, attend, 0)
-    got_out[...] = got[...]
-    head_out[...] = heads[...]
-
-    def finish(row, carry):
-        for step in range(1, seq_devices):
-            outgoing(row, step).wait_send()
-            returning(row, step).wait()
-        branch_ref[row] = back[row]
-        return carry
-
-    lax.fori_loop(0, rows, finish, 0)
-
-
 VMEM_SPEC = pl.BlockSpec(memory_space=pltpu.VMEM)
 SMEM_SPEC = pl.BlockSpec(memory_space=pltpu.SMEM)
 
 
-def attention_forward(seq_devices, x, doc_lengths, gain, w_query, w_key, w_value):
-    rows, length, _ = x.shape
-    total = seq_devices * length
-    message = (rows, seq_devices, length + packed_rows(length), 128)
-    sems = pltpu.SemaphoreType.DMA((rows, seq_devices))
-    return pl.pallas_call(
-        functools.partial(forward_kernel, seq_devices, rows, length),
-        name="attention_forward",
-        out_shape=[
-            jax.ShapeDtypeStruct((rows, length, D), BF16),
-            jax.ShapeDtypeStruct(message, BF16),
-            jax.ShapeDtypeStruct((rows, total, 128), BF16),
-            jax.ShapeDtypeStruct((rows, total, 128), F32),
-        ],
-        in_specs=[VMEM_SPEC, SMEM_SPEC, VMEM_SPEC, VMEM_SPEC, VMEM_SPEC, VMEM_SPEC],
-        out_specs=[VMEM_SPEC] * 4,
-        scratch_shapes=[
-            pltpu.VMEM(message, BF16),
-            pltpu.VMEM(message, BF16),
-            pltpu.VMEM((rows, total, 128), BF16),
-            pltpu.VMEM((rows, length, D), BF16),
-            pltpu.VMEM((2 * H * F, D), BF16),
-            pltpu.VMEM((total, 128), BF16),
-            pltpu.VMEM((2, total, 128), BF16),
-            pltpu.VMEM((2, total, 128), BF16),
-            sems, sems, sems, sems,
-        ],
-        compiler_params=pltpu.CompilerParams(collective_id=0, has_side_effects=True, vmem_limit_bytes=56 << 20),
-    )(x, doc_lengths, gain.reshape(1, D), w_query, w_key, w_value)
-
-
 CHUNK = 256
 STEP_ROWS = 48
-XY_EARLY = 6
+Z_UNITS = 5
 SLOTS = 7
 VMEM_BYTES = 63 << 20
 
@@ -551,14 +443,14 @@
         pl.multiple_of(32 * (8 * group + first * i + second * j + core), 32)
         for i in range(2)
         for j in range(2)
-        for group in range(groups)
+        for group in (0, 2, 1, 3)[:groups]
     ]
 
 
 class Reduction:
-    def __init__(self, groups, source, buffers, slot_of=None, place_of=None):
-        self.groups, self.source = groups, source
-        self.got_a, self.got_b, self.got_z, self.a_sems, self.b_sems, self.z_send, self.z_recv = buffers
+    def __init__(self, source, buffers, slot_of=None, place_of=None):
+        self.source = source
+        self.got_a, self.got_b, self.got_z, self.a_sems, self.b_sems, self.c_sems, self.d_sems = buffers
         self.slot_of = slot_of or (lambda unit: unit)
         self.place_of = place_of or (lambda unit: unit)
         self.group, self.me = lax.axis_index("dp"), lax.axis_index("seq")
@@ -566,12 +458,14 @@
         self.bit_a, self.bit_b = lax.rem(self.me // first, 2), lax.rem(self.me // second, 2)
         self.peer_a = self.me + first * (1 - 2 * self.bit_a)
         self.peer_b = self.me + second * (1 - 2 * self.bit_b)
-
-    def block(self, group):
-        return pl.ds(pl.multiple_of(group * 32, 32), 32)
-
-    def other(self, step):
-        return lax.rem(self.group + step, self.groups)
+        self.bit_c, self.bit_d = lax.rem(self.group, 2), self.group // 2
+        self.group_c = self.group + 1 - 2 * self.bit_c
+        self.group_d = self.group + 2 - 4 * self.bit_d
+
+    def rows(self, bit_c, bit_d=None):
+        if bit_d is None:
+            return pl.ds(pl.multiple_of(64 * bit_c, 64), 64)
+        return pl.ds(pl.multiple_of(64 * bit_c + 32 * bit_d, 32), 32)
 
     def a_copy(self, unit):
         at = self.place_of(unit)
@@ -587,11 +481,18 @@
             self.group, self.peer_b,
         )
 
-    def z_copy(self, unit, step):
-        at = self.place_of(unit)
-        return sending(
-            self.got_b.at[at, self.block(self.other(step)), :], self.got_z.at[at, step - 1],
-            self.z_send.at[at, step - 1], self.z_recv.at[at, step - 1], self.other(step), self.me,
+    def c_copy(self, unit):
+        at = self.place_of(unit)
+        return sending(
+            self.got_b.at[at, self.rows(1 - self.bit_c), :], self.got_z.at[at, pl.ds(0, 64), :],
+            self.c_sems.at[0, at], self.c_sems.at[1, at], self.group_c, self.me,
+        )
+
+    def d_copy(self, unit):
+        at = self.place_of(unit)
+        return sending(
+            self.got_b.at[at, self.rows(self.bit_c, 1 - self.bit_d), :], self.got_z.at[at, pl.ds(64, 32), :],
+            self.d_sems.at[0, at], self.d_sems.at[1, at], self.group_d, self.me,
         )
 
     def a_step(self, unit):
@@ -605,55 +506,70 @@
         at = self.place_of(unit)
         self.b_copy(unit).wait_recv()
         self.got_b[at] = (self.got_a[at, self.bit_b].astype(F32) + self.got_b[at].astype(F32)).astype(BF16)
-        for step in range(1, self.groups):
-            self.z_copy(unit, step).start()
-
-    def z_step(self, unit):
-        at = self.place_of(unit)
-        total = self.got_b[at, self.block(self.group), :].astype(F32)
-        for step in range(1, self.groups):
-            self.z_copy(unit, step).wait_recv()
-            total += self.got_z[at, step - 1].astype(F32)
-        return total
+        self.c_copy(unit).start()
+
+    def c_step(self, unit):
+        at, mine = self.place_of(unit), self.rows(self.bit_c)
+        self.c_copy(unit).wait_recv()
+        self.got_b[at, mine, :] = (
+            self.got_b[at, mine, :].astype(F32) + self.got_z[at, :64, :].astype(F32)
+        ).astype(BF16)
+        self.d_copy(unit).start()
+
+    def d_step(self, unit):
+        at = self.place_of(unit)
+        self.d_copy(unit).wait_recv()
+        return self.got_b[at, self.rows(self.bit_c, self.bit_d), :].astype(F32) + self.got_z[at, 64:, :].astype(F32)
 
     def wait_sent(self, unit):
         self.b_copy(unit).wait_send()
-        for step in range(1, self.groups):
-            self.z_copy(unit, step).wait_send()
+        self.c_copy(unit).wait_send()
+        self.d_copy(unit).wait_send()
 
 
 class GroupsFirst(Reduction):
-    def z_copy(self, unit, step):
-        at = self.place_of(unit)
-        return sending(
-            self.source.at[self.slot_of(unit), :, :, self.block(self.other(step)), :], self.got_z.at[at, step - 1],
-            self.z_send.at[at, step - 1], self.z_recv.at[at, step - 1], self.other(step), self.me,
+    def c_copy(self, unit):
+        at = self.place_of(unit)
+        return sending(
+            self.source.at[self.slot_of(unit), :, :, self.rows(1 - self.bit_c), :],
+            self.got_z.at[at, :, :, pl.ds(0, 64), :],
+            self.c_sems.at[0, at], self.c_sems.at[1, at], self.group_c, self.me,
+        )
+
+    def d_copy(self, unit):
+        at = self.place_of(unit)
+        block = pl.ds(pl.multiple_of(32 * (1 - self.bit_d), 32), 32)
+        return sending(
+            self.got_z.at[at, :, :, block, :], self.got_z.at[at, :, :, pl.ds(64, 32), :],
+            self.d_sems.at[0, at], self.d_sems.at[1, at], self.group_d, self.me,
         )
 
     def a_copy(self, unit):
         at = self.place_of(unit)
         return sending(
-            self.got_z.at[at, 0, 1 - self.bit_a], self.got_a.at[at], self.a_sems.at[0, at], self.a_sems.at[1, at],
-            self.group, self.peer_a,
-        )
-
-    def start(self, unit):
-        for step in range(1, self.groups):
-            self.z_copy(unit, step).start()
-
-    def z_step(self, unit):
-        at = self.place_of(unit)
-        total = self.source[self.slot_of(unit), :, :, self.block(self.group), :].astype(F32)
-        for step in range(1, self.groups):
-            self.z_copy(unit, step).wait_recv()
-            total += self.got_z[at, step - 1].astype(F32)
-        self.got_z[at, 0] = total.astype(BF16)
+            self.got_z.at[at, 1 - self.bit_a, :, pl.ds(64, 32), :], self.got_a.at[at],
+            self.a_sems.at[0, at], self.a_sems.at[1, at], self.group, self.peer_a,
+        )
+
+    def c_step(self, unit):
+        at = self.place_of(unit)
+        self.c_copy(unit).wait_recv()
+        mine = self.source[self.slot_of(unit), :, :, self.rows(self.bit_c), :].astype(F32)
+        self.got_z[at, :, :, :64, :] = (mine + self.got_z[at, :, :, :64, :].astype(F32)).astype(BF16)
+        self.d_copy(unit).start()
+
+    def d_step(self, unit):
+        at = self.place_of(unit)
+        self.d_copy(unit).wait_recv()
+        mine = self.got_z[at, :, :, pl.ds(pl.multiple_of(32 * self.bit_d, 32), 32), :].astype(F32)
+        self.got_z[at, :, :, 64:, :] = (mine + self.got_z[at, :, :, 64:, :].astype(F32)).astype(BF16)
         self.a_copy(unit).start()
 
     def a_step(self, unit):
         at = self.place_of(unit)
         self.a_copy(unit).wait_recv()
-        self.got_a[at] = (self.got_z[at, 0, self.bit_a].astype(F32) + self.got_a[at].astype(F32)).astype(BF16)
+        mine = self.got_z[at, self.bit_a, :, 64:, :].astype(F32)
+        self.got_a[at] = (mine + self.got_a[at].astype(F32)).astype(BF16)
         self.b_copy(unit).start()
 
     def b_step(self, unit):
@@ -662,36 +578,27 @@
         return self.got_a[at, self.bit_b].astype(F32) + self.got_b[at].astype(F32)
 
     def wait_sent(self, unit):
-        self.a_copy(unit).wait_send()
-        self.b_copy(unit).wait_send()
-        for step in range(1, self.groups):
-            self.z_copy(unit, step).wait_send()
-
-
-def reduction_buffers(groups, units, cols):
-    rows = 32 * groups
-    dma = pltpu.SemaphoreType.DMA
+        for copy in (self.a_copy, self.b_copy, self.c_copy, self.d_copy):
+            copy(unit).wait_send()
+
+
+def reduction_buffers(units, cols):
+    sems = pltpu.SemaphoreType.DMA((2, units))
     return [
-        pltpu.VMEM((units, 2, rows, cols), BF16),
-        pltpu.VMEM((units, rows, cols), BF16),
-        pltpu.VMEM((units, groups - 1, 32, cols), BF16),
-        dma((2, units)),
-        dma((2, units)),
-        dma((units, groups - 1)),
-        dma((units, groups - 1)),
+        pltpu.VMEM((units, 2, 128, cols), BF16),
+        pltpu.VMEM((units, 128, cols), BF16),
+        pltpu.VMEM((units, 96, cols), BF16),
+        sems, sems, sems, sems,
     ]
 
 
-def groups_first_buffers(groups, units, cols):
-    dma = pltpu.SemaphoreType.DMA
+def groups_first_buffers(units, cols):
+    sems = pltpu.SemaphoreType.DMA((2, units))
     return [
         pltpu.VMEM((units, 2, 32, cols), BF16),
         pltpu.VMEM((units, 32, cols), BF16),
-        pltpu.VMEM((units, groups - 1, 2, 2, 32, cols), BF16),
-        dma((2, units)),
-        dma((2, units)),
-        dma((units, groups - 1)),
-        dma((units, groups - 1)),
+        pltpu.VMEM((units, 2, 2, 96, cols), BF16),
+        sems, sems, sems, sems,
     ]
 
 
@@ -720,14 +627,13 @@
     up_out[:, pl.ds(at, w)] = total[:, 2 * CHUNK : 2 * CHUNK + w]
 
 
-def backward_kernel(
+def block_kernel(
     groups, seq_devices, rows, length, width,
-    branch_ref, x_ref, cot_ref, gain_ref, wo_ref, wg_hbm, wu_hbm, wd_hbm,
-    doc_ref, got_hbm, heads_hbm, inverse_hbm, gain_attn_ref, wq_ref, wk_ref, wv_hbm,
+    x_ref, cot_ref, gain_ref, wo_ref, wg_hbm, wu_hbm, wd_hbm, doc_ref, gain_attn_ref, wq_ref, wk_ref, wv_hbm,
     output_ref, input_out, gate_out, up_out, down_out, wout_out, query_out, key_out, value_out, gains_out,
-    residual, normed, out_acc, gnf, w_buf, lhs, right, parts, parts_o, q_source,
+    branch, residual, normed, out_acc, gnf, w_buf, lhs, right, parts, parts_o, q_source,
     got, heads, inverse, arrived, back, qa, ka, ve, dn, qs, kt, dqt, gqk, gv, gains, gains_got,
-    w_sem, wv_sems, in_sems, lhs_sems, pair_sems, send_a, recv_a, send_b, recv_b, gain_send, gain_recv,
+    fsend_a, frecv_a, fsend_b, frecv_b, w_sem, wv_sems, lhs_sems, pair_sems, send_a, recv_a, send_b, recv_b, gain_send, gain_recv,
     *buffers,
 ):
     row_group, me = lax.axis_index("dp"), lax.axis_index("seq")
@@ -743,24 +649,25 @@
     half = H * F
 
     def slot_of(unit):
-        return lax.rem(unit, SLOTS)
-
-    z_units = full - 1 - XY_EARLY
+        if isinstance(unit, int):
+            return unit if unit < SLOTS else 2 * (unit - SLOTS)
+        return jnp.where(unit < SLOTS, unit, 2 * (unit - SLOTS))
 
     def place_of(unit):
-        return unit if isinstance(unit, int) and unit < XY_EARLY else jnp.where(unit < XY_EARLY, unit, unit - z_units)
-
-    feed = Reduction(groups, parts, buffers[:7], slot_of, place_of)
-    outer = Reduction(groups, parts_o, buffers[7:14])
-    qkv = Reduction(groups, q_source, buffers[14:21])
-    first = GroupsFirst(groups, parts, buffers[21:28], slot_of, lambda unit: unit - XY_EARLY)
+        if isinstance(unit, int):
+            return unit // 2 if unit < 2 * Z_UNITS else unit - Z_UNITS
+        return jnp.where(unit < 2 * Z_UNITS, unit // 2, unit - Z_UNITS)
+
+    feed = Reduction(parts, buffers[:7], slot_of, place_of)
+    outer = Reduction(parts_o, buffers[7:14])
+    qkv = Reduction(q_source, buffers[14:21])
+    first = GroupsFirst(parts, buffers[21:28], slot_of, lambda unit: unit // 2)
 
     barrier = pltpu.get_barrier_semaphore()
     for step in range(1, seq_devices):
         peer = lax.rem(me + step, seq_devices)
         pl.semaphore_signal(barrier, inc=1, device_id=(row_group, peer), device_id_type=MESH)
-    for step in range(1, groups):
-        other = lax.rem(row_group + step, groups)
+    for other in (feed.group_c, feed.group_d):
         pl.semaphore_signal(barrier, inc=1, device_id=(other, me), device_id_type=MESH)
 
     def loads(chunk, slot, w):
@@ -775,15 +682,96 @@
             wv_hbm.at[pl.ds(part * CHUNK, CHUNK), :], w_buf.at[part // 3, part % 3], wv_sems.at[part]
         )
 
+    def lhs_send(which):
+        return (q_source.at[0], q_source.at[1], parts_o.at[0])[which % 3].at[:, :, :, pl.ds(0, padded)]
+
+    def lhs_copy(which):
+        return sending(
+            lhs_send(which),
+            lhs.at[which % 3, :, :, :, pl.ds(padded, padded)],
+            lhs_sems.at[0, which], lhs_sems.at[1, which], row_group, partner,
+        )
+
+    def prepare_lhs(which, source):
+        turned = right.at[3 if which < 3 else 1, :, pl.ds(0, padded)]
+        turn(source, tokens, padded, turned)
+        split_rows(turned, lhs.at[which % 3, :, :, :, pl.ds(0, padded)], lhs_send(which), core, groups)
+
+    def left(which):
+        return lhs[which].reshape(D // 2, 2 * padded)
+
+    for part in range(D // CHUNK):
+        value_load(part).start()
+    spread = [right.at[1 + part, pl.ds(0, 2 * half), pl.ds(0, D // 2)] for part in range(2)]
+    whole = spread_matrix()
+    for part in range(2):
+        spread[part][...] = whole[:, part * D // 2 : (part + 1) * D // 2]
+    pl.semaphore_wait(barrier, seq_devices + 1)
+    for part in range(D // CHUNK):
+        value_load(part).wait()
+
+    def spreading(row, step):
+        peer = lax.rem(me + step, seq_devices)
+        return sending(
+            back.at[row, peer], got.at[row, me], fsend_a.at[row, step], frecv_a.at[row, step], row_group, peer
+        )
+
+    def merging(row, step):
+        peer = lax.rem(me + step, seq_devices)
+        there = pl.ds(pl.multiple_of(peer * length, 16), length)
+        mine = pl.ds(pl.multiple_of(me * PAIR, 128), PAIR)
+        at = pl.ds(pl.multiple_of(row * length, 16), length)
+        return sending(
+            heads.at[row, there, :], branch.at[at, mine], fsend_b.at[row, step], frecv_b.at[row, step],
+            row_group, peer,
+        )
+
+    def project_row(row, carry):
+        at = pl.ds(pl.multiple_of(row * length, 16), length)
+        low_row = rms_scale(x_ref[at, :].astype(F32), gain_attn_ref[...]).astype(BF16)
+        both = jnp.concatenate([nn(low_row, wq_ref[...]), nn(low_row, wk_ref[...])], axis=1).astype(BF16)
+        sides = [nn(both, spread[part][...]) for part in range(2)]
+        values = sum(
+            nn(low_row[:, part * CHUNK : (part + 1) * CHUNK], w_buf[part // 3, part % 3])
+            for part in range(D // CHUNK)
+        ).astype(BF16)
+        for pair in range(seq_devices):
+            side, col = divmod(pair * 128, D // 2)
+            tile = sides[side][:, col : col + 128]
+            back[row, pair, :length, :] = values[:, pair * PAIR : (pair + 1) * PAIR]
+            back[row, pair, length:, :] = jnp.where(lower, tile[:low], tile[length - low :]).astype(BF16)
+        for step in range(1, seq_devices):
+            spreading(row, step).start()
+        got[row, me] = back[row, me]
+        return carry
+
+    lax.fori_loop(0, rows, project_row, 0)
     for chunk in range(2):
         for copy in loads(chunk, chunk, CHUNK):
             copy.start()
-    saved = [
-        pltpu.make_async_copy(source, target, in_sems.at[i])
-        for i, (source, target) in enumerate(((got_hbm, got), (heads_hbm, heads), (inverse_hbm, inverse)))
-    ]
-    for copy in saved:
-        copy.start()
+    prepare_lhs(0, cot_ref[...])
+    lhs_copy(0).start()
+
+    def attend_rows(row, carry):
+        for step in range(1, seq_devices):
+            spreading(row, step).wait_recv()
+        prepare_row(got, row, qa, ka, ve, seq_devices, length)
+        attend_forward(row_ends(doc_ref, row), qa, ka, ve, heads.at[row], inverse.at[row])
+        for step in range(1, seq_devices):
+            merging(row, step).start()
+        at = pl.ds(pl.multiple_of(row * length, 16), length)
+        branch[at, pl.ds(pl.multiple_of(me * PAIR, 128), PAIR)] = heads[row, here, :]
+        return carry
+
+    lax.fori_loop(0, rows, attend_rows, 0)
+
+    def merged(row, carry):
+        for step in range(1, seq_devices):
+            spreading(row, step).wait_send()
+            merging(row, step).wait()
+        return carry
+
+    lax.fori_loop(0, rows, merged, 0)
 
     def norm_forward(step, carry):
         at = pl.ds(pl.multiple_of(step * STEP_ROWS, 16), STEP_ROWS)
@@ -793,31 +781,11 @@
         normed[at, :] = rms_scale(value, gain_ref[...]).astype(BF16)
         return carry
 
-    residual[...] = nn(branch_ref[...], wo_ref[...])
+    residual[...] = nn(branch[...], wo_ref[...])
     lax.fori_loop(0, tokens // STEP_ROWS, norm_forward, 0)
     gnf[...] = jnp.zeros_like(gnf)
 
-    pl.semaphore_wait(barrier, seq_devices + groups - 2)
-
-    def lhs_copy(which):
-        return sending(
-            q_source.at[0, :, :, :, pl.ds(which % 3 * padded, padded)],
-            lhs.at[which % 3, :, :, :, pl.ds(padded, padded)],
-            lhs_sems.at[0, which], lhs_sems.at[1, which], row_group, partner,
-        )
-
-    def prepare_lhs(which, source):
-        turned = right.at[3 if which < 3 else 1, :, pl.ds(0, padded)]
-        turn(source, tokens, padded, turned)
-        at = which % 3 * padded
-        split_rows(
-            turned, lhs.at[which % 3, :, :, :, pl.ds(0, padded)], q_source.at[0, :, :, :, pl.ds(at, padded)], core, groups
-        )
-
-    def left(which):
-        return lhs[which].reshape(D // 2, 2 * padded)
-
-    for which, source in enumerate((cot_ref, normed, branch_ref)):
+    for which, source in ((1, normed), (2, branch)):
         prepare_lhs(which, source[...])
         lhs_copy(which).start()
     gap = padded - tokens
@@ -870,22 +838,17 @@
     def ticks(chunk):
         @pl.when((chunk >= 4) & (lax.rem(chunk, 2) == 0))
         def _():
-            feed.a_step((chunk - 4) // 2)
+            feed.a_step(chunk - 4)
 
         @pl.when((chunk >= 7) & (lax.rem(chunk, 2) == 1))
         def _():
-            feed.b_step((chunk - 7) // 2)
-
-    def xy_main(chunk, carry):
-        for copy in loads(chunk + 1, lax.rem(chunk + 1, 2), CHUNK):
-            copy.start()
-        forward_step(chunk)
-        grad_part(chunk - 1)
-        feed.a_copy(chunk - 1).start()
-        ticks(chunk)
-        return carry
-
-    def z_main(chunk, carry):
+            feed.b_step(chunk - 7)
+
+        @pl.when(chunk == 8)
+        def _():
+            first.c_step(1)
+
+    def fetch_next(chunk):
         @pl.when(chunk < full - 1)
         def _():
             for copy in loads(chunk + 1, lax.rem(chunk + 1, 2), CHUNK):
@@ -896,30 +859,42 @@
             for copy in loads(full, full % 2, tail):
                 copy.start()
 
+    def main(chunk, carry):
+        fetch_next(chunk)
         forward_step(chunk)
-
-        @pl.when(chunk - 1 >= SLOTS)
+        unit = chunk - 1
+
+        @pl.when(unit >= SLOTS)
         def _():
-            feed.a_copy(chunk - 1 - SLOTS).wait_send()
-
-        grad_part(chunk - 1)
-        first.start(chunk - 1)
+            feed.a_copy(2 * (unit - SLOTS)).wait_send()
+
+        grad_part(unit)
+        along_z = (unit < 2 * Z_UNITS) & (lax.rem(unit, 2) == 1)
+
+        @pl.when(along_z)
+        def _():
+            first.c_copy(unit).start()
+
+        @pl.when(jnp.logical_not(along_z))
+        def _():
+            feed.a_copy(unit).start()
+
         ticks(chunk)
         return carry
 
     forward_step(0)
     for which in range(3):
         lhs_copy(which).wait()
-    lax.fori_loop(1, XY_EARLY + 1, xy_main, 0)
-    lax.fori_loop(XY_EARLY + 1, full, z_main, 0)
+    lax.fori_loop(1, full, main, 0)
     slot = full % 2
     for copy in loads(full, slot, tail):
         copy.wait()
     forward_part(full, w_buf[slot, 0, :tail], w_buf[slot, 1, :tail], w_buf[slot, 2, :tail], tail)
     for part in range(D // CHUNK):
         value_load(part).start()
-    feed.a_copy(full - 1 - SLOTS).wait_send()
+    feed.a_copy(2 * (full - 1 - SLOTS)).wait_send()
     grad_part(full - 1)
+    first.c_copy(full - 1).start()
 
     gains[...] = jnp.zeros_like(gains)
 
@@ -965,14 +940,15 @@
         return carry
 
     lax.fori_loop(0, rows, send_row, 0)
-    feed.a_step(3)
-    feed.a_copy(full - SLOTS).wait_send()
+    feed.a_step(6)
+    feed.a_copy(2 * (full - SLOTS)).wait_send()
     grad_part(full)
     out_pairs = [right_copy(3, 3 * CHUNK, full + 1), right_copy(0, CHUNK, full + 2)]
     for copy in out_pairs:
         copy.start()
-    feed.a_copy(full - 1).start()
-    feed.a_copy(full).start()
+    feed.b_step(4)
+    first.c_step(3)
+    feed.c_step(0)
     prepare_lhs(3, rms_scale(x_ref[...].astype(F32), gain_attn_ref[...]).astype(BF16))
     clear(1, 1)
     for copy in out_pairs:
@@ -983,8 +959,6 @@
         store_blocks(parts_o, 0, col, nn(left(2), columns), groups)
     gather = right.at[3, pl.ds(0, 2 * half), pl.ds(0, 2 * half)]
     gather[...] = gather_matrix()
-    for copy in saved:
-        copy.wait()
 
     def attend(row, carry):
         prepare_row(got, row, qa, ka, ve, seq_devices, length)
@@ -1008,19 +982,29 @@
             returning(row, step).start()
         back[row, me] = got[row, me]
 
-        @pl.when(row < 2)
+        @pl.when(row == 0)
         def _():
-            feed.a_step(4 + row)
-
-        feed.b_step(2 + row)
+            feed.a_copy(full).start()
+            feed.a_step(8)
+            feed.b_step(6)
+            first.c_step(5)
+            first.d_step(1)
+
+        @pl.when(row == 1)
+        def _():
+            outer.a_copy(0).start()
+            feed.c_step(2)
+            first.c_step(7)
+            first.d_step(3)
+
         return carry
 
     lax.fori_loop(0, rows, attend, 0)
-    outer.a_copy(0).start()
-    feed.b_step(2 + rows)
-    feed.a_step(full - 1)
-    first.z_step(XY_EARLY)
-    feed.a_step(full)
+    feed.b_step(8)
+    feed.c_step(4)
+    first.c_step(9)
+    first.d_step(5)
+    feed.a_step(10)
 
     def unpack(row, carry):
         for step in range(1, seq_devices):
@@ -1060,11 +1044,10 @@
     lhs_copy(3).wait()
     for copy in q_pairs:
         copy.wait()
-    for slot in range(2):
+    for unit in range(2):
         for col in range(0, 3 * CHUNK, CHUNK):
-            grads = nn(left(0), right[1 + slot, :, col : col + CHUNK])
-            store_blocks(q_source, 0, slot * 3 * CHUNK + col, grads, groups)
-    qkv.a_copy(0).start()
+            store_blocks(q_source, unit, col, nn(left(0), right[1 + unit, :, col : col + CHUNK]), groups)
+        qkv.a_copy(unit).start()
 
     def norm_backward(step, carry):
         at = pl.ds(pl.multiple_of(step * STEP_ROWS, 16), STEP_ROWS)
@@ -1088,77 +1071,82 @@
         gain_copy(0, row_group, partner),
         gain_copy(1, row_group, feed.peer_a),
         gain_copy(2, row_group, feed.peer_b),
-    ] + [gain_copy(2 + step, lax.rem(row_group + step, groups), me) for step in range(1, groups)]
+        gain_copy(3, feed.group_c, me),
+        gain_copy(4, feed.group_d, me),
+    ]
+
+    def gain_step(step):
+        gain_copies[step].wait()
+        gains[...] += gains_got[step]
+        if step < 4:
+            gain_copies[step + 1].start()
 
     def write_feed(unit, total, w):
         at = unit * CHUNK if isinstance(unit, int) else pl.multiple_of(unit * CHUNK, CHUNK)
         write_unit(total, at, w, gate_out, up_out, down_out)
 
-    def finish(unit, carry):
-        write_feed(unit, feed.z_step(unit), CHUNK)
-        return carry
-
     gain_copies[0].start()
-    first.z_step(XY_EARLY + 1)
+    first.d_step(7)
+    feed.c_step(6)
     outer.a_step(0)
-    gain_copies[0].wait()
-    gains[...] += gains_got[0]
-    gain_copies[1].start()
-    feed.b_step(full - 1)
-    first.a_step(XY_EARLY)
-    first.z_step(XY_EARLY + 2)
-    feed.b_step(full)
-    gain_copies[1].wait()
-    gains[...] += gains_got[1]
-    gain_copies[2].start()
+    feed.b_step(10)
+    gain_step(0)
+    first.a_step(1)
+    feed.c_step(8)
+    first.d_step(9)
+    gain_step(1)
+    first.a_step(3)
+    outer.b_step(0)
     qkv.a_step(0)
-    outer.b_step(0)
-    first.a_step(XY_EARLY + 1)
-    gain_copies[2].wait()
-    gains[...] += gains_got[2]
-    for copy in gain_copies[3:]:
-        copy.start()
-    first.a_step(XY_EARLY + 2)
-    lax.fori_loop(0, XY_EARLY, finish, 0)
+    feed.c_step(10)
+    gain_step(2)
+    first.a_step(5)
+    first.a_step(7)
+    qkv.a_step(1)
+    outer.c_step(0)
+    gain_step(3)
     qkv.b_step(0)
-    lax.fori_loop(full - 1, full, finish, 0)
-    write_feed(full, feed.z_step(full), tail)
-    for unit in range(XY_EARLY, full - 1):
+    first.a_step(9)
+    qkv.b_step(1)
+    qkv.c_step(0)
+    gain_step(4)
+    for unit in range(0, full, 2):
+        write_feed(unit, feed.d_step(unit), CHUNK)
+    qkv.c_step(1)
+    write_feed(full, feed.d_step(full), tail)
+    for unit in range(1, 2 * Z_UNITS, 2):
         write_feed(unit, first.b_step(unit), CHUNK)
-    for copy in gain_copies[3:]:
-        copy.wait()
-    for step in range(1, groups):
-        gains[...] += gains_got[2 + step]
     picked = lax.broadcasted_iota(jnp.int32, (D, 128), 0) == 32 * (seq_devices * row_group + me) + lanes_of((D, 128))
     gains_out[...] = jnp.dot(
         gains[...], jnp.where(picked, 1.0, 0.0), precision=lax.Precision.HIGHEST, preferred_element_type=F32
     )
-    wout_out[...] = outer.z_step(0)
-    total = qkv.z_step(0)
+    wout_out[...] = outer.d_step(0)
+    total = qkv.d_step(0)
     query_out[...] = total[:, :half]
     key_out[...] = total[:, half : 2 * half]
-    value_out[...] = total[:, 2 * half :]
-
-    for unit in range(XY_EARLY, full - 1):
-        first.wait_sent(unit)
+    value_out[:, : 3 * CHUNK - 2 * half] = total[:, 2 * half :]
+    value_out[:, 3 * CHUNK - 2 * half :] = qkv.d_step(1)
+
     for unit in range(full + 1):
-        if unit < XY_EARLY or unit >= full - 1:
+        if unit < 2 * Z_UNITS and unit % 2 == 1:
+            first.wait_sent(unit)
+        else:
             feed.wait_sent(unit)
-            if unit > full - SLOTS:
+            if unit > 2 * (full - SLOTS):
                 feed.a_copy(unit).wait_send()
-    for one in (outer, qkv):
-        one.wait_sent(0)
-        one.a_copy(0).wait_send()
+    for one, unit in ((outer, 0), (qkv, 0), (qkv, 1)):
+        one.wait_sent(unit)
+        one.a_copy(unit).wait_send()
 
 
 ANY_SPEC = pl.BlockSpec(memory_space=pl.ANY)
 
 
-def backward_part(
-    groups, seq_devices, branch, x, cotangent, gain_ffn, w_out, w_gate_t, w_up_t, w_down,
-    doc_lengths, got, heads, inverse, gain_attn, w_query, w_key, w_value,
+def block_step(
+    groups, seq_devices, x, cotangent, gain_ffn, w_out, w_gate_t, w_up_t, w_down, doc_lengths, gain_attn,
+    w_query, w_key, w_value,
 ):
-    tokens = branch.shape[0]
+    tokens = x.shape[0]
     rows = doc_lengths.shape[0]
     length = tokens // rows
     total = seq_devices * length
@@ -1166,12 +1154,12 @@
     full = width // CHUNK
     padded = (tokens + 127) // 128 * 128
     unit_rows = 32 * groups
+    message = (rows, seq_devices, length + packed_rows(length), 128)
     dma = pltpu.SemaphoreType.DMA
     sems = dma((rows, seq_devices))
-    z_units = full - 1 - XY_EARLY
     return pl.pallas_call(
-        functools.partial(backward_kernel, groups, seq_devices, rows, length, width),
-        name="backward",
+        functools.partial(block_kernel, groups, seq_devices, rows, length, width),
+        name="block",
         out_shape=[
             jax.ShapeDtypeStruct((tokens, D), BF16),
             jax.ShapeDtypeStruct((tokens, D), BF16),
@@ -1184,9 +1172,10 @@
             jax.ShapeDtypeStruct((32, D), F32),
             jax.ShapeDtypeStruct((8, 128), F32),
         ],
-        in_specs=[VMEM_SPEC] * 5 + [ANY_SPEC] * 3 + [SMEM_SPEC] + [ANY_SPEC] * 3 + [VMEM_SPEC] * 3 + [ANY_SPEC],
+        in_specs=[VMEM_SPEC] * 4 + [ANY_SPEC] * 3 + [SMEM_SPEC] + [VMEM_SPEC] * 3 + [ANY_SPEC],
         out_specs=[VMEM_SPEC] * 10,
         scratch_shapes=[
+            pltpu.VMEM((tokens, D), BF16),
             pltpu.VMEM((tokens, D), F32),
             pltpu.VMEM((tokens, D), BF16),
             pltpu.VMEM((tokens, D), F32),
@@ -1196,12 +1185,12 @@
             pltpu.VMEM((4, 2 * padded, 3 * CHUNK), BF16),
             pltpu.VMEM((SLOTS, 2, 2, unit_rows, 3 * CHUNK), BF16),
             pltpu.VMEM((1, 2, 2, unit_rows, D), BF16),
-            pltpu.VMEM((1, 2, 2, unit_rows, 6 * CHUNK), BF16),
-            pltpu.VMEM(got.shape, BF16),
-            pltpu.VMEM(heads.shape, BF16),
-            pltpu.VMEM(inverse.shape, F32),
+            pltpu.VMEM((2, 2, 2, unit_rows, 3 * CHUNK), BF16),
+            pltpu.VMEM(message, BF16),
             pltpu.VMEM((rows, total, 128), BF16),
-            pltpu.VMEM(got.shape, BF16),
+            pltpu.VMEM((rows, total, 128), F32),
+            pltpu.VMEM((rows, total, 128), BF16),
+            pltpu.VMEM(message, BF16),
             pltpu.VMEM((total, 128), BF16),
             pltpu.VMEM((2, total, 128), BF16),
             pltpu.VMEM((2, total, 128), BF16),
@@ -1212,19 +1201,38 @@
             pltpu.VMEM((total, 128), F32),
             pltpu.VMEM((total, 128), BF16),
             pltpu.VMEM((8, D), F32),
-            pltpu.VMEM((2 + groups, 8, D), F32),
-            dma((2, 3)), dma((D // CHUNK,)), dma((3,)), dma((2, 4)), dma((2, full + 5)),
-            sems, sems, sems, sems, dma((2 + groups,)), dma((2 + groups,)),
+            pltpu.VMEM((5, 8, D), F32),
+            sems, sems, sems, sems, dma((2, 3)), dma((D // CHUNK,)), dma((2, 4)), dma((2, full + 5)),
+            sems, sems, sems, sems, dma((5,)), dma((5,)),
         ]
-        + reduction_buffers(groups, full + 1 - z_units, 3 * CHUNK)
-        + reduction_buffers(groups, 1, D)
-        + reduction_buffers(groups, 1, 6 * CHUNK)
-        + groups_first_buffers(groups, z_units, 3 * CHUNK),
+        + reduction_buffers(full + 1 - Z_UNITS, 3 * CHUNK)
+        + reduction_buffers(1, D)
+        + reduction_buffers(2, 3 * CHUNK)
+        + groups_first_buffers(Z_UNITS, 3 * CHUNK),
         compiler_params=pltpu.CompilerParams(collective_id=1, has_side_effects=True, vmem_limit_bytes=VMEM_BYTES),
     )(
-        branch, x, cotangent, gain_ffn.reshape(1, D), w_out, w_gate_t, w_up_t, w_down,
-        doc_lengths, got, heads, inverse, gain_attn.reshape(1, D), w_query, w_key, w_value,
-    )
+        x, cotangent, gain_ffn.reshape(1, D), w_out, w_gate_t, w_up_t, w_down, doc_lengths,
+        gain_attn.reshape(1, D), w_query, w_key, w_value,
+    )
+
+
+def publish(results, gains):
+    def kernel(*refs):
+        count = len(results)
+        for source, target in zip(refs[:count], refs[count + 1 : 2 * count + 1]):
+            target[...] = source[...]
+        refs[2 * count + 1][...] = refs[count][1:2, :32]
+        refs[2 * count + 2][...] = refs[count][0:1, :32]
+
+    one = jax.ShapeDtypeStruct((1, 32), F32)
+    return pl.pallas_call(
+        kernel,
+        name="publish",
+        out_shape=[jax.ShapeDtypeStruct(x.shape, x.dtype) for x in results] + [one, one],
+        in_specs=[VMEM_SPEC] * (len(results) + 1),
+        out_specs=[VMEM_SPEC] * (len(results) + 2),
+        compiler_params=pltpu.CompilerParams(vmem_limit_bytes=VMEM_BYTES),
+    )(*results, gains)
 
 
 def tuned_body(
@@ -1233,23 +1241,22 @@
 ):
     row_count, shard_len, _ = inputs.shape
     token_count = row_count * shard_len
-    branch, got, heads, inverse = attention_forward(
-        seq_devices, inputs, doc_lengths, gain_attn, w_query, w_key, w_value
-    )
-    output, input_grad, gate, up, down, out, query, key, value, gains = backward_part(
-        groups, seq_devices, branch.reshape(token_count, D), inputs.reshape(token_count, D),
-        cotangent.reshape(token_count, D), gain_ffn, w_out, w_gate.T, w_up.T, w_down,
-        doc_lengths, got, heads, inverse, gain_attn, w_query, w_key, w_value,
+    output, input_grad, gate, up, down, out, query, key, value, gains = block_step(
+        groups, seq_devices, inputs.reshape(token_count, D), cotangent.reshape(token_count, D), gain_ffn, w_out,
+        w_gate.T, w_up.T, w_down, doc_lengths, gain_attn, w_query, w_key, w_value,
+    )
+    output, input_grad, gate, up, down, out, query, key, value, gain_attn_part, gain_ffn_part = publish(
+        (output, input_grad, gate, up, down, out, query, key, value), gains
     )
     return (
         output.reshape(row_count, shard_len, D),
         input_grad.reshape(row_count, shard_len, D),
-        gains[1, :32],
+        gain_attn_part.reshape(32),
         query,
         key,
         value,
         out,
-        gains[0, :32],
+        gain_ffn_part.reshape(32),
         gate,
         up,
         down.T,

time: 182 us -> 172 us (0.945)
  local copies, waits for them, and re-layouts: 9.17 us -> 0 us
    unnamed x25 -> x0, local copies, waits for them, and re-layouts: 7.89 us -> none
where the time goes in v4:
time: 172 us
  Pallas kernels  171 us (99%)
    pallas_call x1, Pallas kernels, block_step(): pl.pallas_call(functools.partial(block_kernel, groups, seq_devices, rows,...  168 us
    pallas_call x1, Pallas kernels, publish(): pl.pallas_call(kernel, name='publish', out_shape=[jax.ShapeDtypeStruct(x....  3.6 us

profile of v4, /device:TPU:0, one launch (start us, length us, event | category | flops | bytes accessed | tf_op | source)
XLA Modules:
  0.0 172.0 jit_solution(13008194372234680385)
XLA Ops:
  0.6 167.6 %block.1 = (bf16[432,1024]{1,0:T(8,128)(2,1)}, bf16[432,1024]{1,0:T(8,128)(2,1)}, f32[32,2752]{1,0:T(8,128)}, f32[32,2752]{1,0:T(8,128)}, f32[32,2752]{1,0:T(8,1...) custom-call(bf16[432,1024]{1,0:T(8,128)(2,1)} %bitcast.13, ...), custom_call_target="tpu_custom_call" | custom-call | tf_op jit(solution)/shard_map/block/pallas_call | solution.py:1160
  168.3 3.6 %publish.1 = (bf16[432,1024]{1,0:T(8,128)(2,1)}, bf16[432,1024]{1,0:T(8,128)(2,1)}, f32[32,2752]{1,0:T(8,128)}, f32[32,2752]{1,0:T(8,128)}, f32[32,2752]{1,0:T(8...) custom-call(bf16[432,1024]{1,0:T(8,128)(2,1)} %get-tuple-element.32., ...), custom_call_target="tpu_custom_call" | custom-call | tf_op jit(solution)/shard_map/publish/pallas_call | solution.py:1228

commit v5 on v4

--- a/solution.py
+++ b/solution.py
@@ -693,12 +693,18 @@
         )
 
     def prepare_lhs(which, source):
-        turned = right.at[3 if which < 3 else 1, :, pl.ds(0, padded)]
+        turned = right.at[3 if which < 2 else 1, :, pl.ds(0, padded)]
         turn(source, tokens, padded, turned)
         split_rows(turned, lhs.at[which % 3, :, :, :, pl.ds(0, padded)], lhs_send(which), core, groups)
 
     def left(which):
         return lhs[which].reshape(D // 2, 2 * padded)
+
+    gap = padded - tokens
+
+    def clear(slot, count):
+        for base in (tokens, padded + tokens):
+            right[slot : slot + count, base : base + gap, :] = jnp.zeros((count, gap, 3 * CHUNK), BF16)
 
     for part in range(D // CHUNK):
         value_load(part).start()
@@ -752,9 +758,21 @@
     prepare_lhs(0, cot_ref[...])
     lhs_copy(0).start()
 
+    gnf[...] = jnp.zeros_like(gnf)
+    clear(0, 3)
+
+    def residual_row(row):
+        for step in range(1, seq_devices):
+            merging(row, step).wait_recv()
+        at = pl.ds(pl.multiple_of(row * length, 16), length)
+        value = x_ref[at, :].astype(F32) + nn(branch[at, :], wo_ref[...])
+        residual[at, :] = value
+        out_acc[at, :] = value
+        normed[at, :] = rms_scale(value, gain_ref[...]).astype(BF16)
+
     def attend_rows(row, carry):
         for step in range(1, seq_devices):
-            spreading(row, step).wait_recv()
+            spreading(row, step).wait()
         prepare_row(got, row, qa, ka, ve, seq_devices, length)
         attend_forward(row_ends(doc_ref, row), qa, ka, ve, heads.at[row], inverse.at[row])
         for step in range(1, seq_devices):
@@ -765,36 +783,11 @@
 
     lax.fori_loop(0, rows, attend_rows, 0)
 
-    def merged(row, carry):
-        for step in range(1, seq_devices):
-            spreading(row, step).wait_send()
-            merging(row, step).wait()
-        return carry
-
-    lax.fori_loop(0, rows, merged, 0)
-
-    def norm_forward(step, carry):
-        at = pl.ds(pl.multiple_of(step * STEP_ROWS, 16), STEP_ROWS)
-        value = x_ref[at, :].astype(F32) + residual[at, :]
-        residual[at, :] = value
-        out_acc[at, :] = value
-        normed[at, :] = rms_scale(value, gain_ref[...]).astype(BF16)
-        return carry
-
-    residual[...] = nn(branch[...], wo_ref[...])
-    lax.fori_loop(0, tokens // STEP_ROWS, norm_forward, 0)
-    gnf[...] = jnp.zeros_like(gnf)
-
-    for which, source in ((1, normed), (2, branch)):
-        prepare_lhs(which, source[...])
-        lhs_copy(which).start()
-    gap = padded - tokens
-
-    def clear(slot, count):
-        for base in (tokens, padded + tokens):
-            right[slot : slot + count, base : base + gap, :] = jnp.zeros((count, gap, 3 * CHUNK), BF16)
-
-    clear(0, 4)
+    for row in range(rows):
+        residual_row(row)
+    prepare_lhs(1, normed[...])
+    lhs_copy(1).start()
+    clear(3, 1)
 
     def right_copy(slot, cols, sem):
         return sending(
@@ -875,7 +868,7 @@
         def _():
             first.c_copy(unit).start()
 
-        @pl.when(jnp.logical_not(along_z))
+        @pl.when(jnp.logical_not(along_z) & (unit < 10))
         def _():
             feed.a_copy(unit).start()
 
@@ -883,7 +876,7 @@
         return carry
 
     forward_step(0)
-    for which in range(3):
+    for which in range(2):
         lhs_copy(which).wait()
     lax.fori_loop(1, full, main, 0)
     slot = full % 2
@@ -946,6 +939,8 @@
     out_pairs = [right_copy(3, 3 * CHUNK, full + 1), right_copy(0, CHUNK, full + 2)]
     for copy in out_pairs:
         copy.start()
+    prepare_lhs(2, branch[...])
+    lhs_copy(2).start()
     feed.b_step(4)
     first.c_step(3)
     feed.c_step(0)
@@ -954,6 +949,7 @@
     for copy in out_pairs:
         copy.wait()
     lhs_copy(3).start()
+    lhs_copy(2).wait()
     for col in range(0, D, CHUNK):
         columns = right[3, :, col : col + CHUNK] if col < 3 * CHUNK else right[0, :, :CHUNK]
         store_blocks(parts_o, 0, col, nn(left(2), columns), groups)
@@ -984,7 +980,7 @@
 
         @pl.when(row == 0)
         def _():
-            feed.a_copy(full).start()
+            feed.a_copy(10).start()
             feed.a_step(8)
             feed.b_step(6)
             first.c_step(5)
@@ -1086,33 +1082,34 @@
         write_unit(total, at, w, gate_out, up_out, down_out)
 
     gain_copies[0].start()
-    first.d_step(7)
-    feed.c_step(6)
     outer.a_step(0)
     feed.b_step(10)
     gain_step(0)
+    first.d_step(7)
+    feed.c_step(6)
     first.a_step(1)
     feed.c_step(8)
+    gain_step(1)
+    qkv.a_step(0)
+    first.a_step(3)
+    qkv.a_step(1)
+    outer.b_step(0)
+    gain_step(2)
+    qkv.b_step(0)
+    feed.c_step(10)
+    first.a_step(5)
+    qkv.b_step(1)
+    gain_step(3)
+    qkv.c_step(0)
     first.d_step(9)
-    gain_step(1)
-    first.a_step(3)
-    outer.b_step(0)
-    qkv.a_step(0)
-    feed.c_step(10)
-    gain_step(2)
-    first.a_step(5)
+    outer.c_step(0)
+    qkv.c_step(1)
     first.a_step(7)
-    qkv.a_step(1)
-    outer.c_step(0)
-    gain_step(3)
-    qkv.b_step(0)
+    gain_step(4)
     first.a_step(9)
-    qkv.b_step(1)
-    qkv.c_step(0)
-    gain_step(4)
-    for unit in range(0, full, 2):
-        write_feed(unit, feed.d_step(unit), CHUNK)
-    qkv.c_step(1)
+    for unit in range(full):
+        if unit >= 2 * Z_UNITS or unit % 2 == 0:
+            write_feed(unit, feed.d_step(unit), CHUNK)
     write_feed(full, feed.d_step(full), tail)
     for unit in range(1, 2 * Z_UNITS, 2):
         write_feed(unit, first.b_step(unit), CHUNK)
@@ -1134,6 +1131,12 @@
             feed.wait_sent(unit)
             if unit > 2 * (full - SLOTS):
                 feed.a_copy(unit).wait_send()
+    def forward_sent(row, carry):
+        for step in range(1, seq_devices):
+            merging(row, step).wait_send()
+        return carry
+
+    lax.fori_loop(0, rows, forward_sent, 0)
     for one, unit in ((outer, 0), (qkv, 0), (qkv, 1)):
         one.wait_sent(unit)
         one.a_copy(unit).wait_send()

time: 172 us -> 170 us (0.988)
  Pallas kernels: 171 us -> 169 us
    pallas_call x1, Pallas kernels: 168 us -> 165 us  [block_step(): pl.pallas_call(functools.partial(block_kernel, groups, seq_devices, rows,...]
where the time goes in v5:
time: 170 us; the launch traced here: 169 us
  Pallas kernels  169 us (99%)
    pallas_call x1, Pallas kernels, block_step(): pl.pallas_call(functools.partial(block_kernel, groups, seq_devices, rows,...  165 us
    pallas_call x1, Pallas kernels, publish(): pl.pallas_call(kernel, name='publish', out_shape=[jax.ShapeDtypeStruct(x....  3.6 us

profile of v5, /device:TPU:0, one launch (start us, length us, event | category | flops | bytes accessed | tf_op | source)
XLA Modules:
  0.0 169.4 jit_solution(16757569887930813447)
XLA Ops:
  0.6 165.0 %block.1 = (bf16[432,1024]{1,0:T(8,128)(2,1)}, bf16[432,1024]{1,0:T(8,128)(2,1)}, f32[32,2752]{1,0:T(8,128)}, f32[32,2752]{1,0:T(8,128)}, f32[32,2752]{1,0:T(8,1...) custom-call(bf16[432,1024]{1,0:T(8,128)(2,1)} %bitcast.13, ...), custom_call_target="tpu_custom_call" | custom-call | tf_op jit(solution)/shard_map/block/pallas_call | solution.py:1163
  165.7 3.6 %publish.1 = (bf16[432,1024]{1,0:T(8,128)(2,1)}, bf16[432,1024]{1,0:T(8,128)(2,1)}, f32[32,2752]{1,0:T(8,128)}, f32[32,2752]{1,0:T(8,128)}, f32[32,2752]{1,0:T(8...) custom-call(bf16[432,1024]{1,0:T(8,128)(2,1)} %get-tuple-element.32., ...), custom_call_target="tpu_custom_call" | custom-call | tf_op jit(solution)/shard_map/publish/pallas_call | solution.py:1231

commit v6 on v5

--- a/solution.py
+++ b/solution.py
@@ -303,9 +303,8 @@
 
 def spread_matrix():
     half = H * F
-    shape = (2 * half, (H // 2) * 128)
-    source = lax.broadcasted_iota(jnp.int32, shape, 0)
-    column = lax.broadcasted_iota(jnp.int32, shape, 1)
+    source = lax.broadcasted_iota(jnp.int32, (2 * half, 1), 0)
+    column = lax.broadcasted_iota(jnp.int32, (1, (H // 2) * 128), 1)
     pair, lane = column // 128, column % 64
     wanted = pair * 32 + lane + jnp.where(lane < 32, 0, half - 32)
     return jnp.where(source == wanted, 1.0, 0.0).astype(BF16)
@@ -313,9 +312,8 @@
 
 def gather_matrix():
     half = H * F
-    shape = (2 * half, 2 * half)
-    source = lax.broadcasted_iota(jnp.int32, shape, 0)
-    column = lax.broadcasted_iota(jnp.int32, shape, 1)
+    source = lax.broadcasted_iota(jnp.int32, (2 * half, 1), 0)
+    column = lax.broadcasted_iota(jnp.int32, (1, 2 * half), 1)
     pair, lane = source // 64, source % 64
     wanted = pair * 32 + lane + jnp.where(lane < 32, 0, half - 32)
     return jnp.where(column == wanted, 1.0, 0.0).astype(BF16)
@@ -746,12 +744,20 @@
             tile = sides[side][:, col : col + 128]
             back[row, pair, :length, :] = values[:, pair * PAIR : (pair + 1) * PAIR]
             back[row, pair, length:, :] = jnp.where(lower, tile[:low], tile[length - low :]).astype(BF16)
+        got[row, me] = back[row, me]
+
+        @pl.when(row == 0)
+        def _():
+            send_spread(0)
+
+        return carry
+
+    def send_spread(row):
         for step in range(1, seq_devices):
             spreading(row, step).start()
-        got[row, me] = back[row, me]
-        return carry
 
     lax.fori_loop(0, rows, project_row, 0)
+    send_spread(1)
     for chunk in range(2):
         for copy in loads(chunk, chunk, CHUNK):
             copy.start()
@@ -773,6 +779,11 @@
     def attend_rows(row, carry):
         for step in range(1, seq_devices):
             spreading(row, step).wait()
+
+        @pl.when(row + 2 < rows)
+        def _():
+            send_spread(row + 2)
+
         prepare_row(got, row, qa, ka, ve, seq_devices, length)
         attend_forward(row_ends(doc_ref, row), qa, ka, ve, heads.at[row], inverse.at[row])
         for step in range(1, seq_devices):
@@ -932,10 +943,11 @@
         arrived[row, here, :] = normed[at, pl.ds(pl.multiple_of(me * PAIR, 128), PAIR)]
         return carry
 
-    lax.fori_loop(0, rows, send_row, 0)
+    send_row(0, 0)
     feed.a_step(6)
     feed.a_copy(2 * (full - SLOTS)).wait_send()
     grad_part(full)
+    send_row(1, 0)
     out_pairs = [right_copy(3, 3 * CHUNK, full + 1), right_copy(0, CHUNK, full + 2)]
     for copy in out_pairs:
         copy.start()
@@ -944,6 +956,8 @@
     feed.b_step(4)
     first.c_step(3)
     feed.c_step(0)
+    for row in range(2, rows):
+        send_row(row, 0)
     prepare_lhs(3, rms_scale(x_ref[...].astype(F32), gain_attn_ref[...]).astype(BF16))
     clear(1, 1)
     for copy in out_pairs:
@@ -982,21 +996,24 @@
         def _():
             feed.a_copy(10).start()
             feed.a_step(8)
-            feed.b_step(6)
             first.c_step(5)
-            first.d_step(1)
 
         @pl.when(row == 1)
         def _():
             outer.a_copy(0).start()
+            feed.b_step(6)
             feed.c_step(2)
             first.c_step(7)
+            first.d_step(1)
+
+        @pl.when(row == 2)
+        def _():
             first.d_step(3)
+            feed.b_step(8)
 
         return carry
 
     lax.fori_loop(0, rows, attend, 0)
-    feed.b_step(8)
     feed.c_step(4)
     first.c_step(9)
     first.d_step(5)

time: 170 us -> 168 us (0.988)
  Pallas kernels: 169 us -> 167 us
where the time goes in v6:
time: 168 us
  Pallas kernels  167 us (99%)
    pallas_call x1, Pallas kernels, block_step(): pl.pallas_call(functools.partial(block_kernel, groups, seq_devices, rows,...  164 us
    pallas_call x1, Pallas kernels, publish(): pl.pallas_call(kernel, name='publish', out_shape=[jax.ShapeDtypeStruct(x....  3.6 us

profile of v6, /device:TPU:0, one launch (start us, length us, event | category | flops | bytes accessed | tf_op | source)
XLA Modules:
  0.0 168.2 jit_solution(265471142933572197)
XLA Ops:
  0.6 163.8 %block.1 = (bf16[432,1024]{1,0:T(8,128)(2,1)}, bf16[432,1024]{1,0:T(8,128)(2,1)}, f32[32,2752]{1,0:T(8,128)}, f32[32,2752]{1,0:T(8,128)}, f32[32,2752]{1,0:T(8,1...) custom-call(bf16[432,1024]{1,0:T(8,128)(2,1)} %bitcast.13, ...), custom_call_target="tpu_custom_call" | custom-call | tf_op jit(solution)/shard_map/block/pallas_call | solution.py:1180
  164.5 3.6 %publish.1 = (bf16[432,1024]{1,0:T(8,128)(2,1)}, bf16[432,1024]{1,0:T(8,128)(2,1)}, f32[32,2752]{1,0:T(8,128)}, f32[32,2752]{1,0:T(8,128)}, f32[32,2752]{1,0:T(8...) custom-call(bf16[432,1024]{1,0:T(8,128)(2,1)} %get-tuple-element.32., ...), custom_call_target="tpu_custom_call" | custom-call | tf_op jit(solution)/shard_map/publish/pallas_call | solution.py:1248

commit v7 on v6

--- a/solution.py
+++ b/solution.py
@@ -840,13 +840,13 @@
         forward_part(chunk, w_buf[slot, 0], w_buf[slot, 1], w_buf[slot, 2], CHUNK)
 
     def ticks(chunk):
-        @pl.when((chunk >= 4) & (lax.rem(chunk, 2) == 0))
+        @pl.when((chunk >= 3) & (lax.rem(chunk, 2) == 1))
         def _():
-            feed.a_step(chunk - 4)
-
-        @pl.when((chunk >= 7) & (lax.rem(chunk, 2) == 1))
+            feed.a_step(chunk - 3)
+
+        @pl.when((chunk >= 5) & (lax.rem(chunk, 2) == 1))
         def _():
-            feed.b_step(chunk - 7)
+            feed.b_step(chunk - 5)
 
         @pl.when(chunk == 8)
         def _():
@@ -944,7 +944,6 @@
         return carry
 
     send_row(0, 0)
-    feed.a_step(6)
     feed.a_copy(2 * (full - SLOTS)).wait_send()
     grad_part(full)
     send_row(1, 0)
@@ -953,7 +952,6 @@
         copy.start()
     prepare_lhs(2, branch[...])
     lhs_copy(2).start()
-    feed.b_step(4)
     first.c_step(3)
     feed.c_step(0)
     for row in range(2, rows):

time: 168 us -> 168 us (level)
  no operation moved by 1% of the time
where the time goes in v7:
time: 168 us; the launch traced here: 167 us
  Pallas kernels  167 us (99%)
    pallas_call x1, Pallas kernels, block_step(): pl.pallas_call(functools.partial(block_kernel, groups, seq_devices, rows,...  163 us
    pallas_call x1, Pallas kernels, publish(): pl.pallas_call(kernel, name='publish', out_shape=[jax.ShapeDtypeStruct(x....  3.6 us

profile of v7, /device:TPU:0, one launch (start us, length us, event | category | flops | bytes accessed | tf_op | source)
XLA Modules:
  0.0 167.4 jit_solution(7566108473841039540)
XLA Ops:
  0.6 163.0 %block.1 = (bf16[432,1024]{1,0:T(8,128)(2,1)}, bf16[432,1024]{1,0:T(8,128)(2,1)}, f32[32,2752]{1,0:T(8,128)}, f32[32,2752]{1,0:T(8,128)}, f32[32,2752]{1,0:T(8,1...) custom-call(bf16[432,1024]{1,0:T(8,128)(2,1)} %bitcast.13, ...), custom_call_target="tpu_custom_call" | custom-call | tf_op jit(solution)/shard_map/block/pallas_call | solution.py:1178
  163.6 3.6 %publish.1 = (bf16[432,1024]{1,0:T(8,128)(2,1)}, bf16[432,1024]{1,0:T(8,128)(2,1)}, f32[32,2752]{1,0:T(8,128)}, f32[32,2752]{1,0:T(8,128)}, f32[32,2752]{1,0:T(8...) custom-call(bf16[432,1024]{1,0:T(8,128)(2,1)} %get-tuple-element.32., ...), custom_call_target="tpu_custom_call" | custom-call | tf_op jit(solution)/shard_map/publish/pallas_call | solution.py:1246

commit v8 on v7

--- a/solution.py
+++ b/solution.py
@@ -952,7 +952,9 @@
         copy.start()
     prepare_lhs(2, branch[...])
     lhs_copy(2).start()
+    feed.b_step(6)
     first.c_step(3)
+    feed.a_step(8)
     feed.c_step(0)
     for row in range(2, rows):
         send_row(row, 0)
@@ -993,13 +995,11 @@
         @pl.when(row == 0)
         def _():
             feed.a_copy(10).start()
-            feed.a_step(8)
             first.c_step(5)
 
         @pl.when(row == 1)
         def _():
             outer.a_copy(0).start()
-            feed.b_step(6)
             feed.c_step(2)
             first.c_step(7)
             first.d_step(1)

time: 168 us -> 165 us (0.982)
  Pallas kernels: 167 us -> 164 us
    pallas_call x1, Pallas kernels: 163 us -> 161 us  [block_step(): pl.pallas_call(functools.partial(block_kernel, groups, seq_devices, rows,...]
where the time goes in v8:
time: 165 us
  Pallas kernels  164 us (99%)
    pallas_call x1, Pallas kernels, block_step(): pl.pallas_call(functools.partial(block_kernel, groups, seq_devices, rows,...  161 us
    pallas_call x1, Pallas kernels, publish(): pl.pallas_call(kernel, name='publish', out_shape=[jax.ShapeDtypeStruct(x....  3.6 us

profile of v8, /device:TPU:0, one launch (start us, length us, event | category | flops | bytes accessed | tf_op | source)
XLA Modules:
  0.0 165.3 jit_solution(15371365257316599868)
XLA Ops:
  0.6 160.9 %block.1 = (bf16[432,1024]{1,0:T(8,128)(2,1)}, bf16[432,1024]{1,0:T(8,128)(2,1)}, f32[32,2752]{1,0:T(8,128)}, f32[32,2752]{1,0:T(8,128)}, f32[32,2752]{1,0:T(8,1...) custom-call(bf16[432,1024]{1,0:T(8,128)(2,1)} %bitcast.13, ...), custom_call_target="tpu_custom_call" | custom-call | tf_op jit(solution)/shard_map/block/pallas_call | solution.py:1178
  161.5 3.6 %publish.1 = (bf16[432,1024]{1,0:T(8,128)(2,1)}, bf16[432,1024]{1,0:T(8,128)(2,1)}, f32[32,2752]{1,0:T(8,128)}, f32[32,2752]{1,0:T(8,128)}, f32[32,2752]{1,0:T(8...) custom-call(bf16[432,1024]{1,0:T(8,128)(2,1)} %get-tuple-element.32., ...), custom_call_target="tpu_custom_call" | custom-call | tf_op jit(solution)/shard_map/publish/pallas_call | solution.py:1246
